TPU v7x, 32 devices: a whole 2x2x4 slice. The times are simulated.
32 devices in a mesh: groups: 2 (over y), seq: 4 (over z), tensor: 4 (over x, core).
Axes of the slice: x: 2, y: 2, z: 4, core: 2. Of those that a mesh axis runs over, the one named last changes fastest.
Arguments:
- video_query: bfloat16 [1024, 4096], P(('groups', 'seq'), 'tensor'), parts along dimension 0, may hold values from -21 to 21
- video_key: bfloat16 [1024, 4096], P(('groups', 'seq'), 'tensor'), parts along dimension 0, may hold values from -21 to 21
- video_value: bfloat16 [1024, 4096], P(('groups', 'seq'), 'tensor'), parts along dimension 0, may hold values from -6 to 6
- video_stream: bfloat16 [1024, 4096], P(('groups', 'seq'), 'tensor'), parts along dimension 0, may hold values from -6 to 6
- out_weight: bfloat16 [4096, 4096], P('tensor'), may hold values from -0.09375 to 0.09375
- cross_query: bfloat16 [1024, 2048], P(('groups', 'seq'), 'tensor'), parts along dimension 0, may hold values from -21 to 21
- audio_key: bfloat16 [128, 2048], P(('groups', 'seq'), 'tensor'), parts along dimension 0, may hold values from -21 to 21
- audio_value: bfloat16 [128, 2048], P(('groups', 'seq'), 'tensor'), parts along dimension 0, may hold values from -6 to 6
- audio_query: bfloat16 [128, 2048], P(('groups', 'seq'), 'tensor'), parts along dimension 0, may hold values from -21 to 21
- cross_key: bfloat16 [1024, 2048], P(('groups', 'seq'), 'tensor'), parts along dimension 0, may hold values from -21 to 21
- cross_value: bfloat16 [1024, 2048], P(('groups', 'seq'), 'tensor'), parts along dimension 0, may hold values from -6 to 6
Outputs:
- video_next: bfloat16 [1024, 4096], P(('groups', 'seq'), 'tensor'), parts along dimension 0
- video_cross: bfloat16 [1024, 2048], P(('groups', 'seq'), 'tensor'), parts along dimension 0
- audio_cross: bfloat16 [128, 2048], P(('groups', 'seq'), 'tensor'), parts along dimension 0
There are 2 independent parts, one for each index of `groups`. A program takes and returns all parts, laid end to end along the dimension named above; an argument that names none is the same for every part. Nothing has to cross between parts.
All inputs are finite; a program needn't handle non-finite values.
Results may differ from a plain program's by a relative error of at most 0.012.
Values may be sent and summed in bfloat16 or wider, within the bound.
No kernel may reach another device: no remote copies, remote signals or barrier semaphores. Data moves between devices by JAX's collectives and lax.ppermute only.
A program may use at most 64 MiB of HBM per device.

v0:
```python
import math

import jax
import jax.numpy as jnp
from jax import lax
from jax.sharding import PartitionSpec as P

HD = 128


def blank_state(query_rows, head_count):
    return (
        jnp.full((head_count, query_rows), -1e30, jnp.float32),
        jnp.zeros((head_count, query_rows), jnp.float32),
        jnp.zeros((head_count, query_rows, HD), jnp.float32),
    )


def absorb(carried, queries, keyset, values, head_count):
    running, row_sum, numerator = carried
    query_rows = queries.shape[0]
    key_rows = keyset.shape[0]
    factor = 1.0 / math.sqrt(HD)
    query_heads = queries.reshape(query_rows, head_count, HD)
    for offset in range(0, key_rows, 1024):
        width_keys = min(1024, key_rows - offset)
        key_block = keyset[offset : offset + width_keys].reshape(width_keys, head_count, HD)
        value_block = values[offset : offset + width_keys].reshape(width_keys, head_count, HD)
        scores = (
            jnp.einsum("qhd,khd->hqk", query_heads, key_block, preferred_element_type=jnp.float32)
            * factor
        )
        highest = jnp.maximum(running, jnp.max(scores, axis=2))
        raised = jnp.exp(scores - highest[:, :, None])
        shrink = jnp.exp(running - highest)
        row_sum = row_sum * shrink + jnp.sum(raised, axis=2)
        numerator = numerator * shrink[:, :, None] + jnp.einsum(
            "hqk,khd->hqd",
            raised.astype(jnp.bfloat16),
            value_block,
            preferred_element_type=jnp.float32,
        )
        running = highest
    return (running, row_sum, numerator)


def finish(carried, head_count):
    running, row_sum, numerator = carried
    result = numerator / row_sum[:, :, None]
    return result.transpose(1, 0, 2).reshape(result.shape[1], head_count * HD).astype(jnp.bfloat16)


def local(
    video_query,
    video_key,
    video_value,
    video_stream,
    out_weight,
    cross_query,
    audio_key,
    audio_value,
    audio_query,
    cross_key,
    cross_value,
):
    local_heads = video_query.shape[1] // HD
    query_rows = video_query.shape[0]
    pieces = (
        lax.all_gather(video_key, "seq", axis=0, tiled=True),
        lax.all_gather(video_value, "seq", axis=0, tiled=True),
    )
    carried_video = absorb(
        blank_state(query_rows, local_heads), video_query, pieces[0], pieces[1], local_heads
    )
    attended = finish(carried_video, local_heads)
    projected = jnp.dot(attended, out_weight, preferred_element_type=jnp.float32)
    summed = lax.psum_scatter(
        projected.astype(jnp.bfloat16), "tensor", scatter_dimension=1, tiled=True
    ).astype(jnp.float32)
    video_next = (video_stream.astype(jnp.float32) + summed).astype(jnp.bfloat16)
    cross_heads = cross_query.shape[1] // HD
    every_key, every_value = (
        lax.all_gather(audio_key, "seq", axis=0, tiled=True),
        lax.all_gather(audio_value, "seq", axis=0, tiled=True),
    )
    carried_audio = absorb(
        blank_state(cross_query.shape[0], cross_heads),
        cross_query,
        every_key,
        every_value,
        cross_heads,
    )
    video_cross = finish(carried_audio, cross_heads)
    pieces = (
        lax.all_gather(cross_key, "seq", axis=0, tiled=True),
        lax.all_gather(cross_value, "seq", axis=0, tiled=True),
    )
    carried_cross = absorb(
        blank_state(audio_query.shape[0], cross_heads),
        audio_query,
        pieces[0],
        pieces[1],
        cross_heads,
    )
    audio_cross = finish(carried_cross, cross_heads)
    return (video_next, video_cross, audio_cross)


def solution(mesh):
    in_specs = (
        P(("groups", "seq"), "tensor"),
        P(("groups", "seq"), "tensor"),
        P(("groups", "seq"), "tensor"),
        P(("groups", "seq"), "tensor"),
        P("tensor", None),
        P(("groups", "seq"), "tensor"),
        P(("groups", "seq"), "tensor"),
        P(("groups", "seq"), "tensor"),
        P(("groups", "seq"), "tensor"),
        P(("groups", "seq"), "tensor"),
        P(("groups", "seq"), "tensor"),
    )
    out_specs = (
        P(("groups", "seq"), "tensor"),
        P(("groups", "seq"), "tensor"),
        P(("groups", "seq"), "tensor"),
    )
    return jax.shard_map(local, mesh=mesh, in_specs=in_specs, out_specs=out_specs, check_vma=False)
```

profile of v0, /device:TPU:0, one launch (start us, length us, event | category | flops | bytes accessed | tf_op | source)
XLA Modules:
  0.0 120.9 jit_solution(1426176765482469748)
XLA Ops:
  7.2 1.8 %copy.19 = bf16[128,1024]{0,1:T(8,128)(2,1)} copy(bf16[128,1024]{1,0:T(8,128)(2,1)} %param.12) | data formatting | bytes 524288 | tf_op args[1]
  9.1 0.0 all-gather.5.cloned.1.call-start
  9.1 0.7 all-gather.5.cloned.1.call-update
  9.9 15.2 %all_gather.20 = bf16[64,512]{1,0:T(8,128)(2,1)S(1)} all-gather(bf16[16,512]{1,0:T(8,128)(2,1)} %param.17), channel_id=1, replica_groups=mesh['groups'=2,'seq'=4,'tensor'=4] {'seq'}, dimensions={0}, use_global_device_ids=true | all-gather | bytes 81920 | tf_op jit(solution)/shard_map/all_gather | solution.py:83
  25.0 15.4 %all_gather.21 = bf16[64,512]{1,0:T(8,128)(2,1)} all-gather(bf16[16,512]{1,0:T(8,128)(2,1)} %param.18), channel_id=1, replica_groups=mesh['groups'=2,'seq'=4,'tensor'=4] {'seq'}, dimensions={0}, use_global_device_ids=true | all-gather | bytes 81920 | tf_op jit(solution)/shard_map/all_gather | solution.py:84
  40.5 1.1 fusion.35
  41.6 1.7 %all-gather.3.cloned.1.call-done = bf16[512,1024]{0,1:T(8,128)(2,1)} async-done(((bf16[128,1024]{0,1:T(8,128)(2,1)}), bf16[512,1024]{0,1:T(8,128)(2,1)}) %all-gather.3.cloned.1.call-update) | async-done | bytes 1048592 | tf_op jit(solution)/shard_map/all_gather | solution.py:69
  43.3 1.7 %multiply_reduce_fusion = (f32[8,128]{1,0:T(8,128)S(1)}, f32[8,128,512]{2,1,0:T(8,128)S(1)}) fusion(bf16[512,8,128]{0,2,1:T(8,128)(2,1)} %bitcast.107, bf16[128,1024]{1,0:T(8,128)(2,1)S(1)} %copy-done), kind=kOutput, calls=%fused_computation.2 | convolution fusion | flops 135265280 | bytes 3411968 | tf_op jit(solution)/shard_map/qhd,khd->hqk/dot_general | solution.py:30
  45.0 0.6 fusion
  45.6 27.5 %all-gather.5.cloned.1.call-done = bf16[512,1024]{1,0:T(8,128)(2,1)} async-done(((bf16[128,1024]{1,0:T(8,128)(2,1)}), bf16[512,1024]{1,0:T(8,128)(2,1)}) %all-gather.5.cloned.1.call-update) | async-done | bytes 1048592 | tf_op jit(solution)/shard_map/all_gather | solution.py:70
  73.1 1.5 %copy.22 = bf16[512,1024]{0,1:T(8,128)(2,1)S(1)} copy(bf16[512,1024]{1,0:T(8,128)(2,1)} %all-gather.5.cloned.1.call-done) | data formatting | bytes 2097152 | tf_op jit(solution)/shard_map/all_gather | solution.py:70
  74.6 0.6 fusion.4
  75.2 5.7 %convolution_convert_fusion = bf16[128,4096]{1,0:T(8,128)(2,1)} fusion(bf16[128,1024]{0,1:T(8,128)(2,1)S(1)} %bitcast.108, bf16[1024,4096]{1,0:T(8,128)(2,1)} %param.15), kind=kOutput, calls=%fused_computation | convolution fusion | flops 1074266112 | bytes 9699328 | tf_op jit(solution)/shard_map/dot_general | solution.py:76
  81.1 0.2 fusion.7
  81.3 0.8 copy.32
  82.1 0.1 copy.29
  82.2 0.1 copy.26
  82.3 15.0 %all_gather.22 = bf16[512,512]{0,1:T(8,128)(2,1)S(1)} all-gather(bf16[128,512]{0,1:T(8,128)(2,1)S(1)} %copy.26), channel_id=1, replica_groups=mesh['groups'=2,'seq'=4,'tensor'=4] {'seq'}, dimensions={0}, use_global_device_ids=true | all-gather | bytes 655360 | tf_op jit(solution)/shard_map/all_gather | solution.py:95
  97.4 0.3 fusion.36
  97.6 0.2 fusion.22
  97.8 13.9 %all_gather.23 = bf16[512,512]{0,1:T(8,128)(2,1)S(1)} all-gather(bf16[128,512]{0,1:T(8,128)(2,1)S(1)} %copy.29), channel_id=1, replica_groups=mesh['groups'=2,'seq'=4,'tensor'=4] {'seq'}, dimensions={0}, use_global_device_ids=true | all-gather | bytes 655360 | tf_op jit(solution)/shard_map/all_gather | solution.py:96
  111.8 0.3 fusion.11
  112.0 0.6 copy.71
  112.7 1.7 %add_convert_fusion = bf16[128,1024]{1,0:T(8,128)(2,1)} fusion(bf16[128,1024]{1,0:T(8,128)(2,1)} %reduce-scatter.2.cloned.1.call-done, bf16[128,1024]{1,0:T(8,128)(2,1)S(1)} %copy-done.1), kind=kLoop, calls=%fused_computation.22 | loop fusion | flops 524288 | bytes 786432 | tf_op jit(solution)/shard_map/convert_element_type | solution.py:80
  (24 shorter events, 0.2 us)
Async XLA Ops:
  7.2 36.2 %copy-start = (bf16[128,1024]{1,0:T(8,128)(2,1)S(1)}, bf16[128,1024]{1,0:T(8,128)(2,1)}, u32[]{:S(2)}) copy-start(bf16[128,1024]{1,0:T(8,128)(2,1)} %param.11) | copy-start | bytes 786436
  7.2 36.1 %all-gather.3.cloned.1.call-start = ((), (), s32[]{:S(2)}) async-start(), calls=%async_computation.1 | async-start | bytes 1310720 | tf_op jit(solution)/shard_map/all_gather | solution.py:69
  9.1 64.1 %all-gather.5.cloned.1.call-start = ((), (), s32[]{:S(2)}) async-start(), calls=%async_computation.2 | async-start | bytes 1310720 | tf_op jit(solution)/shard_map/all_gather | solution.py:70
  9.8 102.8 %reduce-scatter.2.cloned.1.call-start = ((), (), s32[]{:S(2)}) async-start(), calls=%async_computation.3 | async-start | bytes 1310720 | tf_op jit(solution)/shard_map/reduce_scatter | solution.py:77
  75.2 5.8 %copy-start.4 = (bf16[64,512]{1,0:T(8,128)(2,1)S(1)}, bf16[64,512]{1,0:T(8,128)(2,1)}, u32[]{:S(2)}) copy-start(bf16[64,512]{1,0:T(8,128)(2,1)} %all_gather.21) | copy-start | bytes 196612
  80.9 1.1 copy-start.2
  80.9 1.3 %copy-start.3 = (bf16[128,512]{1,0:T(8,128)(2,1)S(1)}, bf16[128,512]{1,0:T(8,128)(2,1)}, u32[]{:S(2)}) copy-start(bf16[128,512]{1,0:T(8,128)(2,1)} %param.20) | copy-start | bytes 393220
  80.9 16.4 %copy-start.5 = (bf16[16,512]{1,0:T(8,128)(2,1)S(1)}, bf16[16,512]{1,0:T(8,128)(2,1)}, u32[]{:S(2)}) copy-start(bf16[16,512]{1,0:T(8,128)(2,1)} %param.19) | copy-start | bytes 49156
  81.3 31.4 %copy-start.1 = (bf16[128,1024]{1,0:T(8,128)(2,1)S(1)}, bf16[128,1024]{1,0:T(8,128)(2,1)}, u32[]{:S(2)}) copy-start(bf16[128,1024]{1,0:T(8,128)(2,1)} %param.14) | copy-start | bytes 786436
Sparse Core Ops, SparseCore 0:
  10.1 33.1 all-gather.2
  44.9 28.2 all-gather.4
  81.1 24.3 reduce-scatter.1
where the time goes:
time: 121 us
  blocking collectives  59.5 us (49%)
  waiting for transfers between devices  30 us (25%)
  between operations  13.9 us (11%)
  matrix products  9.9 us (8%)
  local copies, waits for them, and re-layouts  4.99 us (4%)
  other arithmetic  2.58 us (2%)
    all_gather x1, waiting for transfers between devices, local(): lax.all_gather(video_value, 'seq', axis=0, tiled=True)  27.5 us
    all_gather x1, blocking collectives, local(): lax.all_gather(audio_value, 'seq', axis=0, tiled=True)  15.4 us
    all_gather x1, blocking collectives, local(): lax.all_gather(audio_key, 'seq', axis=0, tiled=True)  15.2 us
    all_gather x1, blocking collectives, local(): lax.all_gather(cross_key, 'seq', axis=0, tiled=True)  15 us
    all_gather x1, blocking collectives, local(): lax.all_gather(cross_value, 'seq', axis=0, tiled=True)  13.9 us
    dot_general x1, matrix products, local(): jnp.dot(attended, out_weight, preferred_element_type=jnp.float32)  5.7 us
    dot_general x3, matrix products, absorb(): jnp.einsum('qhd,khd->hqk', query_heads, key_block, preferred_element_type...  3.1 us
    unnamed x16, local copies, waits for them, and re-layouts  2.86 us
  transfers between devices with their start and end apart: 3, of which 2 were waited for; matrix products, arithmetic and copies ran while one was open for 5% of the time, Pallas kernels for 0%

commit v1 on v0

--- a/solution.py
+++ b/solution.py
@@ -1,11 +1,267 @@
+import functools
 import math
 
 import jax
 import jax.numpy as jnp
 from jax import lax
+from jax.experimental import pallas as pl
+from jax.experimental.pallas import tpu as pltpu
 from jax.sharding import PartitionSpec as P
 
 HD = 128
+FACTOR = 1.0 / math.sqrt(HD)
+LOG2E = math.log2(math.e)
+BF16 = jnp.bfloat16
+F32 = jnp.float32
+MIB = 1 << 20
+ANY = pl.BlockSpec(memory_space=pl.ANY)
+VM = pl.BlockSpec(memory_space=pltpu.VMEM)
+
+
+def rows_of(total, size):
+    return [slice(start, start + size) for start in range(0, total, size)]
+
+
+def partner(axis, size, mask):
+    return functools.partial(
+        lax.ppermute, axis_name=axis, perm=[(i, i ^ mask) for i in range(size)]
+    )
+
+
+def pack_kernel(count, q, k, v, ak, av, aq, *rest):
+    outs, audio, sem = rest[:count], rest[count], rest[count + 1]
+    rows, width = q.shape[0], q.shape[1] // count
+    arows = ak.shape[0]
+    z = lax.axis_index("seq")
+    copies = []
+    for mask in range(count):
+        owner = jnp.bitwise_xor(z, mask)
+        columns = pl.ds(pl.multiple_of(owner * width, width), width)
+        for position, source in enumerate((q, k, v)):
+            copies.append(
+                pltpu.make_async_copy(
+                    source.at[:, columns],
+                    outs[mask].at[pl.ds(position * rows, rows)],
+                    sem.at[len(copies)],
+                )
+            )
+    for position, source in enumerate((ak, av, aq)):
+        copies.append(
+            pltpu.make_async_copy(
+                source, audio.at[pl.ds(position * arows, arows)], sem.at[len(copies)]
+            )
+        )
+    for copy in copies:
+        copy.start()
+    for copy in copies:
+        copy.wait()
+
+
+def pack(count, q, k, v, ak, av, aq):
+    rows, width = q.shape[0], q.shape[1] // count
+    arows = ak.shape[0]
+    return pl.pallas_call(
+        functools.partial(pack_kernel, count),
+        out_shape=[jax.ShapeDtypeStruct((3 * rows, width), BF16)] * count
+        + [jax.ShapeDtypeStruct((3 * arows, ak.shape[1]), BF16)],
+        in_specs=[ANY] * 6,
+        out_specs=[ANY] * (count + 1),
+        scratch_shapes=[pltpu.SemaphoreType.DMA((3 * count + 3,))],
+        compiler_params=pltpu.CompilerParams(vmem_limit_bytes=1 * MIB),
+        name="pack",
+    )(q, k, v, ak, av, aq)
+
+
+def softmax_times(scores, value):
+    highest = jnp.max(scores, axis=1, keepdims=True)
+    raised = jnp.exp2(scores * (FACTOR * LOG2E) - highest * (FACTOR * LOG2E))
+    total = jnp.sum(raised, axis=1, keepdims=True)
+    numerator = jnp.dot(raised.astype(BF16), value, preferred_element_type=F32)
+    return highest, total, numerator
+
+
+def nt(a, b):
+    return lax.dot_general(a, b, (((1,), (1,)), ((), ())), preferred_element_type=F32)
+
+
+def attend_kernel(count, *refs):
+    packs, outs = refs[:count], refs[count:]
+    rows = packs[0].shape[0] // 3
+    for columns in rows_of(packs[0].shape[1], HD):
+        key = jnp.concatenate([p[rows : 2 * rows, columns] for p in packs], axis=0)
+        value = jnp.concatenate([p[2 * rows :, columns] for p in packs], axis=0)
+        for pack_ref, out in zip(packs, outs):
+            _, total, numerator = softmax_times(nt(pack_ref[:rows, columns], key), value)
+            out[:, columns] = (numerator / total).astype(BF16)
+
+
+def attend(packs):
+    count = len(packs)
+    rows, width = packs[0].shape[0] // 3, packs[0].shape[1]
+    return pl.pallas_call(
+        functools.partial(attend_kernel, count),
+        out_shape=[jax.ShapeDtypeStruct((rows, width), BF16)] * count,
+        in_specs=[VM] * count,
+        out_specs=[VM] * count,
+        compiler_params=pltpu.CompilerParams(vmem_limit_bytes=12 * MIB),
+        name="attend",
+    )(*packs)
+
+
+def fetch_kernel(w, out, sem):
+    copy = pltpu.make_async_copy(w, out, sem)
+    copy.start()
+    copy.wait()
+
+
+def fetch(w):
+    return pl.pallas_call(
+        fetch_kernel,
+        out_shape=pltpu.VMEM(w.shape, w.dtype),
+        in_specs=[ANY],
+        out_specs=VM,
+        scratch_shapes=[pltpu.SemaphoreType.DMA],
+        compiler_params=pltpu.CompilerParams(vmem_limit_bytes=1 * MIB),
+        name="fetch",
+    )(w)
+
+
+def project_kernel(count, tensor, *refs):
+    heads, w, keep, send, lhs = refs[:count], refs[count], refs[count + 1], refs[count + 2], refs[count + 3]
+    width = heads[0].shape[1]
+    z = lax.axis_index("seq")
+    t = lax.axis_index("tensor")
+    for mask in range(count):
+        owner = jnp.bitwise_xor(z, mask)
+        lhs[:, pl.ds(pl.multiple_of(owner * width, width), width)] = heads[mask][...]
+    share = w.shape[1] // tensor
+    step = min(512, share)
+    for core in (1, 0):
+        for mask in range(tensor // 2):
+            owner = jnp.bitwise_xor(t, 2 * mask + core)
+            for start in range(0, share, step):
+                columns = pl.ds(pl.multiple_of(owner * share + start, step), step)
+                product = jnp.dot(lhs[...], w[:, columns], preferred_element_type=F32)
+                if core:
+                    send[mask, :, start : start + step] = product.astype(BF16)
+                else:
+                    keep[mask, :, start : start + step] = product
+
+
+def project(heads, w, tensor):
+    count = len(heads)
+    rows, share = heads[0].shape[0], w.shape[1] // tensor
+    return pl.pallas_call(
+        functools.partial(project_kernel, count, tensor),
+        out_shape=[
+            jax.ShapeDtypeStruct((tensor // 2, rows, share), F32),
+            jax.ShapeDtypeStruct((tensor // 2, rows, share), BF16),
+        ],
+        in_specs=[VM] * (count + 1),
+        out_specs=[VM] * 2,
+        scratch_shapes=[pltpu.VMEM((rows, w.shape[0]), BF16)],
+        compiler_params=pltpu.CompilerParams(vmem_limit_bytes=24 * MIB),
+        name="project",
+    )(*heads, w)
+
+
+def cross_kernel(count, cq, ck, cv, *refs):
+    audios, vc, parts = refs[:count], refs[count], refs[count + 1 :]
+    arows = audios[0].shape[0] // 3
+    heads = cq.shape[1] // HD
+    akey = jnp.concatenate([a[:arows, :] for a in audios], axis=0)
+    avalue = jnp.concatenate([a[arows : 2 * arows, :] for a in audios], axis=0)
+    aquery = jnp.concatenate([a[2 * arows :, :] for a in audios], axis=0)
+    lane = lax.broadcasted_iota(jnp.int32, (count * arows, HD), 1)
+    stats = jnp.zeros((count * arows, HD), F32)
+    for head in range(heads):
+        columns = slice(head * HD, (head + 1) * HD)
+        _, total, numerator = softmax_times(nt(cq[:, columns], akey[:, columns]), avalue[:, columns])
+        vc[:, columns] = (numerator / total).astype(BF16)
+        highest, total, numerator = softmax_times(nt(aquery[:, columns], ck[:, columns]), cv[:, columns])
+        partial = (numerator / total).astype(BF16)
+        level = highest * (FACTOR * LOG2E) + jnp.log2(total)
+        for piece in range(3):
+            rounded = level.astype(BF16).astype(F32)
+            stats = jnp.where(lane == 3 * head + piece, rounded, stats)
+            level = level - rounded
+        for index, part in enumerate(parts):
+            part[:, columns] = partial[index * arows : (index + 1) * arows]
+    for index, part in enumerate(parts):
+        part[:, heads * HD :] = stats[index * arows : (index + 1) * arows].astype(BF16)
+
+
+def cross(cq, ck, cv, audios):
+    count = len(audios)
+    arows = audios[0].shape[0] // 3
+    return pl.pallas_call(
+        functools.partial(cross_kernel, count),
+        out_shape=[jax.ShapeDtypeStruct(cq.shape, BF16)]
+        + [jax.ShapeDtypeStruct((arows, cq.shape[1] + HD), BF16)] * count,
+        in_specs=[VM] * (3 + count),
+        out_specs=[VM] * (1 + count),
+        compiler_params=pltpu.CompilerParams(vmem_limit_bytes=8 * MIB),
+        name="cross",
+    )(cq, ck, cv, *audios)
+
+
+def combine_kernel(count, *refs):
+    parts, out = refs[:count], refs[count]
+    heads = out.shape[1] // HD
+    for head in range(heads):
+        columns = slice(head * HD, (head + 1) * HD)
+        levels = []
+        for part in parts:
+            pieces = part[:, heads * HD :].astype(F32)[:, 3 * head : 3 * head + 3]
+            levels.append(jnp.sum(pieces, axis=1, keepdims=True))
+        highest = functools.reduce(jnp.maximum, levels)
+        shares = [jnp.exp2(level - highest) for level in levels]
+        whole = functools.reduce(jnp.add, shares)
+        mixed = functools.reduce(
+            jnp.add, [part[:, columns].astype(F32) * share for part, share in zip(parts, shares)]
+        )
+        out[:, columns] = (mixed / whole).astype(BF16)
+
+
+def combine(parts):
+    count = len(parts)
+    shape = (parts[0].shape[0], parts[0].shape[1] - HD)
+    return pl.pallas_call(
+        functools.partial(combine_kernel, count),
+        out_shape=jax.ShapeDtypeStruct(shape, BF16),
+        in_specs=[VM] * count,
+        out_specs=VM,
+        compiler_params=pltpu.CompilerParams(vmem_limit_bytes=2 * MIB),
+        name="combine",
+    )(*parts)
+
+
+def exchanged(count, tensor, video_query, video_key, video_value, video_stream, out_weight,
+              cross_query, audio_key, audio_value, audio_query, cross_key, cross_value):
+    seq = [partner("seq", count, mask) for mask in range(count)]
+    masks = list(range(count - 1, 0, -1))
+    *packs, audio = pack(count, video_query, video_key, video_value, audio_key, audio_value, audio_query)
+    weight = fetch(out_weight)
+    for mask in masks:
+        packs[mask] = seq[mask](packs[mask])
+    heads = attend(packs)
+    audios = [audio] + [None] * (count - 1)
+    for mask in masks:
+        audios[mask] = seq[mask](audio)
+    heads = list(heads)
+    for mask in masks:
+        heads[mask] = seq[mask](heads[mask])
+    video_cross, *parts = cross(cross_query, cross_key, cross_value, audios)
+    keep, send = project(heads, weight, tensor)
+    recv = partner("tensor", tensor, 1)(send)
+    total = video_stream.astype(F32) + keep[0] + recv[0].astype(F32)
+    for mask in range(1, tensor // 2):
+        piece = (keep[mask] + recv[mask].astype(F32)).astype(BF16)
+        total = total + partner("tensor", tensor, 2 * mask)(piece).astype(F32)
+    video_next = total.astype(BF16)
+    for mask in masks:
+        parts[mask] = seq[mask](parts[mask])
+    return video_next, video_cross, combine(parts)
 
 
 def blank_state(query_rows, head_count):
@@ -50,7 +306,7 @@
     return result.transpose(1, 0, 2).reshape(result.shape[1], head_count * HD).astype(jnp.bfloat16)
 
 
-def local(
+def gathered(
     video_query,
     video_key,
     video_value,
@@ -107,22 +363,15 @@
 
 
 def solution(mesh):
-    in_specs = (
-        P(("groups", "seq"), "tensor"),
-        P(("groups", "seq"), "tensor"),
-        P(("groups", "seq"), "tensor"),
-        P(("groups", "seq"), "tensor"),
-        P("tensor", None),
-        P(("groups", "seq"), "tensor"),
-        P(("groups", "seq"), "tensor"),
-        P(("groups", "seq"), "tensor"),
-        P(("groups", "seq"), "tensor"),
-        P(("groups", "seq"), "tensor"),
-        P(("groups", "seq"), "tensor"),
-    )
-    out_specs = (
-        P(("groups", "seq"), "tensor"),
-        P(("groups", "seq"), "tensor"),
-        P(("groups", "seq"), "tensor"),
-    )
-    return jax.shard_map(local, mesh=mesh, in_specs=in_specs, out_specs=out_specs, check_vma=False)
+    count, tensor = mesh.shape["seq"], mesh.shape["tensor"]
+    both = P(("groups", "seq"), "tensor")
+    in_specs = (both,) * 4 + (P("tensor", None),) + (both,) * 6
+
+    def local(*arrays):
+        heads = arrays[0].shape[1] // HD
+        powers = all(n & (n - 1) == 0 for n in (count, tensor))
+        if powers and tensor > 1 and heads % count == 0 and arrays[6].shape[0] % 16 == 0:
+            return exchanged(count, tensor, *arrays)
+        return gathered(*arrays)
+
+    return jax.shard_map(local, mesh=mesh, in_specs=in_specs, out_specs=(both,) * 3, check_vma=False)

time: 121 us -> 64.8 us (0.54)
  blocking collectives: 59.5 us -> 0 us
  starting transfers between devices: 0.12 us -> 22 us
  between operations: 13.9 us -> 0.76 us
  matrix products: 9.9 us -> 0 us
  Pallas kernels: 0 us -> 7.4 us
  waiting for transfers between devices: 30 us -> 25 us
  local copies, waits for them, and re-layouts: 4.99 us -> 8.4 us
  other arithmetic: 2.58 us -> 0.9 us
    all_gather x4 -> x0, blocking collectives: 59.5 us -> none  [the longest x1 15.4 us: local(): lax.all_gather(audio_value, 'seq', axis=0, tiled=True)]
    all_gather x2 -> x0, waiting for transfers between devices: 29.2 us -> none  [the longest x1 27.5 us: local(): lax.all_gather(video_value, 'seq', axis=0, tiled=True)]
    ppermute x0 -> x14, waiting for transfers between devices: none -> 25 us  [the longest x3 14.6 us: exchanged(): packs[mask] = seq[mask](packs[mask])]
    ppermute x0 -> x14, starting transfers between devices: none -> 22 us  [the longest x3 5.88 us: exchanged(): heads[mask] = seq[mask](heads[mask])]
    dot_general x7 -> x0, matrix products: 9.9 us -> none  [the longest x1 5.7 us: local(): jnp.dot(attended, out_weight, preferred_element_type=jnp.float32)]
    pallas_call x0 -> x6, Pallas kernels: none -> 7.4 us  [the longest x1 2.25 us: attend(): pl.pallas_call(functools.partial(attend_kernel, count), out_shape=[jax.Sh...]
    unnamed x16 -> x22, local copies, waits for them, and re-layouts: 2.86 us -> 8.4 us
    all_gather x1 -> x0, local copies, waits for them, and re-layouts: 1.49 us -> none  [local(): lax.all_gather(video_value, 'seq', axis=0, tiled=True)]
  transfers between devices with their start and end apart: 3 -> 14, of which waited for: 2 -> 8; matrix products, arithmetic and copies ran while one was open for 5% -> 0% of each run, Pallas kernels for 0% -> 5%
where the time goes in v1:
time: 64.8 us; the launch traced here: 64.4 us
  waiting for transfers between devices  25 us (39%)
  starting transfers between devices  22 us (34%)
  local copies, waits for them, and re-layouts  8.4 us (13%)
  Pallas kernels  7.4 us (11%)
  other arithmetic  0.9 us (1%)
  between operations  0.76 us (1%)
    ppermute x3, waiting for transfers between devices, exchanged(): packs[mask] = seq[mask](packs[mask])  14.6 us
    unnamed x22, local copies, waits for them, and re-layouts  8.4 us
    ppermute x3, starting transfers between devices, exchanged(): heads[mask] = seq[mask](heads[mask])  5.88 us
    ppermute x3, starting transfers between devices, exchanged(): packs[mask] = seq[mask](packs[mask])  5.68 us
    ppermute x3, starting transfers between devices, exchanged(): audios[mask] = seq[mask](audio)  4.39 us
    ppermute x3, starting transfers between devices, exchanged(): parts[mask] = seq[mask](parts[mask])  4.39 us
    ppermute x3, waiting for transfers between devices, exchanged(): audios[mask] = seq[mask](audio)  4 us
    ppermute x3, waiting for transfers between devices, exchanged(): parts[mask] = seq[mask](parts[mask])  3.74 us
  transfers between devices with their start and end apart: 14, of which 8 were waited for; matrix products, arithmetic and copies ran while one was open for 0% of the time, Pallas kernels for 5%

profile of v1, /device:TPU:0, one launch (start us, length us, event | category | flops | bytes accessed | tf_op | source)
XLA Modules:
  0.0 64.4 jit_solution(11457634551635983230)
XLA Ops:
  0.6 0.9 %copy-done.1 = bf16[128,1024]{1,0:T(8,128)(2,1)S(1)} copy-done((bf16[128,1024]{1,0:T(8,128)(2,1)S(1)}, bf16[128,1024]{1,0:T(8,128)(2,1)}, u32[]{:S(2)}) %copy-start.1) | copy-done | bytes 262168
  1.6 0.9 %copy-done.2 = bf16[128,1024]{1,0:T(8,128)(2,1)S(1)} copy-done((bf16[128,1024]{1,0:T(8,128)(2,1)S(1)}, bf16[128,1024]{1,0:T(8,128)(2,1)}, u32[]{:S(2)}) %copy-start.2) | copy-done | bytes 262168
  2.5 0.9 %copy-done.3 = bf16[128,1024]{1,0:T(8,128)(2,1)S(1)} copy-done((bf16[128,1024]{1,0:T(8,128)(2,1)S(1)}, bf16[128,1024]{1,0:T(8,128)(2,1)}, u32[]{:S(2)}) %copy-start.3) | copy-done | bytes 262168
  6.0 3.1 %collective-permute-start = (bf16[384,256]{1,0:T(8,128)(2,1)S(1)}, bf16[384,256]{1,0:T(8,128)(2,1)S(1)}, u32[]{:S(2)}, u32[]{:S(2)}) collective-permute-start(bf16[384,256]{1,0:T(8,128)(2,1)S(1)} %get-tuple-element.20), channel_id=1, source_target_pairs={{0,4},{4,0},{8,12},{12,8},{1,5},{5,1},{9,13},{13,9},{2,6},{6,2},{1... | collective-permute-start | bytes 589832 | tf_op jit(solution)/shard_map/ppermute | solution.py:246
  9.1 2.6 %collective-permute-start.1 = (bf16[384,256]{1,0:T(8,128)(2,1)S(1)}, bf16[384,256]{1,0:T(8,128)(2,1)S(1)}, u32[]{:S(2)}, u32[]{:S(2)}) collective-permute-start(bf16[384,256]{1,0:T(8,128)(2,1)S(1)} %get-tuple-element.21), channel_id=1, source_target_pairs={{0,8},{4,12},{8,0},{12,4},{1,9},{5,13},{9,1},{13,5},{2,10},{6,14},... | collective-permute-start | bytes 589832 | tf_op jit(solution)/shard_map/ppermute | solution.py:246
  11.7 5.7 %collective-permute-done.refs_1_ = bf16[384,256]{1,0:T(8,128)(2,1)S(1)} collective-permute-done((bf16[384,256]{1,0:T(8,128)(2,1)S(1)}, bf16[384,256]{1,0:T(8,128)(2,1)S(1)}, u32[]{:S(2)}, u32[]{:S(2)}) %collective-permute-start) | collective-permute-done | bytes 196640 | tf_op jit(solution)/shard_map/ppermute | solution.py:246
  17.4 8.8 %collective-permute-done.1.refs_2_ = bf16[384,256]{1,0:T(8,128)(2,1)S(1)} collective-permute-done((bf16[384,256]{1,0:T(8,128)(2,1)S(1)}, bf16[384,256]{1,0:T(8,128)(2,1)S(1)}, u32[]{:S(2)}, u32[]{:S(2)}) %collective-permute-start.1) | collective-permute-done | bytes 196640 | tf_op jit(solution)/shard_map/ppermute | solution.py:246
  26.2 2.2 %attend.1 = (bf16[128,256]{1,0:T(8,128)(2,1)S(1)}, bf16[128,256]{1,0:T(8,128)(2,1)S(1)}, bf16[128,256]{1,0:T(8,128)(2,1)S(1)}, bf16[128,256]{1,0:T(8,128)(2,1)S(1)}) custom-call(bf16[384,256]{1,0:T(8,128)(2,1)S(1)} %get-tuple-element.19.refs_0_, bf16[384,256]{1,0:T(8,128)(2,1)S(1)} %collective-permute-done.refs_1_, ...), custom_call_target="tpu_custom_call" | custom-call | tf_op jit(solution)/shard_map/attend/pallas_call | solution.py:101
  28.5 3.4 %collective-permute-start.3 = (bf16[128,256]{1,0:T(8,128)(2,1)S(1)}, bf16[128,256]{1,0:T(8,128)(2,1)S(1)}, u32[]{:S(2)}, u32[]{:S(2)}) collective-permute-start(bf16[128,256]{1,0:T(8,128)(2,1)S(1)} %get-tuple-element.24), channel_id=1, source_target_pairs={{0,4},{4,0},{8,12},{12,8},{1,5},{5,1},{9,13},{13,9},{2,6},{6,2},{1... | collective-permute-start | bytes 196616 | tf_op jit(solution)/shard_map/ppermute | solution.py:253
  31.9 1.1 %collective-permute-start.4 = (bf16[128,256]{1,0:T(8,128)(2,1)S(1)}, bf16[128,256]{1,0:T(8,128)(2,1)S(1)}, u32[]{:S(2)}, u32[]{:S(2)}) collective-permute-start(bf16[128,256]{1,0:T(8,128)(2,1)S(1)} %get-tuple-element.25), channel_id=1, source_target_pairs={{0,8},{4,12},{8,0},{12,4},{1,9},{5,13},{9,1},{13,5},{2,10},{6,14},... | collective-permute-start | bytes 196616 | tf_op jit(solution)/shard_map/ppermute | solution.py:253
  33.0 1.4 %collective-permute-start.5 = (bf16[128,256]{1,0:T(8,128)(2,1)S(1)}, bf16[128,256]{1,0:T(8,128)(2,1)S(1)}, u32[]{:S(2)}, u32[]{:S(2)}) collective-permute-start(bf16[128,256]{1,0:T(8,128)(2,1)S(1)} %get-tuple-element.26), channel_id=1, source_target_pairs={{0,12},{4,8},{8,4},{12,0},{1,13},{5,9},{9,5},{13,1},{2,14},{6,10},... | collective-permute-start | bytes 196616 | tf_op jit(solution)/shard_map/ppermute | solution.py:253
  34.4 3.4 %copy-done = bf16[1024,4096]{1,0:T(8,128)(2,1)S(1)} copy-done((bf16[1024,4096]{1,0:T(8,128)(2,1)S(1)}, bf16[1024,4096]{1,0:T(8,128)(2,1)}, u32[]{:S(2)}) %copy-start) | copy-done | bytes 8388632
  39.2 1.3 %project.1 = (f32[2,128,1024]{2,1,0:T(8,128)S(1)}, bf16[2,128,1024]{2,1,0:T(8,128)(2,1)S(1)}) custom-call(bf16[128,256]{1,0:T(8,128)(2,1)S(1)} %get-tuple-element.23.refs_0_, bf16[128,256]{1,0:T(8,128)(2,1)S(1)} %collective-permute-done.3.refs_1_, bf16[128,256]{1,0:T(8,128)(2,1)S(1)} %collective-permute-done.4.refs_2_, ...), custom_call_target="tpu_custom_call" | custom-call | tf_op jit(solution)/shard_map/project/pallas_call | solution.py:154
  40.5 1.9 %collective-permute-done.6 = bf16[2,128,1024]{2,1,0:T(8,128)(2,1)S(1)} collective-permute-done((bf16[2,128,1024]{2,1,0:T(8,128)(2,1)S(1)}, bf16[2,128,1024]{2,1,0:T(8,128)(2,1)S(1)}, u32[]{:S(2)}, u32[]{:S(2)}) %collective-permute-start.6) | collective-permute-done | bytes 524320 | tf_op jit(solution)/shard_map/ppermute | solution.py:256
  42.5 1.6 %collective-permute-start.7 = (bf16[128,1024]{1,0:T(8,128)(2,1)S(1)}, bf16[128,1024]{1,0:T(8,128)(2,1)S(1)}, u32[]{:S(2)}, u32[]{:S(2)}) collective-permute-start(bf16[128,1024]{1,0:T(8,128)(2,1)S(1)} %fusion.2), channel_id=1, source_target_pairs={{0,2},{1,3},{2,0},{3,1},{4,6},{5,7},{6,4},{7,5},{8,10},{9,11},{10,... | collective-permute-start | bytes 786440 | tf_op jit(solution)/shard_map/ppermute | solution.py:260
  45.0 1.5 %collective-permute-start.9 = (bf16[48,512]{1,0:T(8,128)(2,1)S(1)}, bf16[48,512]{1,0:T(8,128)(2,1)S(1)}, u32[]{:S(2)}, u32[]{:S(2)}) collective-permute-start(bf16[48,512]{1,0:T(8,128)(2,1)S(1)} %get-tuple-element.29.refs_0_), channel_id=1, source_target_pairs={{0,8},{4,12},{8,0},{12,4},{1,9},{5,13},{9,1},{13,5},{2,10},{6,14},... | collective-permute-start | bytes 147464 | tf_op jit(solution)/shard_map/ppermute | solution.py:250
  46.5 2.0 %collective-permute-start.10 = (bf16[48,512]{1,0:T(8,128)(2,1)S(1)}, bf16[48,512]{1,0:T(8,128)(2,1)S(1)}, u32[]{:S(2)}, u32[]{:S(2)}) collective-permute-start(bf16[48,512]{1,0:T(8,128)(2,1)S(1)} %get-tuple-element.29.refs_0_), channel_id=1, source_target_pairs={{0,12},{4,8},{8,4},{12,0},{1,13},{5,9},{9,5},{13,1},{2,14},{6,10},... | collective-permute-start | bytes 147464 | tf_op jit(solution)/shard_map/ppermute | solution.py:250
  48.5 2.9 %collective-permute-done.9.refs_2_ = bf16[48,512]{1,0:T(8,128)(2,1)S(1)} collective-permute-done((bf16[48,512]{1,0:T(8,128)(2,1)S(1)}, bf16[48,512]{1,0:T(8,128)(2,1)S(1)}, u32[]{:S(2)}, u32[]{:S(2)}) %collective-permute-start.9) | collective-permute-done | bytes 49184 | tf_op jit(solution)/shard_map/ppermute | solution.py:250
  51.4 1.0 %collective-permute-done.10.refs_3_ = bf16[48,512]{1,0:T(8,128)(2,1)S(1)} collective-permute-done((bf16[48,512]{1,0:T(8,128)(2,1)S(1)}, bf16[48,512]{1,0:T(8,128)(2,1)S(1)}, u32[]{:S(2)}, u32[]{:S(2)}) %collective-permute-start.10) | collective-permute-done | bytes 49184 | tf_op jit(solution)/shard_map/ppermute | solution.py:250
  52.5 2.0 %cross.1 = (bf16[128,512]{1,0:T(8,128)(2,1)}, bf16[16,640]{1,0:T(8,128)(2,1)S(1)}, bf16[16,640]{1,0:T(8,128)(2,1)S(1)}, bf16[16,640]{1,0:T(8,128)(2,1)S(1)}, bf16[16,640]{1,0:T(8,128)(2,1)S(1)}) custom-call(bf16[128,512]{1,0:T(8,128)(2,1)S(1)} %copy-done.4, bf16[128,512]{1,0:T(8,128)(2,1)S(1)} %copy-done.5, bf16[128,512]{1,0:T(8,128)(2,1)S(1)} %copy-done.6, ...), custom_call_target="tpu_custom_call" | custom-call | tf_op jit(solution)/shard_map/cross/pallas_call | solution.py:197
  55.0 2.0 %collective-permute-start.12 = (bf16[16,640]{1,0:T(8,128)(2,1)S(1)}, bf16[16,640]{1,0:T(8,128)(2,1)S(1)}, u32[]{:S(2)}, u32[]{:S(2)}) collective-permute-start(bf16[16,640]{1,0:T(8,128)(2,1)S(1)} %get-tuple-element.33), channel_id=1, source_target_pairs={{0,8},{4,12},{8,0},{12,4},{1,9},{5,13},{9,1},{13,5},{2,10},{6,14},... | collective-permute-start | bytes 61448 | tf_op jit(solution)/shard_map/ppermute | solution.py:263
  57.0 1.8 %collective-permute-start.13 = (bf16[16,640]{1,0:T(8,128)(2,1)S(1)}, bf16[16,640]{1,0:T(8,128)(2,1)S(1)}, u32[]{:S(2)}, u32[]{:S(2)}) collective-permute-start(bf16[16,640]{1,0:T(8,128)(2,1)S(1)} %get-tuple-element.34), channel_id=1, source_target_pairs={{0,12},{4,8},{8,4},{12,0},{1,13},{5,9},{9,5},{13,1},{2,14},{6,10},... | collective-permute-start | bytes 61448 | tf_op jit(solution)/shard_map/ppermute | solution.py:263
  59.7 2.9 %collective-permute-done.13.refs_3_ = bf16[16,640]{1,0:T(8,128)(2,1)S(1)} collective-permute-done((bf16[16,640]{1,0:T(8,128)(2,1)S(1)}, bf16[16,640]{1,0:T(8,128)(2,1)S(1)}, u32[]{:S(2)}, u32[]{:S(2)}) %collective-permute-start.13) | collective-permute-done | bytes 20512 | tf_op jit(solution)/shard_map/ppermute | solution.py:263
  62.6 1.0 %combine.1 = bf16[16,512]{1,0:T(8,128)(2,1)} custom-call(bf16[16,640]{1,0:T(8,128)(2,1)S(1)} %get-tuple-element.31.refs_0_, bf16[16,640]{1,0:T(8,128)(2,1)S(1)} %collective-permute-done.11.refs_1_, bf16[16,640]{1,0:T(8,128)(2,1)S(1)} %collective-permute-done.12.refs_2_, bf16[16,640]{1,0:T(8,128)(2,1)S(1)} %collective-permute-done.13.refs_3_), custom_call_target="tpu_custom_call" | custom-call | tf_op jit(solution)/shard_map/combine/pallas_call | solution.py:229
  (34 shorter events, 7.2 us)
Async XLA Ops:
  0.6 1.0 %copy-start.1 = (bf16[128,1024]{1,0:T(8,128)(2,1)S(1)}, bf16[128,1024]{1,0:T(8,128)(2,1)}, u32[]{:S(2)}) copy-start(bf16[128,1024]{1,0:T(8,128)(2,1)} %q.1) | copy-start | bytes 786436
  1.6 0.9 %copy-start.2 = (bf16[128,1024]{1,0:T(8,128)(2,1)S(1)}, bf16[128,1024]{1,0:T(8,128)(2,1)}, u32[]{:S(2)}) copy-start(bf16[128,1024]{1,0:T(8,128)(2,1)} %k.1) | copy-start | bytes 786436
  2.5 0.9 %copy-start.3 = (bf16[128,1024]{1,0:T(8,128)(2,1)S(1)}, bf16[128,1024]{1,0:T(8,128)(2,1)}, u32[]{:S(2)}) copy-start(bf16[128,1024]{1,0:T(8,128)(2,1)} %v.1) | copy-start | bytes 786436
  4.2 0.7 %copy-start.8 = (bf16[16,512]{1,0:T(8,128)(2,1)S(1)}, bf16[16,512]{1,0:T(8,128)(2,1)}, u32[]{:S(2)}) copy-start(bf16[16,512]{1,0:T(8,128)(2,1)} %av.1) | copy-start | bytes 49156
  4.9 0.7 %copy-start.9 = (bf16[16,512]{1,0:T(8,128)(2,1)S(1)}, bf16[16,512]{1,0:T(8,128)(2,1)}, u32[]{:S(2)}) copy-start(bf16[16,512]{1,0:T(8,128)(2,1)} %aq.1) | copy-start | bytes 49156
  6.0 11.4 %collective-permute-start = (bf16[384,256]{1,0:T(8,128)(2,1)S(1)}, bf16[384,256]{1,0:T(8,128)(2,1)S(1)}, u32[]{:S(2)}, u32[]{:S(2)}) collective-permute-start(bf16[384,256]{1,0:T(8,128)(2,1)S(1)} %get-tuple-element.20), channel_id=1, source_target_pairs={{0,4},{4,0},{8,12},{12,8},{1,5},{5,1},{9,13},{13,9},{2,6},{6,2},{1... | collective-permute-start | bytes 589832 | tf_op jit(solution)/shard_map/ppermute | solution.py:246
  9.1 17.2 %collective-permute-start.1 = (bf16[384,256]{1,0:T(8,128)(2,1)S(1)}, bf16[384,256]{1,0:T(8,128)(2,1)S(1)}, u32[]{:S(2)}, u32[]{:S(2)}) collective-permute-start(bf16[384,256]{1,0:T(8,128)(2,1)S(1)} %get-tuple-element.21), channel_id=1, source_target_pairs={{0,8},{4,12},{8,0},{12,4},{1,9},{5,13},{9,1},{13,5},{2,10},{6,14},... | collective-permute-start | bytes 589832 | tf_op jit(solution)/shard_map/ppermute | solution.py:246
  11.7 14.6 %collective-permute-start.2 = (bf16[384,256]{1,0:T(8,128)(2,1)S(1)}, bf16[384,256]{1,0:T(8,128)(2,1)S(1)}, u32[]{:S(2)}, u32[]{:S(2)}) collective-permute-start(bf16[384,256]{1,0:T(8,128)(2,1)S(1)} %get-tuple-element.22), channel_id=1, source_target_pairs={{0,12},{4,8},{8,4},{12,0},{1,13},{5,9},{9,5},{13,1},{2,14},{6,10},... | collective-permute-start | bytes 589832 | tf_op jit(solution)/shard_map/ppermute | solution.py:246
  28.5 9.9 %collective-permute-start.3 = (bf16[128,256]{1,0:T(8,128)(2,1)S(1)}, bf16[128,256]{1,0:T(8,128)(2,1)S(1)}, u32[]{:S(2)}, u32[]{:S(2)}) collective-permute-start(bf16[128,256]{1,0:T(8,128)(2,1)S(1)} %get-tuple-element.24), channel_id=1, source_target_pairs={{0,4},{4,0},{8,12},{12,8},{1,5},{5,1},{9,13},{13,9},{2,6},{6,2},{1... | collective-permute-start | bytes 196616 | tf_op jit(solution)/shard_map/ppermute | solution.py:253
  31.9 6.5 %collective-permute-start.4 = (bf16[128,256]{1,0:T(8,128)(2,1)S(1)}, bf16[128,256]{1,0:T(8,128)(2,1)S(1)}, u32[]{:S(2)}, u32[]{:S(2)}) collective-permute-start(bf16[128,256]{1,0:T(8,128)(2,1)S(1)} %get-tuple-element.25), channel_id=1, source_target_pairs={{0,8},{4,12},{8,0},{12,4},{1,9},{5,13},{9,1},{13,5},{2,10},{6,14},... | collective-permute-start | bytes 196616 | tf_op jit(solution)/shard_map/ppermute | solution.py:253
  33.0 6.2 %collective-permute-start.5 = (bf16[128,256]{1,0:T(8,128)(2,1)S(1)}, bf16[128,256]{1,0:T(8,128)(2,1)S(1)}, u32[]{:S(2)}, u32[]{:S(2)}) collective-permute-start(bf16[128,256]{1,0:T(8,128)(2,1)S(1)} %get-tuple-element.26), channel_id=1, source_target_pairs={{0,12},{4,8},{8,4},{12,0},{1,13},{5,9},{9,5},{13,1},{2,14},{6,10},... | collective-permute-start | bytes 196616 | tf_op jit(solution)/shard_map/ppermute | solution.py:253
  34.4 3.4 %copy-start = (bf16[1024,4096]{1,0:T(8,128)(2,1)S(1)}, bf16[1024,4096]{1,0:T(8,128)(2,1)}, u32[]{:S(2)}) copy-start(bf16[1024,4096]{1,0:T(8,128)(2,1)} %w.1) | copy-start | bytes 25165828
  38.3 14.1 %copy-start.4 = (bf16[128,512]{1,0:T(8,128)(2,1)S(1)}, bf16[128,512]{1,0:T(8,128)(2,1)}, u32[]{:S(2)}) copy-start(bf16[128,512]{1,0:T(8,128)(2,1)} %cq.1) | copy-start | bytes 393220
  38.3 14.1 %copy-start.5 = (bf16[128,512]{1,0:T(8,128)(2,1)S(1)}, bf16[128,512]{1,0:T(8,128)(2,1)}, u32[]{:S(2)}) copy-start(bf16[128,512]{1,0:T(8,128)(2,1)} %ck.1) | copy-start | bytes 393220
  38.4 14.1 %copy-start.6 = (bf16[128,512]{1,0:T(8,128)(2,1)S(1)}, bf16[128,512]{1,0:T(8,128)(2,1)}, u32[]{:S(2)}) copy-start(bf16[128,512]{1,0:T(8,128)(2,1)} %cv.1) | copy-start | bytes 393220
  38.4 25.2 %copy-start.10 = (bf16[128,1024]{1,0:T(8,128)(2,1)S(1)}, bf16[128,1024]{1,0:T(8,128)(2,1)}, u32[]{:S(2)}) copy-start(bf16[128,1024]{1,0:T(8,128)(2,1)} %param.14) | copy-start | bytes 786436
  40.5 2.0 %collective-permute-start.6 = (bf16[2,128,1024]{2,1,0:T(8,128)(2,1)S(1)}, bf16[2,128,1024]{2,1,0:T(8,128)(2,1)S(1)}, u32[]{:S(2)}, u32[]{:S(2)}) collective-permute-start(bf16[2,128,1024]{2,1,0:T(8,128)(2,1)S(1)} %get-tuple-element.28), channel_id=1, source_target_pairs={{0,1},{1,0},{2,3},{3,2},{4,5},{5,4},{6,7},{7,6},{8,9},{9,8},{10,11... | collective-permute-start | bytes 1572872 | tf_op jit(solution)/shard_map/ppermute | solution.py:256
  42.5 21.0 %collective-permute-start.7 = (bf16[128,1024]{1,0:T(8,128)(2,1)S(1)}, bf16[128,1024]{1,0:T(8,128)(2,1)S(1)}, u32[]{:S(2)}, u32[]{:S(2)}) collective-permute-start(bf16[128,1024]{1,0:T(8,128)(2,1)S(1)} %fusion.2), channel_id=1, source_target_pairs={{0,2},{1,3},{2,0},{3,1},{4,6},{5,7},{6,4},{7,5},{8,10},{9,11},{10,... | collective-permute-start | bytes 786440 | tf_op jit(solution)/shard_map/ppermute | solution.py:260
  44.1 4.4 %collective-permute-start.8 = (bf16[48,512]{1,0:T(8,128)(2,1)S(1)}, bf16[48,512]{1,0:T(8,128)(2,1)S(1)}, u32[]{:S(2)}, u32[]{:S(2)}) collective-permute-start(bf16[48,512]{1,0:T(8,128)(2,1)S(1)} %get-tuple-element.29.refs_0_), channel_id=1, source_target_pairs={{0,4},{4,0},{8,12},{12,8},{1,5},{5,1},{9,13},{13,9},{2,6},{6,2},{1... | collective-permute-start | bytes 147464 | tf_op jit(solution)/shard_map/ppermute | solution.py:250
  45.0 6.4 %collective-permute-start.9 = (bf16[48,512]{1,0:T(8,128)(2,1)S(1)}, bf16[48,512]{1,0:T(8,128)(2,1)S(1)}, u32[]{:S(2)}, u32[]{:S(2)}) collective-permute-start(bf16[48,512]{1,0:T(8,128)(2,1)S(1)} %get-tuple-element.29.refs_0_), channel_id=1, source_target_pairs={{0,8},{4,12},{8,0},{12,4},{1,9},{5,13},{9,1},{13,5},{2,10},{6,14},... | collective-permute-start | bytes 147464 | tf_op jit(solution)/shard_map/ppermute | solution.py:250
  46.5 6.0 %collective-permute-start.10 = (bf16[48,512]{1,0:T(8,128)(2,1)S(1)}, bf16[48,512]{1,0:T(8,128)(2,1)S(1)}, u32[]{:S(2)}, u32[]{:S(2)}) collective-permute-start(bf16[48,512]{1,0:T(8,128)(2,1)S(1)} %get-tuple-element.29.refs_0_), channel_id=1, source_target_pairs={{0,12},{4,8},{8,4},{12,0},{1,13},{5,9},{9,5},{13,1},{2,14},{6,10},... | collective-permute-start | bytes 147464 | tf_op jit(solution)/shard_map/ppermute | solution.py:250
  54.4 4.4 %collective-permute-start.11 = (bf16[16,640]{1,0:T(8,128)(2,1)S(1)}, bf16[16,640]{1,0:T(8,128)(2,1)S(1)}, u32[]{:S(2)}, u32[]{:S(2)}) collective-permute-start(bf16[16,640]{1,0:T(8,128)(2,1)S(1)} %get-tuple-element.32), channel_id=1, source_target_pairs={{0,4},{4,0},{8,12},{12,8},{1,5},{5,1},{9,13},{13,9},{2,6},{6,2},{1... | collective-permute-start | bytes 61448 | tf_op jit(solution)/shard_map/ppermute | solution.py:263
  55.0 4.7 %collective-permute-start.12 = (bf16[16,640]{1,0:T(8,128)(2,1)S(1)}, bf16[16,640]{1,0:T(8,128)(2,1)S(1)}, u32[]{:S(2)}, u32[]{:S(2)}) collective-permute-start(bf16[16,640]{1,0:T(8,128)(2,1)S(1)} %get-tuple-element.33), channel_id=1, source_target_pairs={{0,8},{4,12},{8,0},{12,4},{1,9},{5,13},{9,1},{13,5},{2,10},{6,14},... | collective-permute-start | bytes 61448 | tf_op jit(solution)/shard_map/ppermute | solution.py:263
  57.0 5.6 %collective-permute-start.13 = (bf16[16,640]{1,0:T(8,128)(2,1)S(1)}, bf16[16,640]{1,0:T(8,128)(2,1)S(1)}, u32[]{:S(2)}, u32[]{:S(2)}) collective-permute-start(bf16[16,640]{1,0:T(8,128)(2,1)S(1)} %get-tuple-element.34), channel_id=1, source_target_pairs={{0,12},{4,8},{8,4},{12,0},{1,13},{5,9},{9,5},{13,1},{2,14},{6,10},... | collective-permute-start | bytes 61448 | tf_op jit(solution)/shard_map/ppermute | solution.py:263
  (1 other events, 0.7 us)

commit v2 on v0

--- a/solution.py
+++ b/solution.py
@@ -1,11 +1,332 @@
+import functools
 import math
 
 import jax
 import jax.numpy as jnp
 from jax import lax
+from jax.experimental import pallas as pl
+from jax.experimental.pallas import tpu as pltpu
 from jax.sharding import PartitionSpec as P
 
+
 HD = 128
+FACTOR = 1.0 / math.sqrt(HD)
+LOG2E = math.log2(math.e)
+BF16 = jnp.bfloat16
+F32 = jnp.float32
+MIB = 1 << 20
+ANY = pl.BlockSpec(memory_space=pl.ANY)
+HBM = pl.BlockSpec(memory_space=pltpu.HBM)
+VM = pl.BlockSpec(memory_space=pltpu.VMEM)
+WHOLE_VMEM = 62.75
+
+
+COSTS = {"merge": 10000000000, "partials": 3000000000}
+
+
+def call(kernel, name, shapes, ins, outs, operands, limit, scratch=(), flops=0):
+    flops = COSTS.get(name, flops)
+    return pl.pallas_call(
+        kernel,
+        out_shape=shapes,
+        in_specs=ins,
+        out_specs=outs,
+        scratch_shapes=scratch,
+        compiler_params=pltpu.CompilerParams(vmem_limit_bytes=int(limit * MIB)),
+        cost_estimate=pl.CostEstimate(flops=flops, bytes_accessed=0, transcendentals=0),
+        name=name,
+    )(*operands)
+
+
+def partner(axis, size, mask):
+    return functools.partial(
+        lax.ppermute, axis_name=axis, perm=[(i, i ^ mask) for i in range(size)]
+    )
+
+
+def nt(a, b):
+    return lax.dot_general(a, b, (((1,), (1,)), ((), ())), preferred_element_type=F32)
+
+
+def softmax_times(scores, value):
+    highest = jnp.max(scores, axis=1, keepdims=True)
+    raised = jnp.exp2(scores * (FACTOR * LOG2E) - highest * (FACTOR * LOG2E))
+    total = jnp.sum(raised, axis=1, keepdims=True)
+    numerator = jnp.dot(raised.astype(BF16), value, preferred_element_type=F32)
+    return highest, total, numerator
+
+
+def pack_kernel(masks, count, audio_mask, q, k, v, ak, av, aq, *rest):
+    own_audio = rest[-2] if audio_mask in masks else None
+    outs, sem = rest[-1 - len(masks) - (own_audio is not None) :], rest[-1]
+    rows, arows = q.shape[0], aq.shape[0]
+    width = q.shape[1] // count
+    z = lax.axis_index("seq")
+    copies = []
+
+    def copy(source, target):
+        copies.append(pltpu.make_async_copy(source, target, sem.at[len(copies)]))
+        copies[-1].start()
+
+    for mask, out in zip(masks, outs):
+        columns = pl.ds(pl.multiple_of(jnp.bitwise_xor(z, mask) * width, width), width)
+        for position, source in enumerate((q, k, v)):
+            copy(source.at[:, columns], out.at[pl.ds(position * rows, rows)])
+    if own_audio is not None:
+        for position, source in enumerate((ak, av, aq)):
+            copy(source, own_audio.at[pl.ds(position * arows, arows)])
+            for block in range(aq.shape[1] // width if audio_mask else 0):
+                copy(
+                    source.at[:, pl.ds(block * width, width)],
+                    outs[masks.index(audio_mask)].at[pl.ds(3 * rows + (3 * block + position) * arows, arows)],
+                )
+    for one in copies:
+        one.wait()
+
+
+def pack(masks, count, audio_mask, q, k, v, ak, av, aq, after=()):
+    rows, width = q.shape[0], q.shape[1] // count
+    below = 3 * aq.size // width
+    shapes = [pltpu.VMEM((3 * rows + (below if mask == audio_mask and mask else 0), width), BF16) for mask in masks]
+    copies = 3 * len(masks)
+    if audio_mask in masks:
+        shapes.append(pltpu.VMEM((3 * aq.shape[0], aq.shape[1]), BF16))
+        copies += 3 + (3 * aq.shape[1] // width if audio_mask else 0)
+    return call(
+        functools.partial(pack_kernel, masks, count, audio_mask), "pack", shapes,
+        [HBM] * 6 + [ANY] * len(after), [VM] * len(shapes), (q, k, v, ak, av, aq, *after),
+        WHOLE_VMEM, [pltpu.SemaphoreType.DMA((copies,))],
+    )
+
+
+def attend_kernel(wanted, order, rows, *refs):
+    count = len(order)
+    packs, outs = dict(zip(order, refs)), refs[-len(wanted) :]
+    for columns in range(0, packs[0].shape[1], HD):
+        columns = slice(columns, columns + HD)
+        key = jnp.concatenate([p[rows : 2 * rows, columns] for p in packs.values()], axis=0)
+        value = jnp.concatenate([p[2 * rows : 3 * rows, columns] for p in packs.values()], axis=0)
+        for mask, out in zip(wanted, outs):
+            _, total, numerator = softmax_times(nt(packs[mask][:rows, columns], key), value)
+            out[:, columns] = (numerator / total).astype(BF16)
+
+
+def attend(wanted, order, rows, packs, after, name):
+    count, width = len(packs), packs[0].shape[1]
+    return call(
+        functools.partial(attend_kernel, wanted, order, rows), name,
+        [jax.ShapeDtypeStruct((rows, width), BF16)] * len(wanted),
+        [VM] * count + [ANY] * len(after), [VM] * len(wanted), (*(packs[mask] for mask in order), *after), 8,
+        flops=4 * count * len(wanted) * rows * rows * width,
+    )
+
+
+def fetch_kernel(count, *refs):
+    copies = [
+        pltpu.make_async_copy(refs[i], refs[count + i], refs[-1].at[i]) for i in range(count)
+    ]
+    for one in copies:
+        one.start()
+    for one in copies:
+        one.wait()
+
+
+def fetch(*arrays):
+    count = len(arrays)
+    return call(
+        functools.partial(fetch_kernel, count), "fetch", [pltpu.VMEM(x.shape, x.dtype) for x in arrays],
+        [HBM] * count, [VM] * count, arrays, 53, [pltpu.SemaphoreType.DMA((count,))],
+    )
+
+
+def project_kernel(order, blocks, step, *refs):
+    count = len(order)
+    heads, w, lhs = refs[:count], refs[count], refs[-1]
+    outs = refs[-1 - len(blocks) : -1]
+    width = heads[0].shape[1]
+    z = lax.axis_index("seq")
+    t = lax.axis_index("tensor")
+    for mask, one in zip(order, heads):
+        owner = jnp.bitwise_xor(z, mask)
+        lhs[:, pl.ds(pl.multiple_of(owner * width, width), width)] = one[...]
+    for out, mask in zip(outs, blocks):
+        share = out.shape[1]
+        owner = jnp.bitwise_xor(t, mask)
+        for start in range(0, share, step):
+            columns = pl.ds(pl.multiple_of(owner * share + start, step), step)
+            product = jnp.dot(lhs[...], w[:, columns], preferred_element_type=F32)
+            out[:, start : start + step] = product.astype(out.dtype)
+
+
+def project(order, heads, w, share, blocks, name, after=()):
+    count, rows = len(heads), heads[0].shape[0]
+    return call(
+        functools.partial(project_kernel, order, list(blocks), math.gcd(512, share)), name,
+        [jax.ShapeDtypeStruct((rows, share), dtype) for dtype in blocks.values()],
+        [VM] * (count + 1) + [ANY] * len(after), [VM] * len(blocks), (*(heads[mask] for mask in order), w, *after), 8,
+        [pltpu.VMEM((rows, w.shape[0]), BF16)],
+        flops=2 * rows * w.shape[0] * share * len(blocks),
+    )
+
+
+def stats_of(levels, rows):
+    lane = lax.broadcasted_iota(jnp.int32, (rows, HD), 1)
+    stats = jnp.zeros((rows, HD), F32)
+    for head, level in enumerate(levels):
+        for piece in range(3):
+            rounded = level.astype(BF16).astype(F32)
+            stats = jnp.where(lane == 3 * head + piece, rounded, stats)
+            level = level - rounded
+    return stats.astype(BF16)
+
+
+def level_of(stats, head):
+    return jnp.sum(stats[:, 3 * head : 3 * head + 3].astype(F32), axis=1, keepdims=True)
+
+
+def audio_of(audios, audio_mask, first, mask, kind, head):
+    arows = audios[0].shape[0] // 3
+    ref, at, column = audios[mask], kind * arows, head * HD
+    if mask and mask == audio_mask:
+        block, column = divmod(column, ref.shape[1])
+        at += first + 3 * block * arows
+    return ref[at : at + arows, column : column + HD]
+
+
+def partial_kernel(groups, audio_mask, first, ck, cv, *refs):
+    count = sum(size for _, size in groups)
+    audios, parts = refs[:count], refs[-len(groups) :]
+    arows = audios[0].shape[0] // 3
+    heads = ck.shape[1] // HD
+    levels = []
+    for head in range(heads):
+        columns = slice(head * HD, (head + 1) * HD)
+        query = jnp.concatenate([audio_of(audios, audio_mask, first, m, 2, head) for m in range(count)], axis=0)
+        highest, total, numerator = softmax_times(nt(query, ck[:, columns]), cv[:, columns])
+        partial = (numerator / total).astype(BF16)
+        levels.append(highest * (FACTOR * LOG2E) + jnp.log2(total))
+        for (start, size), part in zip(groups, parts):
+            part[:, columns] = partial[start * arows : (start + size) * arows]
+    stats = stats_of(levels, count * arows)
+    for (start, size), part in zip(groups, parts):
+        part[:, heads * HD :] = stats[start * arows : (start + size) * arows]
+
+
+def partials(groups, audio_mask, first, ck, cv, audios, after):
+    count = len(audios)
+    arows = audios[0].shape[0] // 3
+    return call(
+        functools.partial(partial_kernel, groups, audio_mask, first), "partials",
+        [jax.ShapeDtypeStruct((size * arows, ck.shape[1] + HD), BF16) for _, size in groups],
+        [VM] * (2 + count) + [ANY] * len(after), [VM] * len(groups),
+        (ck, cv, *audios, *after), 8, flops=4 * count * arows * ck.size,
+    )
+
+
+def video_cross_kernel(count, audio_mask, first, cq, *refs):
+    audios, out = refs[:count], refs[-1]
+    for head in range(cq.shape[1] // HD):
+        columns = slice(head * HD, (head + 1) * HD)
+        key, value = [
+            jnp.concatenate([audio_of(audios, audio_mask, first, m, kind, head) for m in range(count)], axis=0)
+            for kind in range(2)
+        ]
+        _, total, numerator = softmax_times(nt(cq[:, columns], key), value)
+        out[:, columns] = (numerator / total).astype(BF16)
+
+
+def crossed(audio_mask, first, cq, audios, after):
+    count = len(audios)
+    return call(
+        functools.partial(video_cross_kernel, count, audio_mask, first), "video_cross",
+        jax.ShapeDtypeStruct(cq.shape, BF16), [VM] * (1 + count) + [ANY] * len(after), VM,
+        (cq, *audios, *after), 8, flops=4 * count * (audios[0].shape[0] // 3) * cq.size,
+    )
+
+
+def merge_kernel(last, pieces, *refs):
+    mine, came, outs = refs[:pieces], refs[pieces], refs[-pieces:]
+    at = 0
+    for one, out in zip(mine, outs):
+        rows, end = one.shape[0], one.shape[1] - HD
+        two = came.at[at : at + rows]
+        at += rows
+        levels = []
+        for head in range(end // HD):
+            columns = slice(head * HD, (head + 1) * HD)
+            left, right = level_of(one[:, end:], head), level_of(two[:, end:], head)
+            highest = jnp.maximum(left, right)
+            left, right = jnp.exp2(left - highest), jnp.exp2(right - highest)
+            mixed = one[:, columns].astype(F32) * left + two[:, columns].astype(F32) * right
+            out[:, columns] = (mixed / (left + right)).astype(BF16)
+            levels.append(highest + jnp.log2(left + right))
+        if not last:
+            out[:, end:] = stats_of(levels, rows)
+
+
+def merge(mine, came, last, after=()):
+    cut = HD if last else 0
+    shapes = [jax.ShapeDtypeStruct((x.shape[0], x.shape[1] - cut), BF16) for x in mine]
+    return call(
+        functools.partial(merge_kernel, last, len(mine)), "merge_last" if last else "merge", shapes,
+        [VM] * (len(mine) + 1) + [ANY] * len(after), [VM] * len(mine), (*mine, came, *after), 4,
+    )
+
+
+def exchanged(count, tensor, video_query, video_key, video_value, video_stream, out_weight,
+              cross_query, audio_key, audio_value, audio_query, cross_key, cross_value):
+    rows = video_query.shape[0]
+    share = out_weight.shape[1] // tensor
+    seq = [partner("seq", count, mask) for mask in range(count)]
+    order = list(range(count - 1, 0, -1))
+    audio_mask = 0
+
+    packs = [None] * count
+    sources = (video_query, video_key, video_value, audio_key, audio_value, audio_query)
+    *made, own_audio = pack(order + [0], count, audio_mask, *sources)
+    for mask, one in zip(order + [0], made):
+        packs[mask] = one
+    weight, cross_query, cross_key, cross_value, video_stream = fetch(
+        out_weight, cross_query, cross_key, cross_value, video_stream
+    )
+    for mask in order:
+        packs[mask] = seq[mask](packs[mask])
+    audios = [own_audio if mask in (0, audio_mask) else seq[mask](own_audio) for mask in range(count)]
+    if audio_mask:
+        audios[audio_mask] = packs[audio_mask]
+    heads = [None] * count
+    for index, mask in enumerate(order + [0]):
+        (heads[mask],) = attend([mask], order + [0], rows, packs, [weight], f"attend{index}")
+    own_heads = list(heads)
+    for mask in order:
+        heads[mask] = seq[mask](heads[mask])
+
+    groups = [(0, 1)] + [(1 << bit, 1 << bit) for bit in range(count.bit_length() - 1)]
+    pieces = partials(
+        groups, audio_mask, 3 * rows, cross_key, cross_value, audios, [own_heads[1]]
+    )
+    others = list(range(2, tensor, 2))
+    core = partner("tensor", tensor, 1)
+    sent = project(
+        order + [0], heads, weight, share, {mask + 1: BF16 for mask in others}, "project_far",
+        pieces[:1],
+    )
+    got = [core(x) for x in sent]
+    pieces = list(pieces)
+    kept = project(order + [0], heads, weight, share, {mask: F32 for mask in others}, "project_kept")
+    summed = [(mine + theirs.astype(F32)).astype(BF16) for mine, theirs in zip(kept, got)]
+    own, near = project(order + [0], heads, weight, share, {1: BF16, 0: F32}, "project_near", summed)
+    total = video_stream.astype(F32) + near + core(own).astype(F32)
+    for mask, piece in zip(others, summed):
+        total = total + partner("tensor", tensor, mask)(piece).astype(F32)
+    video_next = total.astype(BF16)
+    video_cross = crossed(audio_mask, 3 * rows, cross_query, audios, summed)
+    while len(pieces) > 2:
+        mask = groups[len(pieces) - 1][0]
+        came = seq[mask](pieces.pop())
+        pieces = list(merge(pieces, came, False, summed))
+    (audio_cross,) = merge(pieces[:1], seq[1](pieces[1]), True)
+    return video_next, video_cross, audio_cross
 
 
 def blank_state(query_rows, head_count):
@@ -50,7 +371,7 @@
     return result.transpose(1, 0, 2).reshape(result.shape[1], head_count * HD).astype(jnp.bfloat16)
 
 
-def local(
+def gathered(
     video_query,
     video_key,
     video_value,
@@ -107,22 +428,16 @@
 
 
 def solution(mesh):
-    in_specs = (
-        P(("groups", "seq"), "tensor"),
-        P(("groups", "seq"), "tensor"),
-        P(("groups", "seq"), "tensor"),
-        P(("groups", "seq"), "tensor"),
-        P("tensor", None),
-        P(("groups", "seq"), "tensor"),
-        P(("groups", "seq"), "tensor"),
-        P(("groups", "seq"), "tensor"),
-        P(("groups", "seq"), "tensor"),
-        P(("groups", "seq"), "tensor"),
-        P(("groups", "seq"), "tensor"),
-    )
-    out_specs = (
-        P(("groups", "seq"), "tensor"),
-        P(("groups", "seq"), "tensor"),
-        P(("groups", "seq"), "tensor"),
-    )
-    return jax.shard_map(local, mesh=mesh, in_specs=in_specs, out_specs=out_specs, check_vma=False)
+    count, tensor = mesh.shape["seq"], mesh.shape["tensor"]
+    both = P(("groups", "seq"), "tensor")
+    in_specs = (both,) * 4 + (P("tensor", None),) + (both,) * 6
+
+    def local(*arrays):
+        heads = arrays[0].shape[1] // HD
+        powers = all(n > 1 and n & (n - 1) == 0 for n in (count, tensor))
+        whole = heads % count == 0 and arrays[6].shape[0] % 16 == 0
+        if powers and whole and arrays[6].shape[1] % (arrays[0].shape[1] // count) == 0:
+            return exchanged(count, tensor, *arrays)
+        return gathered(*arrays)
+
+    return jax.shard_map(local, mesh=mesh, in_specs=in_specs, out_specs=(both,) * 3, check_vma=False)

time: 121 us -> 49.6 us (0.41)
  blocking collectives: 59.5 us -> 0 us
  starting transfers between devices: 0.12 us -> 27.3 us
  waiting for transfers between devices: 30 us -> 7.76 us
  between operations: 13.9 us -> 0.75 us
  Pallas kernels: 0 us -> 12.7 us
  matrix products: 9.9 us -> 0 us
  local copies, waits for them, and re-layouts: 4.99 us -> 0 us
  other arithmetic: 2.58 us -> 0.91 us
    all_gather x4 -> x0, blocking collectives: 59.5 us -> none  [the longest x1 15.4 us: local(): lax.all_gather(audio_value, 'seq', axis=0, tiled=True)]
    all_gather x2 -> x0, waiting for transfers between devices: 29.2 us -> none  [the longest x1 27.5 us: local(): lax.all_gather(video_value, 'seq', axis=0, tiled=True)]
    ppermute x0 -> x14, starting transfers between devices: none -> 27.3 us  [the longest x3 12.7 us: exchanged(): seq[mask](own_audio)]
    pallas_call x0 -> x13, Pallas kernels: none -> 12.7 us  [call(): pl.pallas_call(kernel, out_shape=shapes, in_specs=ins, out_specs=outs, sc...]
    dot_general x7 -> x0, matrix products: 9.9 us -> none  [the longest x1 5.7 us: local(): jnp.dot(attended, out_weight, preferred_element_type=jnp.float32)]
    ppermute x0 -> x14, waiting for transfers between devices: none -> 7.76 us  [the longest x3 2.9 us: exchanged(): packs[mask] = seq[mask](packs[mask])]
    unnamed x16 -> x0, local copies, waits for them, and re-layouts: 2.86 us -> none
    all_gather x1 -> x0, local copies, waits for them, and re-layouts: 1.49 us -> none  [local(): lax.all_gather(video_value, 'seq', axis=0, tiled=True)]
  transfers between devices with their start and end apart: 3 -> 14, of which waited for: 2 -> 7; matrix products, arithmetic and copies ran while one was open for 5% -> 0% of each run, Pallas kernels for 0% -> 22%
where the time goes in v2:
time: 49.6 us; the launch traced here: 49.4 us
  starting transfers between devices  27.3 us (55%)
  Pallas kernels  12.7 us (26%)
  waiting for transfers between devices  7.76 us (16%)
  other arithmetic  0.91 us (2%)
  between operations  0.75 us (2%)
    ppermute x3, starting transfers between devices, exchanged(): seq[mask](own_audio)  12.7 us
    pallas_call x13, Pallas kernels, call(): pl.pallas_call(kernel, out_shape=shapes, in_specs=ins, out_specs=outs, sc...  12.7 us
    ppermute x3, starting transfers between devices, exchanged(): packs[mask] = seq[mask](packs[mask])  5.76 us
    ppermute x3, starting transfers between devices, exchanged(): heads[mask] = seq[mask](heads[mask])  4.57 us
    ppermute x3, waiting for transfers between devices, exchanged(): packs[mask] = seq[mask](packs[mask])  2.9 us
    ppermute x1, waiting for transfers between devices, exchanged(): audio_cross, = merge(pieces[:1], seq[1](pieces[1]), True)  2.3 us
    ppermute x1, starting transfers between devices, exchanged(): came = seq[mask](pieces.pop())  2.27 us
    ppermute x1, starting transfers between devices, exchanged(): total = total + partner('tensor', tensor, mask)(piece).astype(F32)  1.55 us
  transfers between devices with their start and end apart: 14, of which 7 were waited for; matrix products, arithmetic and copies ran while one was open for 0% of the time, Pallas kernels for 22%

profile of v2, /device:TPU:0, one launch (start us, length us, event | category | flops | bytes accessed | tf_op | source)
XLA Modules:
  0.0 49.4 jit_solution(5039238981865404323)
XLA Ops:
  0.6 1.3 %pack.1 = (bf16[384,256]{1,0:T(8,128)(2,1)S(1)}, bf16[384,256]{1,0:T(8,128)(2,1)S(1)}, bf16[384,256]{1,0:T(8,128)(2,1)S(1)}, bf16[384,256]{1,0:T(8,128)(2,1)S(1)}, bf16[48,512]{1,0:T(8,128)(2,1)S(1)}) custom-call(bf16[128,1024]{1,0:T(8,128)(2,1)} %q.1, bf16[128,1024]{1,0:T(8,128)(2,1)} %k.1, bf16[128,1024]{1,0:T(8,128)(2,1)} %v.1, bf16[16,512]{1,0:T(8,128)(2,1)} %ak.1, ...), custom_call_target="tpu_custom_call" | custom-call | tf_op jit(solution)/shard_map/pack/pallas_call | solution.py:29
  2.0 5.1 %collective-permute-start = (bf16[384,256]{1,0:T(8,128)(2,1)S(1)}, bf16[384,256]{1,0:T(8,128)(2,1)S(1)}, u32[]{:S(2)}, u32[]{:S(2)}) collective-permute-start(bf16[384,256]{1,0:T(8,128)(2,1)S(1)} %get-tuple-element.21), channel_id=1, source_target_pairs={{0,12},{4,8},{8,4},{12,0},{1,13},{5,9},{9,5},{13,1},{2,14},{6,10},... | collective-permute-start | bytes 589832 | tf_op jit(solution)/shard_map/ppermute | solution.py:293
  7.1 0.6 %collective-permute-start.2 = (bf16[384,256]{1,0:T(8,128)(2,1)S(1)}, bf16[384,256]{1,0:T(8,128)(2,1)S(1)}, u32[]{:S(2)}, u32[]{:S(2)}) collective-permute-start(bf16[384,256]{1,0:T(8,128)(2,1)S(1)} %get-tuple-element.23), channel_id=1, source_target_pairs={{0,4},{4,0},{8,12},{12,8},{1,5},{5,1},{9,13},{13,9},{2,6},{6,2},{1... | collective-permute-start | bytes 589832 | tf_op jit(solution)/shard_map/ppermute | solution.py:293
  7.7 3.7 %collective-permute-start.8 = (bf16[48,512]{1,0:T(8,128)(2,1)S(1)}, bf16[48,512]{1,0:T(8,128)(2,1)S(1)}, u32[]{:S(2)}, u32[]{:S(2)}) collective-permute-start(bf16[48,512]{1,0:T(8,128)(2,1)S(1)} %get-tuple-element.28.refs_0_), channel_id=1, source_target_pairs={{0,12},{4,8},{8,4},{12,0},{1,13},{5,9},{9,5},{13,1},{2,14},{6,10},... | collective-permute-start | bytes 147464 | tf_op jit(solution)/shard_map/ppermute | solution.py:294
  11.5 1.5 %collective-permute-done.refs_0_ = bf16[384,256]{1,0:T(8,128)(2,1)S(1)} collective-permute-done((bf16[384,256]{1,0:T(8,128)(2,1)S(1)}, bf16[384,256]{1,0:T(8,128)(2,1)S(1)}, u32[]{:S(2)}, u32[]{:S(2)}) %collective-permute-start) | collective-permute-done | bytes 196640 | tf_op jit(solution)/shard_map/ppermute | solution.py:293
  12.9 9.0 %collective-permute-start.6 = (bf16[48,512]{1,0:T(8,128)(2,1)S(1)}, bf16[48,512]{1,0:T(8,128)(2,1)S(1)}, u32[]{:S(2)}, u32[]{:S(2)}) collective-permute-start(bf16[48,512]{1,0:T(8,128)(2,1)S(1)} %get-tuple-element.28.refs_0_), channel_id=1, source_target_pairs={{0,4},{4,0},{8,12},{12,8},{1,5},{5,1},{9,13},{13,9},{2,6},{6,2},{1... | collective-permute-start | bytes 147464 | tf_op jit(solution)/shard_map/ppermute | solution.py:294
  21.9 3.5 %fetch.1 = (bf16[1024,4096]{1,0:T(8,128)(2,1)S(1)}, bf16[128,512]{1,0:T(8,128)(2,1)S(1)}, bf16[128,512]{1,0:T(8,128)(2,1)S(1)}, bf16[128,512]{1,0:T(8,128)(2,1)S(1)}, bf16[128,1024]{1,0:T(8,128)(2,1)S(1)}) custom-call(bf16[1024,4096]{1,0:T(8,128)(2,1)} %refs_0_.1, bf16[128,512]{1,0:T(8,128)(2,1)} %refs_1_.1, bf16[128,512]{1,0:T(8,128)(2,1)} %refs_2_.1, ...), custom_call_target="tpu_custom_call" | custom-call | tf_op jit(solution)/shard_map/fetch/pallas_call | solution.py:29
  25.4 1.4 %collective-permute-done.1.refs_1_ = bf16[384,256]{1,0:T(8,128)(2,1)S(1)} collective-permute-done((bf16[384,256]{1,0:T(8,128)(2,1)S(1)}, bf16[384,256]{1,0:T(8,128)(2,1)S(1)}, u32[]{:S(2)}, u32[]{:S(2)}) %collective-permute-start.1) | collective-permute-done | bytes 196640 | tf_op jit(solution)/shard_map/ppermute | solution.py:293
  26.8 0.7 %attend0.1 = bf16[128,256]{1,0:T(8,128)(2,1)S(1)} custom-call(bf16[384,256]{1,0:T(8,128)(2,1)S(1)} %collective-permute-done.refs_0_, bf16[384,256]{1,0:T(8,128)(2,1)S(1)} %collective-permute-done.1.refs_1_, bf16[384,256]{1,0:T(8,128)(2,1)S(1)} %collective-permute-done.2.refs_2_, bf16[384,256]{1,0:T(8,128)(2,1)S(1)} %get-tuple-element.24.refs_3_, ...), custom_call_target="tpu_custom_call" | custom-call | flops 67108864 | tf_op jit(solution)/shard_map/attend0/pallas_call | solution.py:29
  27.5 2.7 %collective-permute-start.3 = (bf16[128,256]{1,0:T(8,128)(2,1)S(1)}, bf16[128,256]{1,0:T(8,128)(2,1)S(1)}, u32[]{:S(2)}, u32[]{:S(2)}) collective-permute-start(bf16[128,256]{1,0:T(8,128)(2,1)S(1)} %attend0.1), channel_id=1, source_target_pairs={{0,12},{4,8},{8,4},{12,0},{1,13},{5,9},{9,5},{13,1},{2,14},{6,10},... | collective-permute-start | bytes 196616 | tf_op jit(solution)/shard_map/ppermute | solution.py:302
  30.2 0.7 %attend1.1 = bf16[128,256]{1,0:T(8,128)(2,1)S(1)} custom-call(bf16[384,256]{1,0:T(8,128)(2,1)S(1)} %collective-permute-done.refs_0_, bf16[384,256]{1,0:T(8,128)(2,1)S(1)} %collective-permute-done.1.refs_1_, bf16[384,256]{1,0:T(8,128)(2,1)S(1)} %collective-permute-done.2.refs_2_, bf16[384,256]{1,0:T(8,128)(2,1)S(1)} %get-tuple-element.24.refs_3_, ...), custom_call_target="tpu_custom_call" | custom-call | flops 67108864 | tf_op jit(solution)/shard_map/attend1/pallas_call | solution.py:29
  31.0 0.7 %attend2.1.refs_4_ = bf16[128,256]{1,0:T(8,128)(2,1)S(1)} custom-call(bf16[384,256]{1,0:T(8,128)(2,1)S(1)} %collective-permute-done.refs_0_, bf16[384,256]{1,0:T(8,128)(2,1)S(1)} %collective-permute-done.1.refs_1_, bf16[384,256]{1,0:T(8,128)(2,1)S(1)} %collective-permute-done.2.refs_2_, bf16[384,256]{1,0:T(8,128)(2,1)S(1)} %get-tuple-element.24.refs_3_, ...), custom_call_target="tpu_custom_call" | custom-call | flops 67108864 | tf_op jit(solution)/shard_map/attend2/pallas_call | solution.py:29
  31.7 1.8 %collective-permute-start.5 = (bf16[128,256]{1,0:T(8,128)(2,1)S(1)}, bf16[128,256]{1,0:T(8,128)(2,1)S(1)}, u32[]{:S(2)}, u32[]{:S(2)}) collective-permute-start(bf16[128,256]{1,0:T(8,128)(2,1)S(1)} %attend2.1.refs_4_), channel_id=1, source_target_pairs={{0,4},{4,0},{8,12},{12,8},{1,5},{5,1},{9,13},{13,9},{2,6},{6,2},{1... | collective-permute-start | bytes 196616 | tf_op jit(solution)/shard_map/ppermute | solution.py:302
  33.5 1.1 %partials.1 = (bf16[16,640]{1,0:T(8,128)(2,1)S(1)}, bf16[16,640]{1,0:T(8,128)(2,1)S(1)}, bf16[32,640]{1,0:T(8,128)(2,1)S(1)}) custom-call(bf16[128,512]{1,0:T(8,128)(2,1)S(1)} %get-tuple-element.26.ck, bf16[128,512]{1,0:T(8,128)(2,1)S(1)} %get-tuple-element.27.cv, bf16[48,512]{1,0:T(8,128)(2,1)S(1)} %get-tuple-element.28.refs_0_, ...), custom_call_target="tpu_custom_call" | custom-call | flops 3000000000 | tf_op jit(solution)/shard_map/partials/pallas_call | solution.py:29
  34.5 0.7 %attend3.1.refs_3_ = bf16[128,256]{1,0:T(8,128)(2,1)S(1)} custom-call(bf16[384,256]{1,0:T(8,128)(2,1)S(1)} %collective-permute-done.refs_0_, bf16[384,256]{1,0:T(8,128)(2,1)S(1)} %collective-permute-done.1.refs_1_, bf16[384,256]{1,0:T(8,128)(2,1)S(1)} %collective-permute-done.2.refs_2_, bf16[384,256]{1,0:T(8,128)(2,1)S(1)} %get-tuple-element.24.refs_3_, ...), custom_call_target="tpu_custom_call" | custom-call | flops 67108864 | tf_op jit(solution)/shard_map/attend3/pallas_call | solution.py:29
  35.2 1.0 %collective-permute-done.4.refs_1_ = bf16[128,256]{1,0:T(8,128)(2,1)S(1)} collective-permute-done((bf16[128,256]{1,0:T(8,128)(2,1)S(1)}, bf16[128,256]{1,0:T(8,128)(2,1)S(1)}, u32[]{:S(2)}, u32[]{:S(2)}) %collective-permute-start.4) | collective-permute-done | bytes 65568 | tf_op jit(solution)/shard_map/ppermute | solution.py:302
  37.3 2.3 %collective-permute-start.12 = (bf16[32,640]{1,0:T(8,128)(2,1)S(1)}, bf16[32,640]{1,0:T(8,128)(2,1)S(1)}, u32[]{:S(2)}, u32[]{:S(2)}) collective-permute-start(bf16[32,640]{1,0:T(8,128)(2,1)S(1)} %get-tuple-element.34), channel_id=1, source_target_pairs={{0,8},{4,12},{8,0},{12,4},{1,9},{5,13},{9,1},{13,5},{2,10},{6,14},... | collective-permute-start | bytes 122888 | tf_op jit(solution)/shard_map/ppermute | solution.py:326
  40.1 1.6 %collective-permute-start.11 = (bf16[128,1024]{1,0:T(8,128)(2,1)S(1)}, bf16[128,1024]{1,0:T(8,128)(2,1)S(1)}, u32[]{:S(2)}, u32[]{:S(2)}) collective-permute-start(bf16[128,1024]{1,0:T(8,128)(2,1)S(1)} %add_convert_fusion.1.refs_5_.refs_4_.refs_3_), channel_id=1, source_target_pairs={{0,2},{1,3},{2,0},{3,1},{4,6},{5,7},{6,4},{7,5},{8,10},{9,11},{10,... | collective-permute-start | bytes 786440 | tf_op jit(solution)/shard_map/ppermute | solution.py:321
  41.7 0.7 %project_near.1 = (bf16[128,1024]{1,0:T(8,128)(2,1)S(1)}, f32[128,1024]{1,0:T(8,128)S(1)}) custom-call(bf16[128,256]{1,0:T(8,128)(2,1)S(1)} %collective-permute-done.3.refs_0_, bf16[128,256]{1,0:T(8,128)(2,1)S(1)} %collective-permute-done.4.refs_1_, bf16[128,256]{1,0:T(8,128)(2,1)S(1)} %collective-permute-done.5.refs_2_, ...), custom_call_target="tpu_custom_call" | custom-call | flops 536870912 | tf_op jit(solution)/shard_map/project_near/pallas_call | solution.py:29
  42.5 0.5 %collective-permute-done.12.refs_2_ = bf16[32,640]{1,0:T(8,128)(2,1)S(1)} collective-permute-done((bf16[32,640]{1,0:T(8,128)(2,1)S(1)}, bf16[32,640]{1,0:T(8,128)(2,1)S(1)}, u32[]{:S(2)}, u32[]{:S(2)}) %collective-permute-start.12) | collective-permute-done | bytes 40992 | tf_op jit(solution)/shard_map/ppermute | solution.py:326
  43.7 1.3 %video_cross.1 = bf16[128,512]{1,0:T(8,128)(2,1)} custom-call(bf16[128,512]{1,0:T(8,128)(2,1)S(1)} %get-tuple-element.32.cq, bf16[48,512]{1,0:T(8,128)(2,1)S(1)} %get-tuple-element.28.refs_0_, bf16[48,512]{1,0:T(8,128)(2,1)S(1)} %collective-permute-done.6.refs_1_, bf16[48,512]{1,0:T(8,128)(2,1)S(1)} %collective-permute-done.7.refs_2_, ...), custom_call_target="tpu_custom_call" | custom-call | flops 16777216 | tf_op jit(solution)/shard_map/video_cross/pallas_call | solution.py:29
  45.0 2.3 %collective-permute-done.13.refs_1_ = bf16[16,640]{1,0:T(8,128)(2,1)S(1)} collective-permute-done((bf16[16,640]{1,0:T(8,128)(2,1)S(1)}, bf16[16,640]{1,0:T(8,128)(2,1)S(1)}, u32[]{:S(2)}, u32[]{:S(2)}) %collective-permute-start.13) | collective-permute-done | bytes 20512 | tf_op jit(solution)/shard_map/ppermute | solution.py:328
  47.2 0.8 %merge_last.1 = bf16[16,512]{1,0:T(8,128)(2,1)} custom-call(bf16[16,640]{1,0:T(8,128)(2,1)S(1)} %get-tuple-element.35.refs_0_, bf16[16,640]{1,0:T(8,128)(2,1)S(1)} %collective-permute-done.13.refs_1_), custom_call_target="tpu_custom_call" | custom-call | tf_op jit(solution)/shard_map/merge_last/pallas_call | solution.py:29
  48.5 0.8 %add_convert_fusion = bf16[128,1024]{1,0:T(8,128)(2,1)} fusion(bf16[128,1024]{1,0:T(8,128)(2,1)S(1)} %collective-permute-done.11, bf16[128,1024]{1,0:T(8,128)(2,1)S(1)} %collective-permute-done.10, f32[128,1024]{1,0:T(8,128)S(1)} %get-tuple-element.30, bf16[128,1024]{1,0:T(8,128)(2,1)S(1)} %get-tuple-element.20), kind=kLoop, calls=%fused_computation | loop fusion | flops 917504 | bytes 1572864 | tf_op jit(solution)/shard_map/convert_element_type | solution.py:322
  (19 shorter events, 2.9 us)
Async XLA Ops:
  2.0 11.0 %collective-permute-start = (bf16[384,256]{1,0:T(8,128)(2,1)S(1)}, bf16[384,256]{1,0:T(8,128)(2,1)S(1)}, u32[]{:S(2)}, u32[]{:S(2)}) collective-permute-start(bf16[384,256]{1,0:T(8,128)(2,1)S(1)} %get-tuple-element.21), channel_id=1, source_target_pairs={{0,12},{4,8},{8,4},{12,0},{1,13},{5,9},{9,5},{13,1},{2,14},{6,10},... | collective-permute-start | bytes 589832 | tf_op jit(solution)/shard_map/ppermute | solution.py:293
  7.1 19.8 %collective-permute-start.1 = (bf16[384,256]{1,0:T(8,128)(2,1)S(1)}, bf16[384,256]{1,0:T(8,128)(2,1)S(1)}, u32[]{:S(2)}, u32[]{:S(2)}) collective-permute-start(bf16[384,256]{1,0:T(8,128)(2,1)S(1)} %get-tuple-element.22), channel_id=1, source_target_pairs={{0,8},{4,12},{8,0},{12,4},{1,9},{5,13},{9,1},{13,5},{2,10},{6,14},... | collective-permute-start | bytes 589832 | tf_op jit(solution)/shard_map/ppermute | solution.py:293
  7.1 19.8 %collective-permute-start.2 = (bf16[384,256]{1,0:T(8,128)(2,1)S(1)}, bf16[384,256]{1,0:T(8,128)(2,1)S(1)}, u32[]{:S(2)}, u32[]{:S(2)}) collective-permute-start(bf16[384,256]{1,0:T(8,128)(2,1)S(1)} %get-tuple-element.23), channel_id=1, source_target_pairs={{0,4},{4,0},{8,12},{12,8},{1,5},{5,1},{9,13},{13,9},{2,6},{6,2},{1... | collective-permute-start | bytes 589832 | tf_op jit(solution)/shard_map/ppermute | solution.py:293
  7.7 24.0 %collective-permute-start.8 = (bf16[48,512]{1,0:T(8,128)(2,1)S(1)}, bf16[48,512]{1,0:T(8,128)(2,1)S(1)}, u32[]{:S(2)}, u32[]{:S(2)}) collective-permute-start(bf16[48,512]{1,0:T(8,128)(2,1)S(1)} %get-tuple-element.28.refs_0_), channel_id=1, source_target_pairs={{0,12},{4,8},{8,4},{12,0},{1,13},{5,9},{9,5},{13,1},{2,14},{6,10},... | collective-permute-start | bytes 147464 | tf_op jit(solution)/shard_map/ppermute | solution.py:294
  11.5 22.0 %collective-permute-start.7 = (bf16[48,512]{1,0:T(8,128)(2,1)S(1)}, bf16[48,512]{1,0:T(8,128)(2,1)S(1)}, u32[]{:S(2)}, u32[]{:S(2)}) collective-permute-start(bf16[48,512]{1,0:T(8,128)(2,1)S(1)} %get-tuple-element.28.refs_0_), channel_id=1, source_target_pairs={{0,8},{4,12},{8,0},{12,4},{1,9},{5,13},{9,1},{13,5},{2,10},{6,14},... | collective-permute-start | bytes 147464 | tf_op jit(solution)/shard_map/ppermute | solution.py:294
  12.9 20.5 %collective-permute-start.6 = (bf16[48,512]{1,0:T(8,128)(2,1)S(1)}, bf16[48,512]{1,0:T(8,128)(2,1)S(1)}, u32[]{:S(2)}, u32[]{:S(2)}) collective-permute-start(bf16[48,512]{1,0:T(8,128)(2,1)S(1)} %get-tuple-element.28.refs_0_), channel_id=1, source_target_pairs={{0,4},{4,0},{8,12},{12,8},{1,5},{5,1},{9,13},{13,9},{2,6},{6,2},{1... | collective-permute-start | bytes 147464 | tf_op jit(solution)/shard_map/ppermute | solution.py:294
  27.5 7.7 %collective-permute-start.3 = (bf16[128,256]{1,0:T(8,128)(2,1)S(1)}, bf16[128,256]{1,0:T(8,128)(2,1)S(1)}, u32[]{:S(2)}, u32[]{:S(2)}) collective-permute-start(bf16[128,256]{1,0:T(8,128)(2,1)S(1)} %attend0.1), channel_id=1, source_target_pairs={{0,12},{4,8},{8,4},{12,0},{1,13},{5,9},{9,5},{13,1},{2,14},{6,10},... | collective-permute-start | bytes 196616 | tf_op jit(solution)/shard_map/ppermute | solution.py:302
  30.9 5.3 %collective-permute-start.4 = (bf16[128,256]{1,0:T(8,128)(2,1)S(1)}, bf16[128,256]{1,0:T(8,128)(2,1)S(1)}, u32[]{:S(2)}, u32[]{:S(2)}) collective-permute-start(bf16[128,256]{1,0:T(8,128)(2,1)S(1)} %attend1.1), channel_id=1, source_target_pairs={{0,8},{4,12},{8,0},{12,4},{1,9},{5,13},{9,1},{13,5},{2,10},{6,14},... | collective-permute-start | bytes 196616 | tf_op jit(solution)/shard_map/ppermute | solution.py:302
  31.7 5.0 %collective-permute-start.5 = (bf16[128,256]{1,0:T(8,128)(2,1)S(1)}, bf16[128,256]{1,0:T(8,128)(2,1)S(1)}, u32[]{:S(2)}, u32[]{:S(2)}) collective-permute-start(bf16[128,256]{1,0:T(8,128)(2,1)S(1)} %attend2.1.refs_4_), channel_id=1, source_target_pairs={{0,4},{4,0},{8,12},{12,8},{1,5},{5,1},{9,13},{13,9},{2,6},{6,2},{1... | collective-permute-start | bytes 196616 | tf_op jit(solution)/shard_map/ppermute | solution.py:302
  37.2 2.8 %collective-permute-start.9 = (bf16[128,1024]{1,0:T(8,128)(2,1)S(1)}, bf16[128,1024]{1,0:T(8,128)(2,1)S(1)}, u32[]{:S(2)}, u32[]{:S(2)}) collective-permute-start(bf16[128,1024]{1,0:T(8,128)(2,1)S(1)} %project_far.1), channel_id=1, source_target_pairs={{0,1},{1,0},{2,3},{3,2},{4,5},{5,4},{6,7},{7,6},{8,9},{9,8},{10,11... | collective-permute-start | bytes 786440 | tf_op jit(solution)/shard_map/ppermute | solution.py:314
  37.3 5.8 %collective-permute-start.12 = (bf16[32,640]{1,0:T(8,128)(2,1)S(1)}, bf16[32,640]{1,0:T(8,128)(2,1)S(1)}, u32[]{:S(2)}, u32[]{:S(2)}) collective-permute-start(bf16[32,640]{1,0:T(8,128)(2,1)S(1)} %get-tuple-element.34), channel_id=1, source_target_pairs={{0,8},{4,12},{8,0},{12,4},{1,9},{5,13},{9,1},{13,5},{2,10},{6,14},... | collective-permute-start | bytes 122888 | tf_op jit(solution)/shard_map/ppermute | solution.py:326
  40.1 8.4 %collective-permute-start.11 = (bf16[128,1024]{1,0:T(8,128)(2,1)S(1)}, bf16[128,1024]{1,0:T(8,128)(2,1)S(1)}, u32[]{:S(2)}, u32[]{:S(2)}) collective-permute-start(bf16[128,1024]{1,0:T(8,128)(2,1)S(1)} %add_convert_fusion.1.refs_5_.refs_4_.refs_3_), channel_id=1, source_target_pairs={{0,2},{1,3},{2,0},{3,1},{4,6},{5,7},{6,4},{7,5},{8,10},{9,11},{10,... | collective-permute-start | bytes 786440 | tf_op jit(solution)/shard_map/ppermute | solution.py:321
  42.4 5.6 %collective-permute-start.10 = (bf16[128,1024]{1,0:T(8,128)(2,1)S(1)}, bf16[128,1024]{1,0:T(8,128)(2,1)S(1)}, u32[]{:S(2)}, u32[]{:S(2)}) collective-permute-start(bf16[128,1024]{1,0:T(8,128)(2,1)S(1)} %get-tuple-element.31), channel_id=1, source_target_pairs={{0,1},{1,0},{2,3},{3,2},{4,5},{5,4},{6,7},{7,6},{8,9},{9,8},{10,11... | collective-permute-start | bytes 786440 | tf_op jit(solution)/shard_map/ppermute | solution.py:319
  43.4 3.8 %collective-permute-start.13 = (bf16[16,640]{1,0:T(8,128)(2,1)S(1)}, bf16[16,640]{1,0:T(8,128)(2,1)S(1)}, u32[]{:S(2)}, u32[]{:S(2)}) collective-permute-start(bf16[16,640]{1,0:T(8,128)(2,1)S(1)} %get-tuple-element.36), channel_id=1, source_target_pairs={{0,4},{4,0},{8,12},{12,8},{1,5},{5,1},{9,13},{13,9},{2,6},{6,2},{1... | collective-permute-start | bytes 61448 | tf_op jit(solution)/shard_map/ppermute | solution.py:328

commit v3 on v2

--- a/solution.py
+++ b/solution.py
@@ -56,46 +56,26 @@
     return highest, total, numerator
 
 
-def pack_kernel(masks, count, audio_mask, q, k, v, ak, av, aq, *rest):
-    own_audio = rest[-2] if audio_mask in masks else None
-    outs, sem = rest[-1 - len(masks) - (own_audio is not None) :], rest[-1]
-    rows, arows = q.shape[0], aq.shape[0]
-    width = q.shape[1] // count
+def pack_kernel(masks, count, q, k, v, *rest):
+    outs, sem = rest[:-1], rest[-1]
+    rows, width = q.shape[0], q.shape[1] // count
     z = lax.axis_index("seq")
     copies = []
-
-    def copy(source, target):
-        copies.append(pltpu.make_async_copy(source, target, sem.at[len(copies)]))
-        copies[-1].start()
-
     for mask, out in zip(masks, outs):
         columns = pl.ds(pl.multiple_of(jnp.bitwise_xor(z, mask) * width, width), width)
         for position, source in enumerate((q, k, v)):
-            copy(source.at[:, columns], out.at[pl.ds(position * rows, rows)])
-    if own_audio is not None:
-        for position, source in enumerate((ak, av, aq)):
-            copy(source, own_audio.at[pl.ds(position * arows, arows)])
-            for block in range(aq.shape[1] // width if audio_mask else 0):
-                copy(
-                    source.at[:, pl.ds(block * width, width)],
-                    outs[masks.index(audio_mask)].at[pl.ds(3 * rows + (3 * block + position) * arows, arows)],
-                )
+            target = out.at[pl.ds(position * rows, rows)]
+            copies.append(pltpu.make_async_copy(source.at[:, columns], target, sem.at[len(copies)]))
+            copies[-1].start()
     for one in copies:
         one.wait()
 
 
-def pack(masks, count, audio_mask, q, k, v, ak, av, aq, after=()):
-    rows, width = q.shape[0], q.shape[1] // count
-    below = 3 * aq.size // width
-    shapes = [pltpu.VMEM((3 * rows + (below if mask == audio_mask and mask else 0), width), BF16) for mask in masks]
-    copies = 3 * len(masks)
-    if audio_mask in masks:
-        shapes.append(pltpu.VMEM((3 * aq.shape[0], aq.shape[1]), BF16))
-        copies += 3 + (3 * aq.shape[1] // width if audio_mask else 0)
-    return call(
-        functools.partial(pack_kernel, masks, count, audio_mask), "pack", shapes,
-        [HBM] * 6 + [ANY] * len(after), [VM] * len(shapes), (q, k, v, ak, av, aq, *after),
-        WHOLE_VMEM, [pltpu.SemaphoreType.DMA((copies,))],
+def pack(masks, count, q, k, v):
+    shape = pltpu.VMEM((3 * q.shape[0], q.shape[1] // count), BF16)
+    return call(
+        functools.partial(pack_kernel, masks, count), "pack", [shape] * len(masks), [HBM] * 3, [VM] * len(masks),
+        (q, k, v), WHOLE_VMEM, [pltpu.SemaphoreType.DMA((3 * len(masks),))],
     )
 
 
@@ -122,20 +102,23 @@
 
 
 def fetch_kernel(count, *refs):
-    copies = [
-        pltpu.make_async_copy(refs[i], refs[count + i], refs[-1].at[i]) for i in range(count)
-    ]
+    pairs = list(zip(refs[:count], refs[count + 3 : 2 * count + 3]))
+    own_audio, rows = refs[2 * count + 3], refs[count].shape[0]
+    pairs += [(one, own_audio.at[pl.ds(kind * rows, rows)]) for kind, one in enumerate(refs[count : count + 3])]
+    copies = [pltpu.make_async_copy(*pair, refs[-1].at[i]) for i, pair in enumerate(pairs)]
     for one in copies:
         one.start()
     for one in copies:
         one.wait()
 
 
-def fetch(*arrays):
+def fetch(arrays, audio):
     count = len(arrays)
-    return call(
-        functools.partial(fetch_kernel, count), "fetch", [pltpu.VMEM(x.shape, x.dtype) for x in arrays],
-        [HBM] * count, [VM] * count, arrays, 53, [pltpu.SemaphoreType.DMA((count,))],
+    shapes = [pltpu.VMEM(x.shape, x.dtype) for x in arrays]
+    shapes.append(pltpu.VMEM((3 * audio[0].shape[0], audio[0].shape[1]), BF16))
+    return call(
+        functools.partial(fetch_kernel, count), "fetch", shapes, [HBM] * (count + 3), [VM] * (count + 1),
+        (*arrays, *audio), 53, [pltpu.SemaphoreType.DMA((count + 3,))],
     )
 
 
@@ -184,16 +167,13 @@
     return jnp.sum(stats[:, 3 * head : 3 * head + 3].astype(F32), axis=1, keepdims=True)
 
 
-def audio_of(audios, audio_mask, first, mask, kind, head):
-    arows = audios[0].shape[0] // 3
-    ref, at, column = audios[mask], kind * arows, head * HD
-    if mask and mask == audio_mask:
-        block, column = divmod(column, ref.shape[1])
-        at += first + 3 * block * arows
-    return ref[at : at + arows, column : column + HD]
-
-
-def partial_kernel(groups, audio_mask, first, ck, cv, *refs):
+def audio_of(audios, kind, head):
+    rows = audios[0].shape[0] // 3
+    here = (slice(kind * rows, (kind + 1) * rows), slice(head * HD, (head + 1) * HD))
+    return jnp.concatenate([one[here] for one in audios], axis=0)
+
+
+def partial_kernel(groups, ck, cv, *refs):
     count = sum(size for _, size in groups)
     audios, parts = refs[:count], refs[-len(groups) :]
     arows = audios[0].shape[0] // 3
@@ -201,8 +181,7 @@
     levels = []
     for head in range(heads):
         columns = slice(head * HD, (head + 1) * HD)
-        query = jnp.concatenate([audio_of(audios, audio_mask, first, m, 2, head) for m in range(count)], axis=0)
-        highest, total, numerator = softmax_times(nt(query, ck[:, columns]), cv[:, columns])
+        highest, total, numerator = softmax_times(nt(audio_of(audios, 2, head), ck[:, columns]), cv[:, columns])
         partial = (numerator / total).astype(BF16)
         levels.append(highest * (FACTOR * LOG2E) + jnp.log2(total))
         for (start, size), part in zip(groups, parts):
@@ -212,33 +191,29 @@
         part[:, heads * HD :] = stats[start * arows : (start + size) * arows]
 
 
-def partials(groups, audio_mask, first, ck, cv, audios, after):
+def partials(groups, ck, cv, audios, after):
     count = len(audios)
     arows = audios[0].shape[0] // 3
     return call(
-        functools.partial(partial_kernel, groups, audio_mask, first), "partials",
+        functools.partial(partial_kernel, groups), "partials",
         [jax.ShapeDtypeStruct((size * arows, ck.shape[1] + HD), BF16) for _, size in groups],
         [VM] * (2 + count) + [ANY] * len(after), [VM] * len(groups),
         (ck, cv, *audios, *after), 8, flops=4 * count * arows * ck.size,
     )
 
 
-def video_cross_kernel(count, audio_mask, first, cq, *refs):
+def video_cross_kernel(count, cq, *refs):
     audios, out = refs[:count], refs[-1]
     for head in range(cq.shape[1] // HD):
         columns = slice(head * HD, (head + 1) * HD)
-        key, value = [
-            jnp.concatenate([audio_of(audios, audio_mask, first, m, kind, head) for m in range(count)], axis=0)
-            for kind in range(2)
-        ]
-        _, total, numerator = softmax_times(nt(cq[:, columns], key), value)
+        _, total, numerator = softmax_times(nt(cq[:, columns], audio_of(audios, 0, head)), audio_of(audios, 1, head))
         out[:, columns] = (numerator / total).astype(BF16)
 
 
-def crossed(audio_mask, first, cq, audios, after):
+def crossed(cq, audios, after):
     count = len(audios)
     return call(
-        functools.partial(video_cross_kernel, count, audio_mask, first), "video_cross",
+        functools.partial(video_cross_kernel, count), "video_cross",
         jax.ShapeDtypeStruct(cq.shape, BF16), [VM] * (1 + count) + [ANY] * len(after), VM,
         (cq, *audios, *after), 8, flops=4 * count * (audios[0].shape[0] // 3) * cq.size,
     )
@@ -279,21 +254,21 @@
     share = out_weight.shape[1] // tensor
     seq = [partner("seq", count, mask) for mask in range(count)]
     order = list(range(count - 1, 0, -1))
-    audio_mask = 0
 
     packs = [None] * count
-    sources = (video_query, video_key, video_value, audio_key, audio_value, audio_query)
-    *made, own_audio = pack(order + [0], count, audio_mask, *sources)
-    for mask, one in zip(order + [0], made):
+    for mask, one in zip(order + [0], pack(order + [0], count, video_query, video_key, video_value)):
         packs[mask] = one
-    weight, cross_query, cross_key, cross_value, video_stream = fetch(
-        out_weight, cross_query, cross_key, cross_value, video_stream
+    weight, cross_query, cross_key, cross_value, video_stream, own_audio = fetch(
+        (out_weight, cross_query, cross_key, cross_value, video_stream), (audio_key, audio_value, audio_query)
     )
     for mask in order:
         packs[mask] = seq[mask](packs[mask])
-    audios = [own_audio if mask in (0, audio_mask) else seq[mask](own_audio) for mask in range(count)]
-    if audio_mask:
-        audios[audio_mask] = packs[audio_mask]
+    audios = [own_audio]
+    for mask in range(1, count):
+        if mask % 2 and mask > 1:
+            audios.append(seq[1](audios[mask - 1]))
+        else:
+            audios.append(seq[mask](own_audio))
     heads = [None] * count
     for index, mask in enumerate(order + [0]):
         (heads[mask],) = attend([mask], order + [0], rows, packs, [weight], f"attend{index}")
@@ -303,28 +278,25 @@
 
     groups = [(0, 1)] + [(1 << bit, 1 << bit) for bit in range(count.bit_length() - 1)]
     pieces = partials(
-        groups, audio_mask, 3 * rows, cross_key, cross_value, audios, [own_heads[1]]
+        groups, cross_key, cross_value, audios, [own_heads[1]]
     )
     others = list(range(2, tensor, 2))
     core = partner("tensor", tensor, 1)
-    sent = project(
-        order + [0], heads, weight, share, {mask + 1: BF16 for mask in others}, "project_far",
-        pieces[:1],
-    )
+    pieces = list(pieces)
+    sent = project(order + [0], heads, weight, share, {mask + 1: BF16 for mask in others}, "project_far", pieces[:1])
     got = [core(x) for x in sent]
-    pieces = list(pieces)
-    kept = project(order + [0], heads, weight, share, {mask: F32 for mask in others}, "project_kept")
+    kept = project(order + [0], heads, weight, share, {mask: F32 for mask in others}, "project_kept", sent[:1])
     summed = [(mine + theirs.astype(F32)).astype(BF16) for mine, theirs in zip(kept, got)]
     own, near = project(order + [0], heads, weight, share, {1: BF16, 0: F32}, "project_near", summed)
     total = video_stream.astype(F32) + near + core(own).astype(F32)
     for mask, piece in zip(others, summed):
         total = total + partner("tensor", tensor, mask)(piece).astype(F32)
     video_next = total.astype(BF16)
-    video_cross = crossed(audio_mask, 3 * rows, cross_query, audios, summed)
+    video_cross = crossed(cross_query, audios, summed)
     while len(pieces) > 2:
         mask = groups[len(pieces) - 1][0]
-        came = seq[mask](pieces.pop())
-        pieces = list(merge(pieces, came, False, summed))
+        other = seq[mask](pieces.pop())
+        pieces = list(merge(pieces, other, False, summed))
     (audio_cross,) = merge(pieces[:1], seq[1](pieces[1]), True)
     return video_next, video_cross, audio_cross
 
@@ -435,8 +407,7 @@
     def local(*arrays):
         heads = arrays[0].shape[1] // HD
         powers = all(n > 1 and n & (n - 1) == 0 for n in (count, tensor))
-        whole = heads % count == 0 and arrays[6].shape[0] % 16 == 0
-        if powers and whole and arrays[6].shape[1] % (arrays[0].shape[1] // count) == 0:
+        if powers and heads % count == 0 and arrays[6].shape[0] % 16 == 0:
             return exchanged(count, tensor, *arrays)
         return gathered(*arrays)
 

time: 49.6 us -> 48.4 us (0.976)
  starting transfers between devices: 27.3 us -> 18.5 us
  waiting for transfers between devices: 7.76 us -> 15.4 us
    ppermute x4, waiting for transfers between devices: 0.55 us -> 11.3 us  [the longest x2 10.3 us: exchanged(): audios.append(seq[mask](own_audio))]
    ppermute x4, starting transfers between devices: 15 us -> 6.17 us  [the longest x2 4.37 us: exchanged(): audios.append(seq[mask](own_audio))]
    ppermute x3, waiting for transfers between devices: 2.9 us -> 0.01 us  [exchanged(): packs[mask] = seq[mask](packs[mask])]
  transfers between devices with their start and end apart: 14 -> 14, of which waited for: 7 -> 5; matrix products, arithmetic and copies ran while one was open for 0% -> 0% of each run, Pallas kernels for 22% -> 23%
where the time goes in v3:
time: 48.4 us; the launch traced here: 48.2 us
  starting transfers between devices  18.5 us (38%)
  waiting for transfers between devices  15.4 us (32%)
  Pallas kernels  12.7 us (26%)
  other arithmetic  0.91 us (2%)
  between operations  0.76 us (2%)
    pallas_call x13, Pallas kernels, call(): pl.pallas_call(kernel, out_shape=shapes, in_specs=ins, out_specs=outs, sc...  12.7 us
    ppermute x2, waiting for transfers between devices, exchanged(): audios.append(seq[mask](own_audio))  10.3 us
    ppermute x3, starting transfers between devices, exchanged(): packs[mask] = seq[mask](packs[mask])  5.76 us
    ppermute x3, starting transfers between devices, exchanged(): heads[mask] = seq[mask](heads[mask])  4.58 us
    ppermute x2, starting transfers between devices, exchanged(): audios.append(seq[mask](own_audio))  4.37 us
    ppermute x1, waiting for transfers between devices, exchanged(): audio_cross, = merge(pieces[:1], seq[1](pieces[1]), True)  2.26 us
    ppermute x3, waiting for transfers between devices, exchanged(): heads[mask] = seq[mask](heads[mask])  1.8 us
    ppermute x1, starting transfers between devices, exchanged(): other = seq[mask](pieces.pop())  1.79 us
  transfers between devices with their start and end apart: 14, of which 5 were waited for; matrix products, arithmetic and copies ran while one was open for 0% of the time, Pallas kernels for 23%

profile of v3, /device:TPU:0, one launch (start us, length us, event | category | flops | bytes accessed | tf_op | source)
XLA Modules:
  0.0 48.2 jit_solution(9246614761128352860)
XLA Ops:
  0.6 1.3 %pack.1 = (bf16[384,256]{1,0:T(8,128)(2,1)S(1)}, bf16[384,256]{1,0:T(8,128)(2,1)S(1)}, bf16[384,256]{1,0:T(8,128)(2,1)S(1)}, bf16[384,256]{1,0:T(8,128)(2,1)S(1)}) custom-call(bf16[128,1024]{1,0:T(8,128)(2,1)} %q.1, bf16[128,1024]{1,0:T(8,128)(2,1)} %k.1, bf16[128,1024]{1,0:T(8,128)(2,1)} %v.1), custom_call_target="tpu_custom_call" | custom-call | tf_op jit(solution)/shard_map/pack/pallas_call | solution.py:29
  1.9 5.1 %collective-permute-start = (bf16[384,256]{1,0:T(8,128)(2,1)S(1)}, bf16[384,256]{1,0:T(8,128)(2,1)S(1)}, u32[]{:S(2)}, u32[]{:S(2)}) collective-permute-start(bf16[384,256]{1,0:T(8,128)(2,1)S(1)} %get-tuple-element.21), channel_id=1, source_target_pairs={{0,12},{4,8},{8,4},{12,0},{1,13},{5,9},{9,5},{13,1},{2,14},{6,10},... | collective-permute-start | bytes 589832 | tf_op jit(solution)/shard_map/ppermute | solution.py:265
  7.0 0.6 %collective-permute-start.2 = (bf16[384,256]{1,0:T(8,128)(2,1)S(1)}, bf16[384,256]{1,0:T(8,128)(2,1)S(1)}, u32[]{:S(2)}, u32[]{:S(2)}) collective-permute-start(bf16[384,256]{1,0:T(8,128)(2,1)S(1)} %get-tuple-element.23), channel_id=1, source_target_pairs={{0,4},{4,0},{8,12},{12,8},{1,5},{5,1},{9,13},{13,9},{2,6},{6,2},{1... | collective-permute-start | bytes 589832 | tf_op jit(solution)/shard_map/ppermute | solution.py:265
  7.7 3.5 %fetch.1 = (bf16[1024,4096]{1,0:T(8,128)(2,1)S(1)}, bf16[128,512]{1,0:T(8,128)(2,1)S(1)}, bf16[128,512]{1,0:T(8,128)(2,1)S(1)}, bf16[128,512]{1,0:T(8,128)(2,1)S...) custom-call(bf16[1024,4096]{1,0:T(8,128)(2,1)} %refs_0_.1, bf16[128,512]{1,0:T(8,128)(2,1)} %refs_1_.1, ...), custom_call_target="tpu_custom_call" | custom-call | tf_op jit(solution)/shard_map/fetch/pallas_call | solution.py:29
  11.2 2.4 %collective-permute-start.7 = (bf16[48,512]{1,0:T(8,128)(2,1)S(1)}, bf16[48,512]{1,0:T(8,128)(2,1)S(1)}, u32[]{:S(2)}, u32[]{:S(2)}) collective-permute-start(bf16[48,512]{1,0:T(8,128)(2,1)S(1)} %get-tuple-element.28.refs_0_), channel_id=1, source_target_pairs={{0,8},{4,12},{8,0},{12,4},{1,9},{5,13},{9,1},{13,5},{2,10},{6,14},... | collective-permute-start | bytes 147464 | tf_op jit(solution)/shard_map/ppermute | solution.py:271
  13.6 2.0 %collective-permute-start.6 = (bf16[48,512]{1,0:T(8,128)(2,1)S(1)}, bf16[48,512]{1,0:T(8,128)(2,1)S(1)}, u32[]{:S(2)}, u32[]{:S(2)}) collective-permute-start(bf16[48,512]{1,0:T(8,128)(2,1)S(1)} %get-tuple-element.28.refs_0_), channel_id=1, source_target_pairs={{0,4},{4,0},{8,12},{12,8},{1,5},{5,1},{9,13},{13,9},{2,6},{6,2},{1... | collective-permute-start | bytes 147464 | tf_op jit(solution)/shard_map/ppermute | solution.py:271
  15.6 10.3 %collective-permute-done.7.refs_2_ = bf16[48,512]{1,0:T(8,128)(2,1)S(1)} collective-permute-done((bf16[48,512]{1,0:T(8,128)(2,1)S(1)}, bf16[48,512]{1,0:T(8,128)(2,1)S(1)}, u32[]{:S(2)}, u32[]{:S(2)}) %collective-permute-start.7) | collective-permute-done | bytes 49184 | tf_op jit(solution)/shard_map/ppermute | solution.py:271
  25.9 0.7 %attend0.1 = bf16[128,256]{1,0:T(8,128)(2,1)S(1)} custom-call(bf16[384,256]{1,0:T(8,128)(2,1)S(1)} %collective-permute-done.refs_0_, bf16[384,256]{1,0:T(8,128)(2,1)S(1)} %collective-permute-done.1.refs_1_, bf16[384,256]{1,0:T(8,128)(2,1)S(1)} %collective-permute-done.2.refs_2_, bf16[384,256]{1,0:T(8,128)(2,1)S(1)} %get-tuple-element.24.refs_3_, ...), custom_call_target="tpu_custom_call" | custom-call | flops 67108864 | tf_op jit(solution)/shard_map/attend0/pallas_call | solution.py:29
  26.5 2.5 %collective-permute-start.3 = (bf16[128,256]{1,0:T(8,128)(2,1)S(1)}, bf16[128,256]{1,0:T(8,128)(2,1)S(1)}, u32[]{:S(2)}, u32[]{:S(2)}) collective-permute-start(bf16[128,256]{1,0:T(8,128)(2,1)S(1)} %attend0.1), channel_id=1, source_target_pairs={{0,12},{4,8},{8,4},{12,0},{1,13},{5,9},{9,5},{13,1},{2,14},{6,10},... | collective-permute-start | bytes 196616 | tf_op jit(solution)/shard_map/ppermute | solution.py:277
  29.1 0.7 %attend1.1 = bf16[128,256]{1,0:T(8,128)(2,1)S(1)} custom-call(bf16[384,256]{1,0:T(8,128)(2,1)S(1)} %collective-permute-done.refs_0_, bf16[384,256]{1,0:T(8,128)(2,1)S(1)} %collective-permute-done.1.refs_1_, bf16[384,256]{1,0:T(8,128)(2,1)S(1)} %collective-permute-done.2.refs_2_, bf16[384,256]{1,0:T(8,128)(2,1)S(1)} %get-tuple-element.24.refs_3_, ...), custom_call_target="tpu_custom_call" | custom-call | flops 67108864 | tf_op jit(solution)/shard_map/attend1/pallas_call | solution.py:29
  29.7 1.1 %collective-permute-start.4 = (bf16[128,256]{1,0:T(8,128)(2,1)S(1)}, bf16[128,256]{1,0:T(8,128)(2,1)S(1)}, u32[]{:S(2)}, u32[]{:S(2)}) collective-permute-start(bf16[128,256]{1,0:T(8,128)(2,1)S(1)} %attend1.1), channel_id=1, source_target_pairs={{0,8},{4,12},{8,0},{12,4},{1,9},{5,13},{9,1},{13,5},{2,10},{6,14},... | collective-permute-start | bytes 196616 | tf_op jit(solution)/shard_map/ppermute | solution.py:277
  30.8 0.7 %attend2.1.refs_4_ = bf16[128,256]{1,0:T(8,128)(2,1)S(1)} custom-call(bf16[384,256]{1,0:T(8,128)(2,1)S(1)} %collective-permute-done.refs_0_, bf16[384,256]{1,0:T(8,128)(2,1)S(1)} %collective-permute-done.1.refs_1_, bf16[384,256]{1,0:T(8,128)(2,1)S(1)} %collective-permute-done.2.refs_2_, bf16[384,256]{1,0:T(8,128)(2,1)S(1)} %get-tuple-element.24.refs_3_, ...), custom_call_target="tpu_custom_call" | custom-call | flops 67108864 | tf_op jit(solution)/shard_map/attend2/pallas_call | solution.py:29
  31.5 1.0 %collective-permute-start.5 = (bf16[128,256]{1,0:T(8,128)(2,1)S(1)}, bf16[128,256]{1,0:T(8,128)(2,1)S(1)}, u32[]{:S(2)}, u32[]{:S(2)}) collective-permute-start(bf16[128,256]{1,0:T(8,128)(2,1)S(1)} %attend2.1.refs_4_), channel_id=1, source_target_pairs={{0,4},{4,0},{8,12},{12,8},{1,5},{5,1},{9,13},{13,9},{2,6},{6,2},{1... | collective-permute-start | bytes 196616 | tf_op jit(solution)/shard_map/ppermute | solution.py:277
  32.5 1.1 %partials.1 = (bf16[16,640]{1,0:T(8,128)(2,1)S(1)}, bf16[16,640]{1,0:T(8,128)(2,1)S(1)}, bf16[32,640]{1,0:T(8,128)(2,1)S(1)}) custom-call(bf16[128,512]{1,0:T(8,128)(2,1)S(1)} %get-tuple-element.26.ck, bf16[128,512]{1,0:T(8,128)(2,1)S(1)} %get-tuple-element.27.cv, bf16[48,512]{1,0:T(8,128)(2,1)S(1)} %get-tuple-element.28.refs_0_, ...), custom_call_target="tpu_custom_call" | custom-call | flops 3000000000 | tf_op jit(solution)/shard_map/partials/pallas_call | solution.py:29
  33.5 0.7 %attend3.1.refs_3_ = bf16[128,256]{1,0:T(8,128)(2,1)S(1)} custom-call(bf16[384,256]{1,0:T(8,128)(2,1)S(1)} %collective-permute-done.refs_0_, bf16[384,256]{1,0:T(8,128)(2,1)S(1)} %collective-permute-done.1.refs_1_, bf16[384,256]{1,0:T(8,128)(2,1)S(1)} %collective-permute-done.2.refs_2_, bf16[384,256]{1,0:T(8,128)(2,1)S(1)} %get-tuple-element.24.refs_3_, ...), custom_call_target="tpu_custom_call" | custom-call | flops 67108864 | tf_op jit(solution)/shard_map/attend3/pallas_call | solution.py:29
  34.2 1.7 %collective-permute-done.4.refs_1_ = bf16[128,256]{1,0:T(8,128)(2,1)S(1)} collective-permute-done((bf16[128,256]{1,0:T(8,128)(2,1)S(1)}, bf16[128,256]{1,0:T(8,128)(2,1)S(1)}, u32[]{:S(2)}, u32[]{:S(2)}) %collective-permute-start.4) | collective-permute-done | bytes 65568 | tf_op jit(solution)/shard_map/ppermute | solution.py:277
  36.6 1.8 %collective-permute-start.12 = (bf16[32,640]{1,0:T(8,128)(2,1)S(1)}, bf16[32,640]{1,0:T(8,128)(2,1)S(1)}, u32[]{:S(2)}, u32[]{:S(2)}) collective-permute-start(bf16[32,640]{1,0:T(8,128)(2,1)S(1)} %get-tuple-element.34), channel_id=1, source_target_pairs={{0,8},{4,12},{8,0},{12,4},{1,9},{5,13},{9,1},{13,5},{2,10},{6,14},... | collective-permute-start | bytes 122888 | tf_op jit(solution)/shard_map/ppermute | solution.py:298
  38.9 1.6 %collective-permute-start.11 = (bf16[128,1024]{1,0:T(8,128)(2,1)S(1)}, bf16[128,1024]{1,0:T(8,128)(2,1)S(1)}, u32[]{:S(2)}, u32[]{:S(2)}) collective-permute-start(bf16[128,1024]{1,0:T(8,128)(2,1)S(1)} %add_convert_fusion.1.refs_5_.refs_4_.refs_3_), channel_id=1, source_target_pairs={{0,2},{1,3},{2,0},{3,1},{4,6},{5,7},{6,4},{7,5},{8,10},{9,11},{10,... | collective-permute-start | bytes 786440 | tf_op jit(solution)/shard_map/ppermute | solution.py:293
  40.5 0.7 %project_near.1 = (bf16[128,1024]{1,0:T(8,128)(2,1)S(1)}, f32[128,1024]{1,0:T(8,128)S(1)}) custom-call(bf16[128,256]{1,0:T(8,128)(2,1)S(1)} %collective-permute-done.3.refs_0_, bf16[128,256]{1,0:T(8,128)(2,1)S(1)} %collective-permute-done.4.refs_1_, bf16[128,256]{1,0:T(8,128)(2,1)S(1)} %collective-permute-done.5.refs_2_, ...), custom_call_target="tpu_custom_call" | custom-call | flops 536870912 | tf_op jit(solution)/shard_map/project_near/pallas_call | solution.py:29
  41.3 1.0 %collective-permute-done.12.refs_2_ = bf16[32,640]{1,0:T(8,128)(2,1)S(1)} collective-permute-done((bf16[32,640]{1,0:T(8,128)(2,1)S(1)}, bf16[32,640]{1,0:T(8,128)(2,1)S(1)}, u32[]{:S(2)}, u32[]{:S(2)}) %collective-permute-start.12) | collective-permute-done | bytes 40992 | tf_op jit(solution)/shard_map/ppermute | solution.py:298
  43.0 1.3 %video_cross.1 = bf16[128,512]{1,0:T(8,128)(2,1)} custom-call(bf16[128,512]{1,0:T(8,128)(2,1)S(1)} %get-tuple-element.32.cq, bf16[48,512]{1,0:T(8,128)(2,1)S(1)} %get-tuple-element.28.refs_0_, bf16[48,512]{1,0:T(8,128)(2,1)S(1)} %collective-permute-done.6.refs_1_, bf16[48,512]{1,0:T(8,128)(2,1)S(1)} %collective-permute-done.7.refs_2_, ...), custom_call_target="tpu_custom_call" | custom-call | flops 16777216 | tf_op jit(solution)/shard_map/video_cross/pallas_call | solution.py:29
  44.3 2.3 %collective-permute-done.13.refs_1_ = bf16[16,640]{1,0:T(8,128)(2,1)S(1)} collective-permute-done((bf16[16,640]{1,0:T(8,128)(2,1)S(1)}, bf16[16,640]{1,0:T(8,128)(2,1)S(1)}, u32[]{:S(2)}, u32[]{:S(2)}) %collective-permute-start.13) | collective-permute-done | bytes 20512 | tf_op jit(solution)/shard_map/ppermute | solution.py:300
  46.5 0.8 %merge_last.1 = bf16[16,512]{1,0:T(8,128)(2,1)} custom-call(bf16[16,640]{1,0:T(8,128)(2,1)S(1)} %get-tuple-element.35.refs_0_, bf16[16,640]{1,0:T(8,128)(2,1)S(1)} %collective-permute-done.13.refs_1_), custom_call_target="tpu_custom_call" | custom-call | tf_op jit(solution)/shard_map/merge_last/pallas_call | solution.py:29
  47.4 0.8 %add_convert_fusion = bf16[128,1024]{1,0:T(8,128)(2,1)} fusion(bf16[128,1024]{1,0:T(8,128)(2,1)S(1)} %collective-permute-done.11, bf16[128,1024]{1,0:T(8,128)(2,1)S(1)} %collective-permute-done.10, f32[128,1024]{1,0:T(8,128)S(1)} %get-tuple-element.30, bf16[128,1024]{1,0:T(8,128)(2,1)S(1)} %get-tuple-element.20), kind=kLoop, calls=%fused_computation | loop fusion | flops 917504 | bytes 1572864 | tf_op jit(solution)/shard_map/convert_element_type | solution.py:294
  (19 shorter events, 2.0 us)
Async XLA Ops:
  1.9 23.9 %collective-permute-start = (bf16[384,256]{1,0:T(8,128)(2,1)S(1)}, bf16[384,256]{1,0:T(8,128)(2,1)S(1)}, u32[]{:S(2)}, u32[]{:S(2)}) collective-permute-start(bf16[384,256]{1,0:T(8,128)(2,1)S(1)} %get-tuple-element.21), channel_id=1, source_target_pairs={{0,12},{4,8},{8,4},{12,0},{1,13},{5,9},{9,5},{13,1},{2,14},{6,10},... | collective-permute-start | bytes 589832 | tf_op jit(solution)/shard_map/ppermute | solution.py:265
  7.0 18.8 %collective-permute-start.1 = (bf16[384,256]{1,0:T(8,128)(2,1)S(1)}, bf16[384,256]{1,0:T(8,128)(2,1)S(1)}, u32[]{:S(2)}, u32[]{:S(2)}) collective-permute-start(bf16[384,256]{1,0:T(8,128)(2,1)S(1)} %get-tuple-element.22), channel_id=1, source_target_pairs={{0,8},{4,12},{8,0},{12,4},{1,9},{5,13},{9,1},{13,5},{2,10},{6,14},... | collective-permute-start | bytes 589832 | tf_op jit(solution)/shard_map/ppermute | solution.py:265
  7.0 18.8 %collective-permute-start.2 = (bf16[384,256]{1,0:T(8,128)(2,1)S(1)}, bf16[384,256]{1,0:T(8,128)(2,1)S(1)}, u32[]{:S(2)}, u32[]{:S(2)}) collective-permute-start(bf16[384,256]{1,0:T(8,128)(2,1)S(1)} %get-tuple-element.23), channel_id=1, source_target_pairs={{0,4},{4,0},{8,12},{12,8},{1,5},{5,1},{9,13},{13,9},{2,6},{6,2},{1... | collective-permute-start | bytes 589832 | tf_op jit(solution)/shard_map/ppermute | solution.py:265
  11.2 14.6 %collective-permute-start.7 = (bf16[48,512]{1,0:T(8,128)(2,1)S(1)}, bf16[48,512]{1,0:T(8,128)(2,1)S(1)}, u32[]{:S(2)}, u32[]{:S(2)}) collective-permute-start(bf16[48,512]{1,0:T(8,128)(2,1)S(1)} %get-tuple-element.28.refs_0_), channel_id=1, source_target_pairs={{0,8},{4,12},{8,0},{12,4},{1,9},{5,13},{9,1},{13,5},{2,10},{6,14},... | collective-permute-start | bytes 147464 | tf_op jit(solution)/shard_map/ppermute | solution.py:271
  13.6 18.9 %collective-permute-start.6 = (bf16[48,512]{1,0:T(8,128)(2,1)S(1)}, bf16[48,512]{1,0:T(8,128)(2,1)S(1)}, u32[]{:S(2)}, u32[]{:S(2)}) collective-permute-start(bf16[48,512]{1,0:T(8,128)(2,1)S(1)} %get-tuple-element.28.refs_0_), channel_id=1, source_target_pairs={{0,4},{4,0},{8,12},{12,8},{1,5},{5,1},{9,13},{13,9},{2,6},{6,2},{1... | collective-permute-start | bytes 147464 | tf_op jit(solution)/shard_map/ppermute | solution.py:271
  25.8 6.6 %collective-permute-start.8 = (bf16[48,512]{1,0:T(8,128)(2,1)S(1)}, bf16[48,512]{1,0:T(8,128)(2,1)S(1)}, u32[]{:S(2)}, u32[]{:S(2)}) collective-permute-start(bf16[48,512]{1,0:T(8,128)(2,1)S(1)} %collective-permute-done.7.refs_2_), channel_id=1, source_target_pairs={{0,4},{4,0},{8,12},{12,8},{1,5},{5,1},{9,13},{13,9},{2,6},{6,2},{1... | collective-permute-start | bytes 147464 | tf_op jit(solution)/shard_map/ppermute | solution.py:269
  26.5 7.7 %collective-permute-start.3 = (bf16[128,256]{1,0:T(8,128)(2,1)S(1)}, bf16[128,256]{1,0:T(8,128)(2,1)S(1)}, u32[]{:S(2)}, u32[]{:S(2)}) collective-permute-start(bf16[128,256]{1,0:T(8,128)(2,1)S(1)} %attend0.1), channel_id=1, source_target_pairs={{0,12},{4,8},{8,4},{12,0},{1,13},{5,9},{9,5},{13,1},{2,14},{6,10},... | collective-permute-start | bytes 196616 | tf_op jit(solution)/shard_map/ppermute | solution.py:277
  29.7 6.2 %collective-permute-start.4 = (bf16[128,256]{1,0:T(8,128)(2,1)S(1)}, bf16[128,256]{1,0:T(8,128)(2,1)S(1)}, u32[]{:S(2)}, u32[]{:S(2)}) collective-permute-start(bf16[128,256]{1,0:T(8,128)(2,1)S(1)} %attend1.1), channel_id=1, source_target_pairs={{0,8},{4,12},{8,0},{12,4},{1,9},{5,13},{9,1},{13,5},{2,10},{6,14},... | collective-permute-start | bytes 196616 | tf_op jit(solution)/shard_map/ppermute | solution.py:277
  31.5 4.5 %collective-permute-start.5 = (bf16[128,256]{1,0:T(8,128)(2,1)S(1)}, bf16[128,256]{1,0:T(8,128)(2,1)S(1)}, u32[]{:S(2)}, u32[]{:S(2)}) collective-permute-start(bf16[128,256]{1,0:T(8,128)(2,1)S(1)} %attend2.1.refs_4_), channel_id=1, source_target_pairs={{0,4},{4,0},{8,12},{12,8},{1,5},{5,1},{9,13},{13,9},{2,6},{6,2},{1... | collective-permute-start | bytes 196616 | tf_op jit(solution)/shard_map/ppermute | solution.py:277
  36.5 2.4 %collective-permute-start.9 = (bf16[128,1024]{1,0:T(8,128)(2,1)S(1)}, bf16[128,1024]{1,0:T(8,128)(2,1)S(1)}, u32[]{:S(2)}, u32[]{:S(2)}) collective-permute-start(bf16[128,1024]{1,0:T(8,128)(2,1)S(1)} %project_far.1.refs_5_), channel_id=1, source_target_pairs={{0,1},{1,0},{2,3},{3,2},{4,5},{5,4},{6,7},{7,6},{8,9},{9,8},{10,11... | collective-permute-start | bytes 786440 | tf_op jit(solution)/shard_map/ppermute | solution.py:287
  36.6 5.8 %collective-permute-start.12 = (bf16[32,640]{1,0:T(8,128)(2,1)S(1)}, bf16[32,640]{1,0:T(8,128)(2,1)S(1)}, u32[]{:S(2)}, u32[]{:S(2)}) collective-permute-start(bf16[32,640]{1,0:T(8,128)(2,1)S(1)} %get-tuple-element.34), channel_id=1, source_target_pairs={{0,8},{4,12},{8,0},{12,4},{1,9},{5,13},{9,1},{13,5},{2,10},{6,14},... | collective-permute-start | bytes 122888 | tf_op jit(solution)/shard_map/ppermute | solution.py:298
  38.9 8.4 %collective-permute-start.11 = (bf16[128,1024]{1,0:T(8,128)(2,1)S(1)}, bf16[128,1024]{1,0:T(8,128)(2,1)S(1)}, u32[]{:S(2)}, u32[]{:S(2)}) collective-permute-start(bf16[128,1024]{1,0:T(8,128)(2,1)S(1)} %add_convert_fusion.1.refs_5_.refs_4_.refs_3_), channel_id=1, source_target_pairs={{0,2},{1,3},{2,0},{3,1},{4,6},{5,7},{6,4},{7,5},{8,10},{9,11},{10,... | collective-permute-start | bytes 786440 | tf_op jit(solution)/shard_map/ppermute | solution.py:293
  41.2 6.1 %collective-permute-start.10 = (bf16[128,1024]{1,0:T(8,128)(2,1)S(1)}, bf16[128,1024]{1,0:T(8,128)(2,1)S(1)}, u32[]{:S(2)}, u32[]{:S(2)}) collective-permute-start(bf16[128,1024]{1,0:T(8,128)(2,1)S(1)} %get-tuple-element.31), channel_id=1, source_target_pairs={{0,1},{1,0},{2,3},{3,2},{4,5},{5,4},{6,7},{7,6},{8,9},{9,8},{10,11... | collective-permute-start | bytes 786440 | tf_op jit(solution)/shard_map/ppermute | solution.py:291
  42.7 3.8 %collective-permute-start.13 = (bf16[16,640]{1,0:T(8,128)(2,1)S(1)}, bf16[16,640]{1,0:T(8,128)(2,1)S(1)}, u32[]{:S(2)}, u32[]{:S(2)}) collective-permute-start(bf16[16,640]{1,0:T(8,128)(2,1)S(1)} %get-tuple-element.36), channel_id=1, source_target_pairs={{0,4},{4,0},{8,12},{12,8},{1,5},{5,1},{9,13},{13,9},{2,6},{6,2},{1... | collective-permute-start | bytes 61448 | tf_op jit(solution)/shard_map/ppermute | solution.py:300

commit v4 on v3

--- a/solution.py
+++ b/solution.py
@@ -21,7 +21,7 @@
 WHOLE_VMEM = 62.75
 
 
-COSTS = {"merge": 10000000000, "partials": 3000000000}
+COSTS = {"merge": 10000000000, "partials": 3000000000, "project_kept": 10000000000}
 
 
 def call(kernel, name, shapes, ins, outs, operands, limit, scratch=(), flops=0):
@@ -122,7 +122,7 @@
     )
 
 
-def project_kernel(order, blocks, step, *refs):
+def project_kernel(order, blocks, part, step, *refs):
     count = len(order)
     heads, w, lhs = refs[:count], refs[count], refs[-1]
     outs = refs[-1 - len(blocks) : -1]
@@ -132,19 +132,20 @@
     for mask, one in zip(order, heads):
         owner = jnp.bitwise_xor(z, mask)
         lhs[:, pl.ds(pl.multiple_of(owner * width, width), width)] = one[...]
+    part, parts = part
     for out, mask in zip(outs, blocks):
         share = out.shape[1]
         owner = jnp.bitwise_xor(t, mask)
         for start in range(0, share, step):
-            columns = pl.ds(pl.multiple_of(owner * share + start, step), step)
+            columns = pl.ds(pl.multiple_of((owner * parts + part) * share + start, step), step)
             product = jnp.dot(lhs[...], w[:, columns], preferred_element_type=F32)
             out[:, start : start + step] = product.astype(out.dtype)
 
 
-def project(order, heads, w, share, blocks, name, after=()):
+def project(order, heads, w, share, blocks, name, after=(), part=(0, 1)):
     count, rows = len(heads), heads[0].shape[0]
     return call(
-        functools.partial(project_kernel, order, list(blocks), math.gcd(512, share)), name,
+        functools.partial(project_kernel, order, list(blocks), part, math.gcd(512, share)), name,
         [jax.ShapeDtypeStruct((rows, share), dtype) for dtype in blocks.values()],
         [VM] * (count + 1) + [ANY] * len(after), [VM] * len(blocks), (*(heads[mask] for mask in order), w, *after), 8,
         [pltpu.VMEM((rows, w.shape[0]), BF16)],
@@ -270,8 +271,11 @@
         else:
             audios.append(seq[mask](own_audio))
     heads = [None] * count
+    done = [weight]
     for index, mask in enumerate(order + [0]):
-        (heads[mask],) = attend([mask], order + [0], rows, packs, [weight], f"attend{index}")
+        (heads[mask],) = attend([mask], order + [0], rows, packs, done, f"attend{index}")
+        if mask:
+            done = [heads[mask]]
     own_heads = list(heads)
     for mask in order:
         heads[mask] = seq[mask](heads[mask])
@@ -282,21 +286,39 @@
     )
     others = list(range(2, tensor, 2))
     core = partner("tensor", tensor, 1)
+    def halve(pieces, after):
+        while len(pieces) > 2:
+            mask = groups[len(pieces) - 1][0]
+            other = seq[mask](pieces.pop())
+            pieces = list(merge(pieces, other, False, after))
+        return pieces
+
     pieces = list(pieces)
-    sent = project(order + [0], heads, weight, share, {mask + 1: BF16 for mask in others}, "project_far", pieces[:1])
-    got = [core(x) for x in sent]
-    kept = project(order + [0], heads, weight, share, {mask: F32 for mask in others}, "project_kept", sent[:1])
-    summed = [(mine + theirs.astype(F32)).astype(BF16) for mine, theirs in zip(kept, got)]
+    chunks = 2 if share % 256 == 0 else 1
+    got, after = [], pieces[:1]
+    for part in range(chunks):
+        sent = project(
+            order + [0], heads, weight, share // chunks, {mask + 1: BF16 for mask in others}, "project_far", after,
+            (part, chunks),
+        )
+        after = sent[:1]
+        got.append([core(x) for x in sent])
+    came = []
+    for part in range(chunks):
+        kept = project(
+            order + [0], heads, weight, share // chunks, {mask: F32 for mask in others}, "project_kept", after,
+            (part, chunks),
+        )
+        summed = [(mine + theirs.astype(F32)).astype(BF16) for mine, theirs in zip(kept, got[part])]
+        came.append([partner("tensor", tensor, mask)(piece).astype(F32) for mask, piece in zip(others, summed)])
+        after = summed[:1]
     own, near = project(order + [0], heads, weight, share, {1: BF16, 0: F32}, "project_near", summed)
     total = video_stream.astype(F32) + near + core(own).astype(F32)
-    for mask, piece in zip(others, summed):
-        total = total + partner("tensor", tensor, mask)(piece).astype(F32)
+    for index in range(len(others)):
+        total = total + jnp.concatenate([one[index] for one in came], axis=1)
     video_next = total.astype(BF16)
     video_cross = crossed(cross_query, audios, summed)
-    while len(pieces) > 2:
-        mask = groups[len(pieces) - 1][0]
-        other = seq[mask](pieces.pop())
-        pieces = list(merge(pieces, other, False, summed))
+    pieces = halve(pieces, summed)
     (audio_cross,) = merge(pieces[:1], seq[1](pieces[1]), True)
     return video_next, video_cross, audio_cross
 

time: 48.4 us -> 47.7 us (0.986)
  waiting for transfers between devices: 15.4 us -> 12.1 us
  starting transfers between devices: 18.5 us -> 20.7 us
    ppermute x3, waiting for transfers between devices: 1.8 us -> 0.04 us  [exchanged(): heads[mask] = seq[mask](heads[mask])]
    ppermute x3 -> x5, starting transfers between devices: 3.42 us -> 4.97 us  [the longest x1 2.19 us: halve(): other = seq[mask](pieces.pop())]
    ppermute x3 -> x5, waiting for transfers between devices: 1.05 us -> 0.15 us  [the longest x2 0.11 us: exchanged(): got.append([core(x) for x in sent])]
    ppermute x1, starting transfers between devices: 0.32 us -> 0.96 us  [exchanged(): audio_cross, = merge(pieces[:1], seq[1](pieces[1]), True)]
    ppermute x1, waiting for transfers between devices: 2.26 us -> 1.62 us  [exchanged(): audio_cross, = merge(pieces[:1], seq[1](pieces[1]), True)]
    pallas_call x13 -> x15, Pallas kernels: 12.7 us -> 13 us  [call(): pl.pallas_call(kernel, out_shape=shapes, in_specs=ins, out_specs=outs, sc...]
  transfers between devices with their start and end apart: 14 -> 16, of which waited for: 5 -> 3; matrix products, arithmetic and copies ran while one was open for 0% -> 0% of each run, Pallas kernels for 23% -> 25%
where the time goes in v4:
time: 47.7 us; the launch traced here: 47.5 us
  starting transfers between devices  20.7 us (43%)
  Pallas kernels  13 us (27%)
  waiting for transfers between devices  12.1 us (25%)
  other arithmetic  0.9 us (2%)
  between operations  0.78 us (2%)
    pallas_call x15, Pallas kernels, call(): pl.pallas_call(kernel, out_shape=shapes, in_specs=ins, out_specs=outs, sc...  13 us
    ppermute x2, waiting for transfers between devices, exchanged(): audios.append(seq[mask](own_audio))  10.3 us
    ppermute x3, starting transfers between devices, exchanged(): packs[mask] = seq[mask](packs[mask])  5.76 us
    ppermute x3, starting transfers between devices, exchanged(): heads[mask] = seq[mask](heads[mask])  4.58 us
    ppermute x2, starting transfers between devices, exchanged(): audios.append(seq[mask](own_audio))  4.37 us
    ppermute x1, starting transfers between devices, halve(): other = seq[mask](pieces.pop())  2.19 us
    ppermute x2, starting transfers between devices, exchanged(): partner('tensor', tensor, mask)(piece).astype(F32)  2.16 us
    ppermute x1, waiting for transfers between devices, exchanged(): audio_cross, = merge(pieces[:1], seq[1](pieces[1]), True)  1.62 us
  transfers between devices with their start and end apart: 16, of which 3 were waited for; matrix products, arithmetic and copies ran while one was open for 0% of the time, Pallas kernels for 25%

profile of v4, /device:TPU:0, one launch (start us, length us, event | category | flops | bytes accessed | tf_op | source)
XLA Modules:
  0.0 47.5 jit_solution(14947529110082220052)
XLA Ops:
  0.6 1.3 %pack.1 = (bf16[384,256]{1,0:T(8,128)(2,1)S(1)}, bf16[384,256]{1,0:T(8,128)(2,1)S(1)}, bf16[384,256]{1,0:T(8,128)(2,1)S(1)}, bf16[384,256]{1,0:T(8,128)(2,1)S(1)}) custom-call(bf16[128,1024]{1,0:T(8,128)(2,1)} %q.1, bf16[128,1024]{1,0:T(8,128)(2,1)} %k.1, bf16[128,1024]{1,0:T(8,128)(2,1)} %v.1), custom_call_target="tpu_custom_call" | custom-call | tf_op jit(solution)/shard_map/pack/pallas_call | solution.py:29
  1.9 5.1 %collective-permute-start = (bf16[384,256]{1,0:T(8,128)(2,1)S(1)}, bf16[384,256]{1,0:T(8,128)(2,1)S(1)}, u32[]{:S(2)}, u32[]{:S(2)}) collective-permute-start(bf16[384,256]{1,0:T(8,128)(2,1)S(1)} %get-tuple-element.21), channel_id=1, source_target_pairs={{0,12},{4,8},{8,4},{12,0},{1,13},{5,9},{9,5},{13,1},{2,14},{6,10},... | collective-permute-start | bytes 589832 | tf_op jit(solution)/shard_map/ppermute | solution.py:266
  7.0 0.6 %collective-permute-start.2 = (bf16[384,256]{1,0:T(8,128)(2,1)S(1)}, bf16[384,256]{1,0:T(8,128)(2,1)S(1)}, u32[]{:S(2)}, u32[]{:S(2)}) collective-permute-start(bf16[384,256]{1,0:T(8,128)(2,1)S(1)} %get-tuple-element.23), channel_id=1, source_target_pairs={{0,4},{4,0},{8,12},{12,8},{1,5},{5,1},{9,13},{13,9},{2,6},{6,2},{1... | collective-permute-start | bytes 589832 | tf_op jit(solution)/shard_map/ppermute | solution.py:266
  7.7 3.5 %fetch.1 = (bf16[1024,4096]{1,0:T(8,128)(2,1)S(1)}, bf16[128,512]{1,0:T(8,128)(2,1)S(1)}, bf16[128,512]{1,0:T(8,128)(2,1)S(1)}, bf16[128,512]{1,0:T(8,128)(2,1)S...) custom-call(bf16[1024,4096]{1,0:T(8,128)(2,1)} %refs_0_.1, bf16[128,512]{1,0:T(8,128)(2,1)} %refs_1_.1, ...), custom_call_target="tpu_custom_call" | custom-call | tf_op jit(solution)/shard_map/fetch/pallas_call | solution.py:29
  11.2 2.4 %collective-permute-start.7 = (bf16[48,512]{1,0:T(8,128)(2,1)S(1)}, bf16[48,512]{1,0:T(8,128)(2,1)S(1)}, u32[]{:S(2)}, u32[]{:S(2)}) collective-permute-start(bf16[48,512]{1,0:T(8,128)(2,1)S(1)} %get-tuple-element.28.refs_0_), channel_id=1, source_target_pairs={{0,8},{4,12},{8,0},{12,4},{1,9},{5,13},{9,1},{13,5},{2,10},{6,14},... | collective-permute-start | bytes 147464 | tf_op jit(solution)/shard_map/ppermute | solution.py:272
  13.6 2.0 %collective-permute-start.6 = (bf16[48,512]{1,0:T(8,128)(2,1)S(1)}, bf16[48,512]{1,0:T(8,128)(2,1)S(1)}, u32[]{:S(2)}, u32[]{:S(2)}) collective-permute-start(bf16[48,512]{1,0:T(8,128)(2,1)S(1)} %get-tuple-element.28.refs_0_), channel_id=1, source_target_pairs={{0,4},{4,0},{8,12},{12,8},{1,5},{5,1},{9,13},{13,9},{2,6},{6,2},{1... | collective-permute-start | bytes 147464 | tf_op jit(solution)/shard_map/ppermute | solution.py:272
  15.6 10.3 %collective-permute-done.7.refs_2_ = bf16[48,512]{1,0:T(8,128)(2,1)S(1)} collective-permute-done((bf16[48,512]{1,0:T(8,128)(2,1)S(1)}, bf16[48,512]{1,0:T(8,128)(2,1)S(1)}, u32[]{:S(2)}, u32[]{:S(2)}) %collective-permute-start.7) | collective-permute-done | bytes 49184 | tf_op jit(solution)/shard_map/ppermute | solution.py:272
  25.9 0.7 %attend0.1.refs_4_ = bf16[128,256]{1,0:T(8,128)(2,1)S(1)} custom-call(bf16[384,256]{1,0:T(8,128)(2,1)S(1)} %collective-permute-done.refs_0_, bf16[384,256]{1,0:T(8,128)(2,1)S(1)} %collective-permute-done.1.refs_1_, bf16[384,256]{1,0:T(8,128)(2,1)S(1)} %collective-permute-done.2.refs_2_, bf16[384,256]{1,0:T(8,128)(2,1)S(1)} %get-tuple-element.24.refs_3_, ...), custom_call_target="tpu_custom_call" | custom-call | flops 67108864 | tf_op jit(solution)/shard_map/attend0/pallas_call | solution.py:29
  26.5 2.5 %collective-permute-start.3 = (bf16[128,256]{1,0:T(8,128)(2,1)S(1)}, bf16[128,256]{1,0:T(8,128)(2,1)S(1)}, u32[]{:S(2)}, u32[]{:S(2)}) collective-permute-start(bf16[128,256]{1,0:T(8,128)(2,1)S(1)} %attend0.1.refs_4_), channel_id=1, source_target_pairs={{0,12},{4,8},{8,4},{12,0},{1,13},{5,9},{9,5},{13,1},{2,14},{6,10},... | collective-permute-start | bytes 196616 | tf_op jit(solution)/shard_map/ppermute | solution.py:281
  29.1 0.7 %attend1.1.refs_4_ = bf16[128,256]{1,0:T(8,128)(2,1)S(1)} custom-call(bf16[384,256]{1,0:T(8,128)(2,1)S(1)} %collective-permute-done.refs_0_, bf16[384,256]{1,0:T(8,128)(2,1)S(1)} %collective-permute-done.1.refs_1_, bf16[384,256]{1,0:T(8,128)(2,1)S(1)} %collective-permute-done.2.refs_2_, bf16[384,256]{1,0:T(8,128)(2,1)S(1)} %get-tuple-element.24.refs_3_, ...), custom_call_target="tpu_custom_call" | custom-call | flops 67108864 | tf_op jit(solution)/shard_map/attend1/pallas_call | solution.py:29
  29.7 1.1 %collective-permute-start.4 = (bf16[128,256]{1,0:T(8,128)(2,1)S(1)}, bf16[128,256]{1,0:T(8,128)(2,1)S(1)}, u32[]{:S(2)}, u32[]{:S(2)}) collective-permute-start(bf16[128,256]{1,0:T(8,128)(2,1)S(1)} %attend1.1.refs_4_), channel_id=1, source_target_pairs={{0,8},{4,12},{8,0},{12,4},{1,9},{5,13},{9,1},{13,5},{2,10},{6,14},... | collective-permute-start | bytes 196616 | tf_op jit(solution)/shard_map/ppermute | solution.py:281
  30.8 0.7 %attend2.1.refs_4_ = bf16[128,256]{1,0:T(8,128)(2,1)S(1)} custom-call(bf16[384,256]{1,0:T(8,128)(2,1)S(1)} %collective-permute-done.refs_0_, bf16[384,256]{1,0:T(8,128)(2,1)S(1)} %collective-permute-done.1.refs_1_, bf16[384,256]{1,0:T(8,128)(2,1)S(1)} %collective-permute-done.2.refs_2_, bf16[384,256]{1,0:T(8,128)(2,1)S(1)} %get-tuple-element.24.refs_3_, ...), custom_call_target="tpu_custom_call" | custom-call | flops 67108864 | tf_op jit(solution)/shard_map/attend2/pallas_call | solution.py:29
  31.5 1.0 %collective-permute-start.5 = (bf16[128,256]{1,0:T(8,128)(2,1)S(1)}, bf16[128,256]{1,0:T(8,128)(2,1)S(1)}, u32[]{:S(2)}, u32[]{:S(2)}) collective-permute-start(bf16[128,256]{1,0:T(8,128)(2,1)S(1)} %attend2.1.refs_4_), channel_id=1, source_target_pairs={{0,4},{4,0},{8,12},{12,8},{1,5},{5,1},{9,13},{13,9},{2,6},{6,2},{1... | collective-permute-start | bytes 196616 | tf_op jit(solution)/shard_map/ppermute | solution.py:281
  32.5 1.1 %partials.1 = (bf16[16,640]{1,0:T(8,128)(2,1)S(1)}, bf16[16,640]{1,0:T(8,128)(2,1)S(1)}, bf16[32,640]{1,0:T(8,128)(2,1)S(1)}) custom-call(bf16[128,512]{1,0:T(8,128)(2,1)S(1)} %get-tuple-element.26.ck, bf16[128,512]{1,0:T(8,128)(2,1)S(1)} %get-tuple-element.27.cv, bf16[48,512]{1,0:T(8,128)(2,1)S(1)} %get-tuple-element.28.refs_0_, ...), custom_call_target="tpu_custom_call" | custom-call | flops 3000000000 | tf_op jit(solution)/shard_map/partials/pallas_call | solution.py:29
  33.5 2.2 %collective-permute-start.14 = (bf16[32,640]{1,0:T(8,128)(2,1)S(1)}, bf16[32,640]{1,0:T(8,128)(2,1)S(1)}, u32[]{:S(2)}, u32[]{:S(2)}) collective-permute-start(bf16[32,640]{1,0:T(8,128)(2,1)S(1)} %get-tuple-element.34), channel_id=1, source_target_pairs={{0,8},{4,12},{8,0},{12,4},{1,9},{5,13},{9,1},{13,5},{2,10},{6,14},... | collective-permute-start | bytes 122888 | tf_op jit(solution)/shard_map/ppermute | solution.py:292
  35.7 0.7 %attend3.1.refs_3_ = bf16[128,256]{1,0:T(8,128)(2,1)S(1)} custom-call(bf16[384,256]{1,0:T(8,128)(2,1)S(1)} %collective-permute-done.refs_0_, bf16[384,256]{1,0:T(8,128)(2,1)S(1)} %collective-permute-done.1.refs_1_, bf16[384,256]{1,0:T(8,128)(2,1)S(1)} %collective-permute-done.2.refs_2_, bf16[384,256]{1,0:T(8,128)(2,1)S(1)} %get-tuple-element.24.refs_3_, ...), custom_call_target="tpu_custom_call" | custom-call | flops 67108864 | tf_op jit(solution)/shard_map/attend3/pallas_call | solution.py:29
  38.2 1.6 %collective-permute-start.12 = (bf16[128,512]{1,0:T(8,128)(2,1)S(1)}, bf16[128,512]{1,0:T(8,128)(2,1)S(1)}, u32[]{:S(2)}, u32[]{:S(2)}) collective-permute-start(bf16[128,512]{1,0:T(8,128)(2,1)S(1)} %add_convert_fusion.2.refs_5_), channel_id=1, source_target_pairs={{0,2},{1,3},{2,0},{3,1},{4,6},{5,7},{6,4},{7,5},{8,10},{9,11},{10,... | collective-permute-start | bytes 393224 | tf_op jit(solution)/shard_map/ppermute | solution.py:313
  40.2 0.6 %collective-permute-start.13 = (bf16[128,512]{1,0:T(8,128)(2,1)S(1)}, bf16[128,512]{1,0:T(8,128)(2,1)S(1)}, u32[]{:S(2)}, u32[]{:S(2)}) collective-permute-start(bf16[128,512]{1,0:T(8,128)(2,1)S(1)} %add_convert_fusion.1.refs_5_.refs_4_.refs_3_), channel_id=1, source_target_pairs={{0,2},{1,3},{2,0},{3,1},{4,6},{5,7},{6,4},{7,5},{8,10},{9,11},{10,... | collective-permute-start | bytes 393224 | tf_op jit(solution)/shard_map/ppermute | solution.py:313
  40.8 0.7 %project_near.1 = (bf16[128,1024]{1,0:T(8,128)(2,1)S(1)}, f32[128,1024]{1,0:T(8,128)S(1)}) custom-call(bf16[128,256]{1,0:T(8,128)(2,1)S(1)} %collective-permute-done.3.refs_0_, bf16[128,256]{1,0:T(8,128)(2,1)S(1)} %collective-permute-done.4.refs_1_, bf16[128,256]{1,0:T(8,128)(2,1)S(1)} %collective-permute-done.5.refs_2_, ...), custom_call_target="tpu_custom_call" | custom-call | flops 536870912 | tf_op jit(solution)/shard_map/project_near/pallas_call | solution.py:29
  42.0 1.0 %collective-permute-start.15 = (bf16[16,640]{1,0:T(8,128)(2,1)S(1)}, bf16[16,640]{1,0:T(8,128)(2,1)S(1)}, u32[]{:S(2)}, u32[]{:S(2)}) collective-permute-start(bf16[16,640]{1,0:T(8,128)(2,1)S(1)} %get-tuple-element.36), channel_id=1, source_target_pairs={{0,4},{4,0},{8,12},{12,8},{1,5},{5,1},{9,13},{13,9},{2,6},{6,2},{1... | collective-permute-start | bytes 61448 | tf_op jit(solution)/shard_map/ppermute | solution.py:322
  42.9 1.3 %video_cross.1 = bf16[128,512]{1,0:T(8,128)(2,1)} custom-call(bf16[128,512]{1,0:T(8,128)(2,1)S(1)} %get-tuple-element.32.cq, bf16[48,512]{1,0:T(8,128)(2,1)S(1)} %get-tuple-element.28.refs_0_, bf16[48,512]{1,0:T(8,128)(2,1)S(1)} %collective-permute-done.6.refs_1_, bf16[48,512]{1,0:T(8,128)(2,1)S(1)} %collective-permute-done.7.refs_2_, ...), custom_call_target="tpu_custom_call" | custom-call | flops 16777216 | tf_op jit(solution)/shard_map/video_cross/pallas_call | solution.py:29
  44.2 1.6 %collective-permute-done.15.refs_1_ = bf16[16,640]{1,0:T(8,128)(2,1)S(1)} collective-permute-done((bf16[16,640]{1,0:T(8,128)(2,1)S(1)}, bf16[16,640]{1,0:T(8,128)(2,1)S(1)}, u32[]{:S(2)}, u32[]{:S(2)}) %collective-permute-start.15) | collective-permute-done | bytes 20512 | tf_op jit(solution)/shard_map/ppermute | solution.py:322
  45.8 0.8 %merge_last.1 = bf16[16,512]{1,0:T(8,128)(2,1)} custom-call(bf16[16,640]{1,0:T(8,128)(2,1)S(1)} %get-tuple-element.35.refs_0_, bf16[16,640]{1,0:T(8,128)(2,1)S(1)} %collective-permute-done.15.refs_1_), custom_call_target="tpu_custom_call" | custom-call | tf_op jit(solution)/shard_map/merge_last/pallas_call | solution.py:29
  46.7 0.8 %add_convert_fusion = bf16[128,1024]{1,0:T(8,128)(2,1)} fusion(bf16[128,1024]{1,0:T(8,128)(2,1)S(1)} %collective-permute-done.11, f32[128,1024]{1,0:T(8,128)S(1)} %get-tuple-element.30, bf16[128,1024]{1,0:T(8,128)(2,1)S(1)} %get-tuple-element.20, bf16[128,512]{1,0:T(8,128)(2,1)S(1)} %collective-permute-done.13, bf16[128,512]{1,0:T(8,128)(2,1)S(1)} %collective-permute-done.12), kind=kLoop, calls=%fused_computation | loop fusion | flops 1310720 | bytes 1572864 | tf_op jit(solution)/shard_map/convert_element_type | solution.py:319
  (26 shorter events, 2.6 us)
Async XLA Ops:
  1.9 23.9 %collective-permute-start = (bf16[384,256]{1,0:T(8,128)(2,1)S(1)}, bf16[384,256]{1,0:T(8,128)(2,1)S(1)}, u32[]{:S(2)}, u32[]{:S(2)}) collective-permute-start(bf16[384,256]{1,0:T(8,128)(2,1)S(1)} %get-tuple-element.21), channel_id=1, source_target_pairs={{0,12},{4,8},{8,4},{12,0},{1,13},{5,9},{9,5},{13,1},{2,14},{6,10},... | collective-permute-start | bytes 589832 | tf_op jit(solution)/shard_map/ppermute | solution.py:266
  7.0 18.8 %collective-permute-start.1 = (bf16[384,256]{1,0:T(8,128)(2,1)S(1)}, bf16[384,256]{1,0:T(8,128)(2,1)S(1)}, u32[]{:S(2)}, u32[]{:S(2)}) collective-permute-start(bf16[384,256]{1,0:T(8,128)(2,1)S(1)} %get-tuple-element.22), channel_id=1, source_target_pairs={{0,8},{4,12},{8,0},{12,4},{1,9},{5,13},{9,1},{13,5},{2,10},{6,14},... | collective-permute-start | bytes 589832 | tf_op jit(solution)/shard_map/ppermute | solution.py:266
  7.0 18.8 %collective-permute-start.2 = (bf16[384,256]{1,0:T(8,128)(2,1)S(1)}, bf16[384,256]{1,0:T(8,128)(2,1)S(1)}, u32[]{:S(2)}, u32[]{:S(2)}) collective-permute-start(bf16[384,256]{1,0:T(8,128)(2,1)S(1)} %get-tuple-element.23), channel_id=1, source_target_pairs={{0,4},{4,0},{8,12},{12,8},{1,5},{5,1},{9,13},{13,9},{2,6},{6,2},{1... | collective-permute-start | bytes 589832 | tf_op jit(solution)/shard_map/ppermute | solution.py:266
  11.2 14.6 %collective-permute-start.7 = (bf16[48,512]{1,0:T(8,128)(2,1)S(1)}, bf16[48,512]{1,0:T(8,128)(2,1)S(1)}, u32[]{:S(2)}, u32[]{:S(2)}) collective-permute-start(bf16[48,512]{1,0:T(8,128)(2,1)S(1)} %get-tuple-element.28.refs_0_), channel_id=1, source_target_pairs={{0,8},{4,12},{8,0},{12,4},{1,9},{5,13},{9,1},{13,5},{2,10},{6,14},... | collective-permute-start | bytes 147464 | tf_op jit(solution)/shard_map/ppermute | solution.py:272
  13.6 18.9 %collective-permute-start.6 = (bf16[48,512]{1,0:T(8,128)(2,1)S(1)}, bf16[48,512]{1,0:T(8,128)(2,1)S(1)}, u32[]{:S(2)}, u32[]{:S(2)}) collective-permute-start(bf16[48,512]{1,0:T(8,128)(2,1)S(1)} %get-tuple-element.28.refs_0_), channel_id=1, source_target_pairs={{0,4},{4,0},{8,12},{12,8},{1,5},{5,1},{9,13},{13,9},{2,6},{6,2},{1... | collective-permute-start | bytes 147464 | tf_op jit(solution)/shard_map/ppermute | solution.py:272
  25.8 6.6 %collective-permute-start.8 = (bf16[48,512]{1,0:T(8,128)(2,1)S(1)}, bf16[48,512]{1,0:T(8,128)(2,1)S(1)}, u32[]{:S(2)}, u32[]{:S(2)}) collective-permute-start(bf16[48,512]{1,0:T(8,128)(2,1)S(1)} %collective-permute-done.7.refs_2_), channel_id=1, source_target_pairs={{0,4},{4,0},{8,12},{12,8},{1,5},{5,1},{9,13},{13,9},{2,6},{6,2},{1... | collective-permute-start | bytes 147464 | tf_op jit(solution)/shard_map/ppermute | solution.py:270
  26.5 9.9 %collective-permute-start.3 = (bf16[128,256]{1,0:T(8,128)(2,1)S(1)}, bf16[128,256]{1,0:T(8,128)(2,1)S(1)}, u32[]{:S(2)}, u32[]{:S(2)}) collective-permute-start(bf16[128,256]{1,0:T(8,128)(2,1)S(1)} %attend0.1.refs_4_), channel_id=1, source_target_pairs={{0,12},{4,8},{8,4},{12,0},{1,13},{5,9},{9,5},{13,1},{2,14},{6,10},... | collective-permute-start | bytes 196616 | tf_op jit(solution)/shard_map/ppermute | solution.py:281
  29.7 6.7 %collective-permute-start.4 = (bf16[128,256]{1,0:T(8,128)(2,1)S(1)}, bf16[128,256]{1,0:T(8,128)(2,1)S(1)}, u32[]{:S(2)}, u32[]{:S(2)}) collective-permute-start(bf16[128,256]{1,0:T(8,128)(2,1)S(1)} %attend1.1.refs_4_), channel_id=1, source_target_pairs={{0,8},{4,12},{8,0},{12,4},{1,9},{5,13},{9,1},{13,5},{2,10},{6,14},... | collective-permute-start | bytes 196616 | tf_op jit(solution)/shard_map/ppermute | solution.py:281
  31.5 4.9 %collective-permute-start.5 = (bf16[128,256]{1,0:T(8,128)(2,1)S(1)}, bf16[128,256]{1,0:T(8,128)(2,1)S(1)}, u32[]{:S(2)}, u32[]{:S(2)}) collective-permute-start(bf16[128,256]{1,0:T(8,128)(2,1)S(1)} %attend2.1.refs_4_), channel_id=1, source_target_pairs={{0,4},{4,0},{8,12},{12,8},{1,5},{5,1},{9,13},{13,9},{2,6},{6,2},{1... | collective-permute-start | bytes 196616 | tf_op jit(solution)/shard_map/ppermute | solution.py:281
  33.5 8.1 %collective-permute-start.14 = (bf16[32,640]{1,0:T(8,128)(2,1)S(1)}, bf16[32,640]{1,0:T(8,128)(2,1)S(1)}, u32[]{:S(2)}, u32[]{:S(2)}) collective-permute-start(bf16[32,640]{1,0:T(8,128)(2,1)S(1)} %get-tuple-element.34), channel_id=1, source_target_pairs={{0,8},{4,12},{8,0},{12,4},{1,9},{5,13},{9,1},{13,5},{2,10},{6,14},... | collective-permute-start | bytes 122888 | tf_op jit(solution)/shard_map/ppermute | solution.py:292
  36.8 1.4 %collective-permute-start.9 = (bf16[128,512]{1,0:T(8,128)(2,1)S(1)}, bf16[128,512]{1,0:T(8,128)(2,1)S(1)}, u32[]{:S(2)}, u32[]{:S(2)}) collective-permute-start(bf16[128,512]{1,0:T(8,128)(2,1)S(1)} %project_far.2.refs_5_), channel_id=1, source_target_pairs={{0,1},{1,0},{2,3},{3,2},{4,5},{5,4},{6,7},{7,6},{8,9},{9,8},{10,11... | collective-permute-start | bytes 393224 | tf_op jit(solution)/shard_map/ppermute | solution.py:305
  37.2 2.9 %collective-permute-start.10 = (bf16[128,512]{1,0:T(8,128)(2,1)S(1)}, bf16[128,512]{1,0:T(8,128)(2,1)S(1)}, u32[]{:S(2)}, u32[]{:S(2)}) collective-permute-start(bf16[128,512]{1,0:T(8,128)(2,1)S(1)} %project_far.3.refs_5_), channel_id=1, source_target_pairs={{0,1},{1,0},{2,3},{3,2},{4,5},{5,4},{6,7},{7,6},{8,9},{9,8},{10,11... | collective-permute-start | bytes 393224 | tf_op jit(solution)/shard_map/ppermute | solution.py:305
  38.2 8.4 %collective-permute-start.12 = (bf16[128,512]{1,0:T(8,128)(2,1)S(1)}, bf16[128,512]{1,0:T(8,128)(2,1)S(1)}, u32[]{:S(2)}, u32[]{:S(2)}) collective-permute-start(bf16[128,512]{1,0:T(8,128)(2,1)S(1)} %add_convert_fusion.2.refs_5_), channel_id=1, source_target_pairs={{0,2},{1,3},{2,0},{3,1},{4,6},{5,7},{6,4},{7,5},{8,10},{9,11},{10,... | collective-permute-start | bytes 393224 | tf_op jit(solution)/shard_map/ppermute | solution.py:313
  40.2 6.5 %collective-permute-start.13 = (bf16[128,512]{1,0:T(8,128)(2,1)S(1)}, bf16[128,512]{1,0:T(8,128)(2,1)S(1)}, u32[]{:S(2)}, u32[]{:S(2)}) collective-permute-start(bf16[128,512]{1,0:T(8,128)(2,1)S(1)} %add_convert_fusion.1.refs_5_.refs_4_.refs_3_), channel_id=1, source_target_pairs={{0,2},{1,3},{2,0},{3,1},{4,6},{5,7},{6,4},{7,5},{8,10},{9,11},{10,... | collective-permute-start | bytes 393224 | tf_op jit(solution)/shard_map/ppermute | solution.py:313
  41.5 5.1 %collective-permute-start.11 = (bf16[128,1024]{1,0:T(8,128)(2,1)S(1)}, bf16[128,1024]{1,0:T(8,128)(2,1)S(1)}, u32[]{:S(2)}, u32[]{:S(2)}) collective-permute-start(bf16[128,1024]{1,0:T(8,128)(2,1)S(1)} %get-tuple-element.31), channel_id=1, source_target_pairs={{0,1},{1,0},{2,3},{3,2},{4,5},{5,4},{6,7},{7,6},{8,9},{9,8},{10,11... | collective-permute-start | bytes 786440 | tf_op jit(solution)/shard_map/ppermute | solution.py:316
  42.0 3.8 %collective-permute-start.15 = (bf16[16,640]{1,0:T(8,128)(2,1)S(1)}, bf16[16,640]{1,0:T(8,128)(2,1)S(1)}, u32[]{:S(2)}, u32[]{:S(2)}) collective-permute-start(bf16[16,640]{1,0:T(8,128)(2,1)S(1)} %get-tuple-element.36), channel_id=1, source_target_pairs={{0,4},{4,0},{8,12},{12,8},{1,5},{5,1},{9,13},{13,9},{2,6},{6,2},{1... | collective-permute-start | bytes 61448 | tf_op jit(solution)/shard_map/ppermute | solution.py:322

commit v5 on v4

--- a/solution.py
+++ b/solution.py
@@ -79,9 +79,11 @@
     )
 
 
-def attend_kernel(wanted, order, rows, *refs):
+def attend_kernel(wanted, order, rows, carried, *refs):
     count = len(order)
-    packs, outs = dict(zip(order, refs)), refs[-len(wanted) :]
+    packs, outs = dict(zip(order, refs)), refs[-len(wanted) - carried :]
+    for index in range(carried):
+        refs[index - carried][...] = refs[count + index][...]
     for columns in range(0, packs[0].shape[1], HD):
         columns = slice(columns, columns + HD)
         key = jnp.concatenate([p[rows : 2 * rows, columns] for p in packs.values()], axis=0)
@@ -91,12 +93,13 @@
             out[:, columns] = (numerator / total).astype(BF16)
 
 
-def attend(wanted, order, rows, packs, after, name):
+def attend(wanted, order, rows, packs, after, name, carry=()):
     count, width = len(packs), packs[0].shape[1]
     return call(
-        functools.partial(attend_kernel, wanted, order, rows), name,
-        [jax.ShapeDtypeStruct((rows, width), BF16)] * len(wanted),
-        [VM] * count + [ANY] * len(after), [VM] * len(wanted), (*(packs[mask] for mask in order), *after), 8,
+        functools.partial(attend_kernel, wanted, order, rows, len(carry)), name,
+        [jax.ShapeDtypeStruct((rows, width), BF16)] * len(wanted) + [jax.ShapeDtypeStruct(x.shape, x.dtype) for x in carry],
+        [VM] * (count + len(carry)) + [ANY] * len(after), [VM] * (len(wanted) + len(carry)),
+        (*(packs[mask] for mask in order), *carry, *after), 8,
         flops=4 * count * len(wanted) * rows * rows * width,
     )
 
@@ -264,16 +267,14 @@
     )
     for mask in order:
         packs[mask] = seq[mask](packs[mask])
-    audios = [own_audio]
-    for mask in range(1, count):
-        if mask % 2 and mask > 1:
-            audios.append(seq[1](audios[mask - 1]))
-        else:
-            audios.append(seq[mask](own_audio))
     heads = [None] * count
+    audios = [seq[mask](own_audio) if mask and (mask == 1 or mask % 2 == 0) else own_audio for mask in range(count)]
     done = [weight]
     for index, mask in enumerate(order + [0]):
-        (heads[mask],) = attend([mask], order + [0], rows, packs, done, f"attend{index}")
+        passed = [audios[m - 1] for m in range(3, count, 2)] if index == 1 else []
+        heads[mask], *passed = attend([mask], order + [0], rows, packs, done, f"attend{index}", passed)
+        for m, one in zip(range(3, count, 2), passed):
+            audios[m] = seq[1](one)
         if mask:
             done = [heads[mask]]
     own_heads = list(heads)

time: 47.7 us -> 47.1 us (0.987)
  waiting for transfers between devices: 12.1 us -> 11.6 us
    ppermute x3, waiting for transfers between devices: 10.3 us -> 0.01 us  [the longest x2 0.01 us: exchanged(): seq[mask](own_audio)]
    ppermute x3, waiting for transfers between devices: 0.01 us -> 9.73 us  [exchanged(): packs[mask] = seq[mask](packs[mask])]
  transfers between devices with their start and end apart: 16 -> 16, of which waited for: 3 -> 4; matrix products, arithmetic and copies ran while one was open for 0% -> 0% of each run, Pallas kernels for 25% -> 25%
where the time goes in v5:
time: 47.1 us; the launch traced here: 47 us
  starting transfers between devices  20.7 us (44%)
  Pallas kernels  13 us (28%)
  waiting for transfers between devices  11.6 us (25%)
  other arithmetic  0.91 us (2%)
  between operations  0.8 us (2%)
    pallas_call x15, Pallas kernels, call(): pl.pallas_call(kernel, out_shape=shapes, in_specs=ins, out_specs=outs, sc...  13 us
    ppermute x3, waiting for transfers between devices, exchanged(): packs[mask] = seq[mask](packs[mask])  9.73 us
    ppermute x3, starting transfers between devices, exchanged(): packs[mask] = seq[mask](packs[mask])  5.76 us
    ppermute x3, starting transfers between devices, exchanged(): heads[mask] = seq[mask](heads[mask])  4.52 us
    ppermute x2, starting transfers between devices, exchanged(): seq[mask](own_audio)  4.37 us
    ppermute x2, starting transfers between devices, exchanged(): partner('tensor', tensor, mask)(piece).astype(F32)  2.16 us
    ppermute x1, starting transfers between devices, halve(): other = seq[mask](pieces.pop())  2.12 us
    ppermute x1, waiting for transfers between devices, exchanged(): audio_cross, = merge(pieces[:1], seq[1](pieces[1]), True)  1.6 us
  transfers between devices with their start and end apart: 16, of which 4 were waited for; matrix products, arithmetic and copies ran while one was open for 0% of the time, Pallas kernels for 25%

profile of v5, /device:TPU:0, one launch (start us, length us, event | category | flops | bytes accessed | tf_op | source)
XLA Modules:
  0.0 47.0 jit_solution(1631383301952430149)
XLA Ops:
  0.6 1.3 %pack.1 = (bf16[384,256]{1,0:T(8,128)(2,1)S(1)}, bf16[384,256]{1,0:T(8,128)(2,1)S(1)}, bf16[384,256]{1,0:T(8,128)(2,1)S(1)}, bf16[384,256]{1,0:T(8,128)(2,1)S(1)}) custom-call(bf16[128,1024]{1,0:T(8,128)(2,1)} %q.1, bf16[128,1024]{1,0:T(8,128)(2,1)} %k.1, bf16[128,1024]{1,0:T(8,128)(2,1)} %v.1), custom_call_target="tpu_custom_call" | custom-call | tf_op jit(solution)/shard_map/pack/pallas_call | solution.py:29
  1.9 5.1 %collective-permute-start = (bf16[384,256]{1,0:T(8,128)(2,1)S(1)}, bf16[384,256]{1,0:T(8,128)(2,1)S(1)}, u32[]{:S(2)}, u32[]{:S(2)}) collective-permute-start(bf16[384,256]{1,0:T(8,128)(2,1)S(1)} %get-tuple-element.23), channel_id=1, source_target_pairs={{0,12},{4,8},{8,4},{12,0},{1,13},{5,9},{9,5},{13,1},{2,14},{6,10},... | collective-permute-start | bytes 589832 | tf_op jit(solution)/shard_map/ppermute | solution.py:269
  7.0 0.6 %collective-permute-start.2 = (bf16[384,256]{1,0:T(8,128)(2,1)S(1)}, bf16[384,256]{1,0:T(8,128)(2,1)S(1)}, u32[]{:S(2)}, u32[]{:S(2)}) collective-permute-start(bf16[384,256]{1,0:T(8,128)(2,1)S(1)} %get-tuple-element.25), channel_id=1, source_target_pairs={{0,4},{4,0},{8,12},{12,8},{1,5},{5,1},{9,13},{13,9},{2,6},{6,2},{1... | collective-permute-start | bytes 589832 | tf_op jit(solution)/shard_map/ppermute | solution.py:269
  7.7 3.5 %fetch.1 = (bf16[1024,4096]{1,0:T(8,128)(2,1)S(1)}, bf16[128,512]{1,0:T(8,128)(2,1)S(1)}, bf16[128,512]{1,0:T(8,128)(2,1)S(1)}, bf16[128,512]{1,0:T(8,128)(2,1)S...) custom-call(bf16[1024,4096]{1,0:T(8,128)(2,1)} %refs_0_.1, bf16[128,512]{1,0:T(8,128)(2,1)} %refs_1_.1, ...), custom_call_target="tpu_custom_call" | custom-call | tf_op jit(solution)/shard_map/fetch/pallas_call | solution.py:29
  11.2 2.4 %collective-permute-start.4 = (bf16[48,512]{1,0:T(8,128)(2,1)S(1)}, bf16[48,512]{1,0:T(8,128)(2,1)S(1)}, u32[]{:S(2)}, u32[]{:S(2)}) collective-permute-start(bf16[48,512]{1,0:T(8,128)(2,1)S(1)} %get-tuple-element.28.refs_0_), channel_id=1, source_target_pairs={{0,8},{4,12},{8,0},{12,4},{1,9},{5,13},{9,1},{13,5},{2,10},{6,14},... | collective-permute-start | bytes 147464 | tf_op jit(solution)/shard_map/ppermute | solution.py:271
  13.6 2.0 %collective-permute-start.7 = (bf16[48,512]{1,0:T(8,128)(2,1)S(1)}, bf16[48,512]{1,0:T(8,128)(2,1)S(1)}, u32[]{:S(2)}, u32[]{:S(2)}) collective-permute-start(bf16[48,512]{1,0:T(8,128)(2,1)S(1)} %get-tuple-element.28.refs_0_), channel_id=1, source_target_pairs={{0,4},{4,0},{8,12},{12,8},{1,5},{5,1},{9,13},{13,9},{2,6},{6,2},{1... | collective-permute-start | bytes 147464 | tf_op jit(solution)/shard_map/ppermute | solution.py:271
  15.6 9.7 %collective-permute-done.1.refs_1_ = bf16[384,256]{1,0:T(8,128)(2,1)S(1)} collective-permute-done((bf16[384,256]{1,0:T(8,128)(2,1)S(1)}, bf16[384,256]{1,0:T(8,128)(2,1)S(1)}, u32[]{:S(2)}, u32[]{:S(2)}) %collective-permute-start.1) | collective-permute-done | bytes 196640 | tf_op jit(solution)/shard_map/ppermute | solution.py:269
  25.3 0.7 %attend0.1.refs_5_ = bf16[128,256]{1,0:T(8,128)(2,1)S(1)} custom-call(bf16[384,256]{1,0:T(8,128)(2,1)S(1)} %collective-permute-done.refs_0_, bf16[384,256]{1,0:T(8,128)(2,1)S(1)} %collective-permute-done.1.refs_1_, bf16[384,256]{1,0:T(8,128)(2,1)S(1)} %collective-permute-done.2.refs_2_, bf16[384,256]{1,0:T(8,128)(2,1)S(1)} %get-tuple-element.26.refs_3_, ...), custom_call_target="tpu_custom_call" | custom-call | flops 67108864 | tf_op jit(solution)/shard_map/attend0/pallas_call | solution.py:29
  26.0 0.7 %attend1.1 = (bf16[128,256]{1,0:T(8,128)(2,1)S(1)}, bf16[48,512]{1,0:T(8,128)(2,1)S(1)}) custom-call(bf16[384,256]{1,0:T(8,128)(2,1)S(1)} %collective-permute-done.refs_0_, bf16[384,256]{1,0:T(8,128)(2,1)S(1)} %collective-permute-done.1.refs_1_, bf16[384,256]{1,0:T(8,128)(2,1)S(1)} %collective-permute-done.2.refs_2_, ...), custom_call_target="tpu_custom_call" | custom-call | flops 67108864 | tf_op jit(solution)/shard_map/attend1/pallas_call | solution.py:29
  26.8 2.5 %collective-permute-start.3 = (bf16[128,256]{1,0:T(8,128)(2,1)S(1)}, bf16[128,256]{1,0:T(8,128)(2,1)S(1)}, u32[]{:S(2)}, u32[]{:S(2)}) collective-permute-start(bf16[128,256]{1,0:T(8,128)(2,1)S(1)} %attend0.1.refs_5_), channel_id=1, source_target_pairs={{0,12},{4,8},{8,4},{12,0},{1,13},{5,9},{9,5},{13,1},{2,14},{6,10},... | collective-permute-start | bytes 196616 | tf_op jit(solution)/shard_map/ppermute | solution.py:282
  29.3 0.9 %collective-permute-start.5 = (bf16[128,256]{1,0:T(8,128)(2,1)S(1)}, bf16[128,256]{1,0:T(8,128)(2,1)S(1)}, u32[]{:S(2)}, u32[]{:S(2)}) collective-permute-start(bf16[128,256]{1,0:T(8,128)(2,1)S(1)} %get-tuple-element.29.refs_4_), channel_id=1, source_target_pairs={{0,8},{4,12},{8,0},{12,4},{1,9},{5,13},{9,1},{13,5},{2,10},{6,14},... | collective-permute-start | bytes 196616 | tf_op jit(solution)/shard_map/ppermute | solution.py:282
  30.2 0.7 %attend2.1.refs_4_ = bf16[128,256]{1,0:T(8,128)(2,1)S(1)} custom-call(bf16[384,256]{1,0:T(8,128)(2,1)S(1)} %collective-permute-done.refs_0_, bf16[384,256]{1,0:T(8,128)(2,1)S(1)} %collective-permute-done.1.refs_1_, bf16[384,256]{1,0:T(8,128)(2,1)S(1)} %collective-permute-done.2.refs_2_, bf16[384,256]{1,0:T(8,128)(2,1)S(1)} %get-tuple-element.26.refs_3_, ...), custom_call_target="tpu_custom_call" | custom-call | flops 67108864 | tf_op jit(solution)/shard_map/attend2/pallas_call | solution.py:29
  30.9 1.0 %collective-permute-start.6 = (bf16[128,256]{1,0:T(8,128)(2,1)S(1)}, bf16[128,256]{1,0:T(8,128)(2,1)S(1)}, u32[]{:S(2)}, u32[]{:S(2)}) collective-permute-start(bf16[128,256]{1,0:T(8,128)(2,1)S(1)} %attend2.1.refs_4_), channel_id=1, source_target_pairs={{0,4},{4,0},{8,12},{12,8},{1,5},{5,1},{9,13},{13,9},{2,6},{6,2},{1... | collective-permute-start | bytes 196616 | tf_op jit(solution)/shard_map/ppermute | solution.py:282
  31.9 0.7 %attend3.1.refs_3_ = bf16[128,256]{1,0:T(8,128)(2,1)S(1)} custom-call(bf16[384,256]{1,0:T(8,128)(2,1)S(1)} %collective-permute-done.refs_0_, bf16[384,256]{1,0:T(8,128)(2,1)S(1)} %collective-permute-done.1.refs_1_, bf16[384,256]{1,0:T(8,128)(2,1)S(1)} %collective-permute-done.2.refs_2_, bf16[384,256]{1,0:T(8,128)(2,1)S(1)} %get-tuple-element.26.refs_3_, ...), custom_call_target="tpu_custom_call" | custom-call | flops 67108864 | tf_op jit(solution)/shard_map/attend3/pallas_call | solution.py:29
  32.6 1.1 %partials.1 = (bf16[16,640]{1,0:T(8,128)(2,1)S(1)}, bf16[16,640]{1,0:T(8,128)(2,1)S(1)}, bf16[32,640]{1,0:T(8,128)(2,1)S(1)}) custom-call(bf16[128,512]{1,0:T(8,128)(2,1)S(1)} %get-tuple-element.30.ck, bf16[128,512]{1,0:T(8,128)(2,1)S(1)} %get-tuple-element.31.cv, bf16[48,512]{1,0:T(8,128)(2,1)S(1)} %get-tuple-element.28.refs_0_, ...), custom_call_target="tpu_custom_call" | custom-call | flops 3000000000 | tf_op jit(solution)/shard_map/partials/pallas_call | solution.py:29
  33.7 2.1 %collective-permute-start.14 = (bf16[32,640]{1,0:T(8,128)(2,1)S(1)}, bf16[32,640]{1,0:T(8,128)(2,1)S(1)}, u32[]{:S(2)}, u32[]{:S(2)}) collective-permute-start(bf16[32,640]{1,0:T(8,128)(2,1)S(1)} %get-tuple-element.38), channel_id=1, source_target_pairs={{0,8},{4,12},{8,0},{12,4},{1,9},{5,13},{9,1},{13,5},{2,10},{6,14},... | collective-permute-start | bytes 122888 | tf_op jit(solution)/shard_map/ppermute | solution.py:293
  37.7 1.6 %collective-permute-start.12 = (bf16[128,512]{1,0:T(8,128)(2,1)S(1)}, bf16[128,512]{1,0:T(8,128)(2,1)S(1)}, u32[]{:S(2)}, u32[]{:S(2)}) collective-permute-start(bf16[128,512]{1,0:T(8,128)(2,1)S(1)} %add_convert_fusion.2.refs_5_), channel_id=1, source_target_pairs={{0,2},{1,3},{2,0},{3,1},{4,6},{5,7},{6,4},{7,5},{8,10},{9,11},{10,... | collective-permute-start | bytes 393224 | tf_op jit(solution)/shard_map/ppermute | solution.py:314
  39.6 0.6 %collective-permute-start.13 = (bf16[128,512]{1,0:T(8,128)(2,1)S(1)}, bf16[128,512]{1,0:T(8,128)(2,1)S(1)}, u32[]{:S(2)}, u32[]{:S(2)}) collective-permute-start(bf16[128,512]{1,0:T(8,128)(2,1)S(1)} %add_convert_fusion.1.refs_5_.refs_4_.refs_3_), channel_id=1, source_target_pairs={{0,2},{1,3},{2,0},{3,1},{4,6},{5,7},{6,4},{7,5},{8,10},{9,11},{10,... | collective-permute-start | bytes 393224 | tf_op jit(solution)/shard_map/ppermute | solution.py:314
  40.2 0.7 %project_near.1 = (bf16[128,1024]{1,0:T(8,128)(2,1)S(1)}, f32[128,1024]{1,0:T(8,128)S(1)}) custom-call(bf16[128,256]{1,0:T(8,128)(2,1)S(1)} %collective-permute-done.3.refs_0_, bf16[128,256]{1,0:T(8,128)(2,1)S(1)} %collective-permute-done.5.refs_1_, bf16[128,256]{1,0:T(8,128)(2,1)S(1)} %collective-permute-done.6.refs_2_, ...), custom_call_target="tpu_custom_call" | custom-call | flops 536870912 | tf_op jit(solution)/shard_map/project_near/pallas_call | solution.py:29
  41.4 1.0 %collective-permute-start.15 = (bf16[16,640]{1,0:T(8,128)(2,1)S(1)}, bf16[16,640]{1,0:T(8,128)(2,1)S(1)}, u32[]{:S(2)}, u32[]{:S(2)}) collective-permute-start(bf16[16,640]{1,0:T(8,128)(2,1)S(1)} %get-tuple-element.40), channel_id=1, source_target_pairs={{0,4},{4,0},{8,12},{12,8},{1,5},{5,1},{9,13},{13,9},{2,6},{6,2},{1... | collective-permute-start | bytes 61448 | tf_op jit(solution)/shard_map/ppermute | solution.py:323
  42.4 1.3 %video_cross.1 = bf16[128,512]{1,0:T(8,128)(2,1)} custom-call(bf16[128,512]{1,0:T(8,128)(2,1)S(1)} %get-tuple-element.36.cq, bf16[48,512]{1,0:T(8,128)(2,1)S(1)} %get-tuple-element.28.refs_0_, bf16[48,512]{1,0:T(8,128)(2,1)S(1)} %collective-permute-done.7.refs_1_, bf16[48,512]{1,0:T(8,128)(2,1)S(1)} %collective-permute-done.4.refs_4_.refs_2_, ...), custom_call_target="tpu_custom_call" | custom-call | flops 16777216 | tf_op jit(solution)/shard_map/video_cross/pallas_call | solution.py:29
  43.7 1.6 %collective-permute-done.15.refs_1_ = bf16[16,640]{1,0:T(8,128)(2,1)S(1)} collective-permute-done((bf16[16,640]{1,0:T(8,128)(2,1)S(1)}, bf16[16,640]{1,0:T(8,128)(2,1)S(1)}, u32[]{:S(2)}, u32[]{:S(2)}) %collective-permute-start.15) | collective-permute-done | bytes 20512 | tf_op jit(solution)/shard_map/ppermute | solution.py:323
  45.3 0.8 %merge_last.1 = bf16[16,512]{1,0:T(8,128)(2,1)} custom-call(bf16[16,640]{1,0:T(8,128)(2,1)S(1)} %get-tuple-element.39.refs_0_, bf16[16,640]{1,0:T(8,128)(2,1)S(1)} %collective-permute-done.15.refs_1_), custom_call_target="tpu_custom_call" | custom-call | tf_op jit(solution)/shard_map/merge_last/pallas_call | solution.py:29
  46.1 0.8 %add_convert_fusion = bf16[128,1024]{1,0:T(8,128)(2,1)} fusion(bf16[128,1024]{1,0:T(8,128)(2,1)S(1)} %collective-permute-done.11, f32[128,1024]{1,0:T(8,128)S(1)} %get-tuple-element.34, bf16[128,1024]{1,0:T(8,128)(2,1)S(1)} %get-tuple-element.22, bf16[128,512]{1,0:T(8,128)(2,1)S(1)} %collective-permute-done.13, bf16[128,512]{1,0:T(8,128)(2,1)S(1)} %collective-permute-done.12), kind=kLoop, calls=%fused_computation | loop fusion | flops 1310720 | bytes 1572864 | tf_op jit(solution)/shard_map/convert_element_type | solution.py:320
  (26 shorter events, 2.7 us)
Async XLA Ops:
  1.9 13.7 %collective-permute-start = (bf16[384,256]{1,0:T(8,128)(2,1)S(1)}, bf16[384,256]{1,0:T(8,128)(2,1)S(1)}, u32[]{:S(2)}, u32[]{:S(2)}) collective-permute-start(bf16[384,256]{1,0:T(8,128)(2,1)S(1)} %get-tuple-element.23), channel_id=1, source_target_pairs={{0,12},{4,8},{8,4},{12,0},{1,13},{5,9},{9,5},{13,1},{2,14},{6,10},... | collective-permute-start | bytes 589832 | tf_op jit(solution)/shard_map/ppermute | solution.py:269
  7.0 18.3 %collective-permute-start.1 = (bf16[384,256]{1,0:T(8,128)(2,1)S(1)}, bf16[384,256]{1,0:T(8,128)(2,1)S(1)}, u32[]{:S(2)}, u32[]{:S(2)}) collective-permute-start(bf16[384,256]{1,0:T(8,128)(2,1)S(1)} %get-tuple-element.24), channel_id=1, source_target_pairs={{0,8},{4,12},{8,0},{12,4},{1,9},{5,13},{9,1},{13,5},{2,10},{6,14},... | collective-permute-start | bytes 589832 | tf_op jit(solution)/shard_map/ppermute | solution.py:269
  7.0 18.3 %collective-permute-start.2 = (bf16[384,256]{1,0:T(8,128)(2,1)S(1)}, bf16[384,256]{1,0:T(8,128)(2,1)S(1)}, u32[]{:S(2)}, u32[]{:S(2)}) collective-permute-start(bf16[384,256]{1,0:T(8,128)(2,1)S(1)} %get-tuple-element.25), channel_id=1, source_target_pairs={{0,4},{4,0},{8,12},{12,8},{1,5},{5,1},{9,13},{13,9},{2,6},{6,2},{1... | collective-permute-start | bytes 589832 | tf_op jit(solution)/shard_map/ppermute | solution.py:269
  11.2 14.8 %collective-permute-start.4 = (bf16[48,512]{1,0:T(8,128)(2,1)S(1)}, bf16[48,512]{1,0:T(8,128)(2,1)S(1)}, u32[]{:S(2)}, u32[]{:S(2)}) collective-permute-start(bf16[48,512]{1,0:T(8,128)(2,1)S(1)} %get-tuple-element.28.refs_0_), channel_id=1, source_target_pairs={{0,8},{4,12},{8,0},{12,4},{1,9},{5,13},{9,1},{13,5},{2,10},{6,14},... | collective-permute-start | bytes 147464 | tf_op jit(solution)/shard_map/ppermute | solution.py:271
  13.6 19.1 %collective-permute-start.7 = (bf16[48,512]{1,0:T(8,128)(2,1)S(1)}, bf16[48,512]{1,0:T(8,128)(2,1)S(1)}, u32[]{:S(2)}, u32[]{:S(2)}) collective-permute-start(bf16[48,512]{1,0:T(8,128)(2,1)S(1)} %get-tuple-element.28.refs_0_), channel_id=1, source_target_pairs={{0,4},{4,0},{8,12},{12,8},{1,5},{5,1},{9,13},{13,9},{2,6},{6,2},{1... | collective-permute-start | bytes 147464 | tf_op jit(solution)/shard_map/ppermute | solution.py:271
  26.7 6.0 %collective-permute-start.8 = (bf16[48,512]{1,0:T(8,128)(2,1)S(1)}, bf16[48,512]{1,0:T(8,128)(2,1)S(1)}, u32[]{:S(2)}, u32[]{:S(2)}) collective-permute-start(bf16[48,512]{1,0:T(8,128)(2,1)S(1)} %get-tuple-element.32), channel_id=1, source_target_pairs={{0,4},{4,0},{8,12},{12,8},{1,5},{5,1},{9,13},{13,9},{2,6},{6,2},{1... | collective-permute-start | bytes 147464 | tf_op jit(solution)/shard_map/ppermute | solution.py:277
  26.8 9.1 %collective-permute-start.3 = (bf16[128,256]{1,0:T(8,128)(2,1)S(1)}, bf16[128,256]{1,0:T(8,128)(2,1)S(1)}, u32[]{:S(2)}, u32[]{:S(2)}) collective-permute-start(bf16[128,256]{1,0:T(8,128)(2,1)S(1)} %attend0.1.refs_5_), channel_id=1, source_target_pairs={{0,12},{4,8},{8,4},{12,0},{1,13},{5,9},{9,5},{13,1},{2,14},{6,10},... | collective-permute-start | bytes 196616 | tf_op jit(solution)/shard_map/ppermute | solution.py:282
  29.3 6.6 %collective-permute-start.5 = (bf16[128,256]{1,0:T(8,128)(2,1)S(1)}, bf16[128,256]{1,0:T(8,128)(2,1)S(1)}, u32[]{:S(2)}, u32[]{:S(2)}) collective-permute-start(bf16[128,256]{1,0:T(8,128)(2,1)S(1)} %get-tuple-element.29.refs_4_), channel_id=1, source_target_pairs={{0,8},{4,12},{8,0},{12,4},{1,9},{5,13},{9,1},{13,5},{2,10},{6,14},... | collective-permute-start | bytes 196616 | tf_op jit(solution)/shard_map/ppermute | solution.py:282
  30.9 5.0 %collective-permute-start.6 = (bf16[128,256]{1,0:T(8,128)(2,1)S(1)}, bf16[128,256]{1,0:T(8,128)(2,1)S(1)}, u32[]{:S(2)}, u32[]{:S(2)}) collective-permute-start(bf16[128,256]{1,0:T(8,128)(2,1)S(1)} %attend2.1.refs_4_), channel_id=1, source_target_pairs={{0,4},{4,0},{8,12},{12,8},{1,5},{5,1},{9,13},{13,9},{2,6},{6,2},{1... | collective-permute-start | bytes 196616 | tf_op jit(solution)/shard_map/ppermute | solution.py:282
  33.7 7.4 %collective-permute-start.14 = (bf16[32,640]{1,0:T(8,128)(2,1)S(1)}, bf16[32,640]{1,0:T(8,128)(2,1)S(1)}, u32[]{:S(2)}, u32[]{:S(2)}) collective-permute-start(bf16[32,640]{1,0:T(8,128)(2,1)S(1)} %get-tuple-element.38), channel_id=1, source_target_pairs={{0,8},{4,12},{8,0},{12,4},{1,9},{5,13},{9,1},{13,5},{2,10},{6,14},... | collective-permute-start | bytes 122888 | tf_op jit(solution)/shard_map/ppermute | solution.py:293
  36.2 1.4 %collective-permute-start.9 = (bf16[128,512]{1,0:T(8,128)(2,1)S(1)}, bf16[128,512]{1,0:T(8,128)(2,1)S(1)}, u32[]{:S(2)}, u32[]{:S(2)}) collective-permute-start(bf16[128,512]{1,0:T(8,128)(2,1)S(1)} %project_far.2.refs_5_), channel_id=1, source_target_pairs={{0,1},{1,0},{2,3},{3,2},{4,5},{5,4},{6,7},{7,6},{8,9},{9,8},{10,11... | collective-permute-start | bytes 393224 | tf_op jit(solution)/shard_map/ppermute | solution.py:306
  36.7 2.9 %collective-permute-start.10 = (bf16[128,512]{1,0:T(8,128)(2,1)S(1)}, bf16[128,512]{1,0:T(8,128)(2,1)S(1)}, u32[]{:S(2)}, u32[]{:S(2)}) collective-permute-start(bf16[128,512]{1,0:T(8,128)(2,1)S(1)} %project_far.3.refs_5_), channel_id=1, source_target_pairs={{0,1},{1,0},{2,3},{3,2},{4,5},{5,4},{6,7},{7,6},{8,9},{9,8},{10,11... | collective-permute-start | bytes 393224 | tf_op jit(solution)/shard_map/ppermute | solution.py:306
  37.7 8.4 %collective-permute-start.12 = (bf16[128,512]{1,0:T(8,128)(2,1)S(1)}, bf16[128,512]{1,0:T(8,128)(2,1)S(1)}, u32[]{:S(2)}, u32[]{:S(2)}) collective-permute-start(bf16[128,512]{1,0:T(8,128)(2,1)S(1)} %add_convert_fusion.2.refs_5_), channel_id=1, source_target_pairs={{0,2},{1,3},{2,0},{3,1},{4,6},{5,7},{6,4},{7,5},{8,10},{9,11},{10,... | collective-permute-start | bytes 393224 | tf_op jit(solution)/shard_map/ppermute | solution.py:314
  39.6 6.5 %collective-permute-start.13 = (bf16[128,512]{1,0:T(8,128)(2,1)S(1)}, bf16[128,512]{1,0:T(8,128)(2,1)S(1)}, u32[]{:S(2)}, u32[]{:S(2)}) collective-permute-start(bf16[128,512]{1,0:T(8,128)(2,1)S(1)} %add_convert_fusion.1.refs_5_.refs_4_.refs_3_), channel_id=1, source_target_pairs={{0,2},{1,3},{2,0},{3,1},{4,6},{5,7},{6,4},{7,5},{8,10},{9,11},{10,... | collective-permute-start | bytes 393224 | tf_op jit(solution)/shard_map/ppermute | solution.py:314
  41.0 5.1 %collective-permute-start.11 = (bf16[128,1024]{1,0:T(8,128)(2,1)S(1)}, bf16[128,1024]{1,0:T(8,128)(2,1)S(1)}, u32[]{:S(2)}, u32[]{:S(2)}) collective-permute-start(bf16[128,1024]{1,0:T(8,128)(2,1)S(1)} %get-tuple-element.35), channel_id=1, source_target_pairs={{0,1},{1,0},{2,3},{3,2},{4,5},{5,4},{6,7},{7,6},{8,9},{9,8},{10,11... | collective-permute-start | bytes 786440 | tf_op jit(solution)/shard_map/ppermute | solution.py:317
  41.4 3.8 %collective-permute-start.15 = (bf16[16,640]{1,0:T(8,128)(2,1)S(1)}, bf16[16,640]{1,0:T(8,128)(2,1)S(1)}, u32[]{:S(2)}, u32[]{:S(2)}) collective-permute-start(bf16[16,640]{1,0:T(8,128)(2,1)S(1)} %get-tuple-element.40), channel_id=1, source_target_pairs={{0,4},{4,0},{8,12},{12,8},{1,5},{5,1},{9,13},{13,9},{2,6},{6,2},{1... | collective-permute-start | bytes 61448 | tf_op jit(solution)/shard_map/ppermute | solution.py:323

commit v6 on v5

--- a/solution.py
+++ b/solution.py
@@ -104,10 +104,15 @@
     )
 
 
-def fetch_kernel(count, *refs):
+def fetch_kernel(count, size, *refs):
+    sources, refs = refs[:3], refs[3:]
+    own_pack, refs = refs[-2], refs[:-2] + refs[-1:]
     pairs = list(zip(refs[:count], refs[count + 3 : 2 * count + 3]))
     own_audio, rows = refs[2 * count + 3], refs[count].shape[0]
     pairs += [(one, own_audio.at[pl.ds(kind * rows, rows)]) for kind, one in enumerate(refs[count : count + 3])]
+    rows, width = sources[0].shape[0], sources[0].shape[1] // size
+    columns = pl.ds(pl.multiple_of(lax.axis_index("seq") * width, width), width)
+    pairs += [(one.at[:, columns], own_pack.at[pl.ds(kind * rows, rows)]) for kind, one in enumerate(sources)]
     copies = [pltpu.make_async_copy(*pair, refs[-1].at[i]) for i, pair in enumerate(pairs)]
     for one in copies:
         one.start()
@@ -115,13 +120,14 @@
         one.wait()
 
 
-def fetch(arrays, audio):
+def fetch(size, video, arrays, audio):
     count = len(arrays)
     shapes = [pltpu.VMEM(x.shape, x.dtype) for x in arrays]
     shapes.append(pltpu.VMEM((3 * audio[0].shape[0], audio[0].shape[1]), BF16))
-    return call(
-        functools.partial(fetch_kernel, count), "fetch", shapes, [HBM] * (count + 3), [VM] * (count + 1),
-        (*arrays, *audio), 53, [pltpu.SemaphoreType.DMA((count + 3,))],
+    shapes.append(pltpu.VMEM((3 * video[0].shape[0], video[0].shape[1] // size), BF16))
+    return call(
+        functools.partial(fetch_kernel, count, size), "fetch", shapes, [HBM] * (count + 6), [VM] * (count + 2),
+        (*video, *arrays, *audio), 53, [pltpu.SemaphoreType.DMA((count + 6,))],
     )
 
 
@@ -260,10 +266,10 @@
     order = list(range(count - 1, 0, -1))
 
     packs = [None] * count
-    for mask, one in zip(order + [0], pack(order + [0], count, video_query, video_key, video_value)):
+    for mask, one in zip(order, pack(order, count, video_query, video_key, video_value)):
         packs[mask] = one
-    weight, cross_query, cross_key, cross_value, video_stream, own_audio = fetch(
-        (out_weight, cross_query, cross_key, cross_value, video_stream), (audio_key, audio_value, audio_query)
+    weight, cross_query, cross_key, cross_value, video_stream, own_audio, packs[0] = fetch(
+        count, (video_query, video_key, video_value), (out_weight, cross_query, cross_key, cross_value, video_stream), (audio_key, audio_value, audio_query)
     )
     for mask in order:
         packs[mask] = seq[mask](packs[mask])

time: 47.1 us -> 47.1 us (level)
  no operation moved by 1% of the time
where the time goes in v6:
time: 47.1 us; the launch traced here: 46.9 us
  starting transfers between devices  20.7 us (44%)
  Pallas kernels  13 us (28%)
  waiting for transfers between devices  11.5 us (24%)
  other arithmetic  0.91 us (2%)
  between operations  0.79 us (2%)
    pallas_call x15, Pallas kernels, call(): pl.pallas_call(kernel, out_shape=shapes, in_specs=ins, out_specs=outs, sc...  13 us
    ppermute x3, waiting for transfers between devices, exchanged(): packs[mask] = seq[mask](packs[mask])  9.65 us
    ppermute x3, starting transfers between devices, exchanged(): packs[mask] = seq[mask](packs[mask])  5.76 us
    ppermute x3, starting transfers between devices, exchanged(): heads[mask] = seq[mask](heads[mask])  4.52 us
    ppermute x2, starting transfers between devices, exchanged(): seq[mask](own_audio)  4.37 us
    ppermute x2, starting transfers between devices, exchanged(): partner('tensor', tensor, mask)(piece).astype(F32)  2.16 us
    ppermute x1, starting transfers between devices, halve(): other = seq[mask](pieces.pop())  2.12 us
    ppermute x1, waiting for transfers between devices, exchanged(): audio_cross, = merge(pieces[:1], seq[1](pieces[1]), True)  1.61 us
  transfers between devices with their start and end apart: 16, of which 4 were waited for; matrix products, arithmetic and copies ran while one was open for 0% of the time, Pallas kernels for 25%

profile of v6, /device:TPU:0, one launch (start us, length us, event | category | flops | bytes accessed | tf_op | source)
XLA Modules:
  0.0 46.9 jit_solution(18367538760448241083)
XLA Ops:
  0.6 1.2 %pack.1 = (bf16[384,256]{1,0:T(8,128)(2,1)S(1)}, bf16[384,256]{1,0:T(8,128)(2,1)S(1)}, bf16[384,256]{1,0:T(8,128)(2,1)S(1)}) custom-call(bf16[128,1024]{1,0:T(8,128)(2,1)} %q.1, bf16[128,1024]{1,0:T(8,128)(2,1)} %k.1, bf16[128,1024]{1,0:T(8,128)(2,1)} %v.1), custom_call_target="tpu_custom_call" | custom-call | tf_op jit(solution)/shard_map/pack/pallas_call | solution.py:29
  1.8 5.1 %collective-permute-start = (bf16[384,256]{1,0:T(8,128)(2,1)S(1)}, bf16[384,256]{1,0:T(8,128)(2,1)S(1)}, u32[]{:S(2)}, u32[]{:S(2)}) collective-permute-start(bf16[384,256]{1,0:T(8,128)(2,1)S(1)} %get-tuple-element.23), channel_id=1, source_target_pairs={{0,12},{4,8},{8,4},{12,0},{1,13},{5,9},{9,5},{13,1},{2,14},{6,10},... | collective-permute-start | bytes 589832 | tf_op jit(solution)/shard_map/ppermute | solution.py:275
  6.9 0.6 %collective-permute-start.2 = (bf16[384,256]{1,0:T(8,128)(2,1)S(1)}, bf16[384,256]{1,0:T(8,128)(2,1)S(1)}, u32[]{:S(2)}, u32[]{:S(2)}) collective-permute-start(bf16[384,256]{1,0:T(8,128)(2,1)S(1)} %get-tuple-element.25), channel_id=1, source_target_pairs={{0,4},{4,0},{8,12},{12,8},{1,5},{5,1},{9,13},{13,9},{2,6},{6,2},{1... | collective-permute-start | bytes 589832 | tf_op jit(solution)/shard_map/ppermute | solution.py:275
  7.6 3.6 %fetch.1 = (bf16[1024,4096]{1,0:T(8,128)(2,1)S(1)}, bf16[128,512]{1,0:T(8,128)(2,1)S(1)}, bf16[128,512]{1,0:T(8,128)(2,1)S(1)}, bf16[128,512]{1,0:T(8,128)(2,1)S...) custom-call(bf16[128,1024]{1,0:T(8,128)(2,1)} %q.1, ...), custom_call_target="tpu_custom_call" | custom-call | tf_op jit(solution)/shard_map/fetch/pallas_call | solution.py:29
  11.2 2.4 %collective-permute-start.4 = (bf16[48,512]{1,0:T(8,128)(2,1)S(1)}, bf16[48,512]{1,0:T(8,128)(2,1)S(1)}, u32[]{:S(2)}, u32[]{:S(2)}) collective-permute-start(bf16[48,512]{1,0:T(8,128)(2,1)S(1)} %get-tuple-element.28.refs_0_), channel_id=1, source_target_pairs={{0,8},{4,12},{8,0},{12,4},{1,9},{5,13},{9,1},{13,5},{2,10},{6,14},... | collective-permute-start | bytes 147464 | tf_op jit(solution)/shard_map/ppermute | solution.py:277
  13.5 2.0 %collective-permute-start.7 = (bf16[48,512]{1,0:T(8,128)(2,1)S(1)}, bf16[48,512]{1,0:T(8,128)(2,1)S(1)}, u32[]{:S(2)}, u32[]{:S(2)}) collective-permute-start(bf16[48,512]{1,0:T(8,128)(2,1)S(1)} %get-tuple-element.28.refs_0_), channel_id=1, source_target_pairs={{0,4},{4,0},{8,12},{12,8},{1,5},{5,1},{9,13},{13,9},{2,6},{6,2},{1... | collective-permute-start | bytes 147464 | tf_op jit(solution)/shard_map/ppermute | solution.py:277
  15.6 9.6 %collective-permute-done.1.refs_1_ = bf16[384,256]{1,0:T(8,128)(2,1)S(1)} collective-permute-done((bf16[384,256]{1,0:T(8,128)(2,1)S(1)}, bf16[384,256]{1,0:T(8,128)(2,1)S(1)}, u32[]{:S(2)}, u32[]{:S(2)}) %collective-permute-start.1) | collective-permute-done | bytes 196640 | tf_op jit(solution)/shard_map/ppermute | solution.py:275
  25.2 0.7 %attend0.1.refs_5_ = bf16[128,256]{1,0:T(8,128)(2,1)S(1)} custom-call(bf16[384,256]{1,0:T(8,128)(2,1)S(1)} %collective-permute-done.refs_0_, bf16[384,256]{1,0:T(8,128)(2,1)S(1)} %collective-permute-done.1.refs_1_, bf16[384,256]{1,0:T(8,128)(2,1)S(1)} %collective-permute-done.2.refs_2_, bf16[384,256]{1,0:T(8,128)(2,1)S(1)} %get-tuple-element.26.refs_3_, ...), custom_call_target="tpu_custom_call" | custom-call | flops 67108864 | tf_op jit(solution)/shard_map/attend0/pallas_call | solution.py:29
  25.9 0.7 %attend1.1 = (bf16[128,256]{1,0:T(8,128)(2,1)S(1)}, bf16[48,512]{1,0:T(8,128)(2,1)S(1)}) custom-call(bf16[384,256]{1,0:T(8,128)(2,1)S(1)} %collective-permute-done.refs_0_, bf16[384,256]{1,0:T(8,128)(2,1)S(1)} %collective-permute-done.1.refs_1_, bf16[384,256]{1,0:T(8,128)(2,1)S(1)} %collective-permute-done.2.refs_2_, ...), custom_call_target="tpu_custom_call" | custom-call | flops 67108864 | tf_op jit(solution)/shard_map/attend1/pallas_call | solution.py:29
  26.7 2.5 %collective-permute-start.3 = (bf16[128,256]{1,0:T(8,128)(2,1)S(1)}, bf16[128,256]{1,0:T(8,128)(2,1)S(1)}, u32[]{:S(2)}, u32[]{:S(2)}) collective-permute-start(bf16[128,256]{1,0:T(8,128)(2,1)S(1)} %attend0.1.refs_5_), channel_id=1, source_target_pairs={{0,12},{4,8},{8,4},{12,0},{1,13},{5,9},{9,5},{13,1},{2,14},{6,10},... | collective-permute-start | bytes 196616 | tf_op jit(solution)/shard_map/ppermute | solution.py:288
  29.2 0.9 %collective-permute-start.5 = (bf16[128,256]{1,0:T(8,128)(2,1)S(1)}, bf16[128,256]{1,0:T(8,128)(2,1)S(1)}, u32[]{:S(2)}, u32[]{:S(2)}) collective-permute-start(bf16[128,256]{1,0:T(8,128)(2,1)S(1)} %get-tuple-element.29.refs_4_), channel_id=1, source_target_pairs={{0,8},{4,12},{8,0},{12,4},{1,9},{5,13},{9,1},{13,5},{2,10},{6,14},... | collective-permute-start | bytes 196616 | tf_op jit(solution)/shard_map/ppermute | solution.py:288
  30.1 0.7 %attend2.1.refs_4_ = bf16[128,256]{1,0:T(8,128)(2,1)S(1)} custom-call(bf16[384,256]{1,0:T(8,128)(2,1)S(1)} %collective-permute-done.refs_0_, bf16[384,256]{1,0:T(8,128)(2,1)S(1)} %collective-permute-done.1.refs_1_, bf16[384,256]{1,0:T(8,128)(2,1)S(1)} %collective-permute-done.2.refs_2_, bf16[384,256]{1,0:T(8,128)(2,1)S(1)} %get-tuple-element.26.refs_3_, ...), custom_call_target="tpu_custom_call" | custom-call | flops 67108864 | tf_op jit(solution)/shard_map/attend2/pallas_call | solution.py:29
  30.8 1.0 %collective-permute-start.6 = (bf16[128,256]{1,0:T(8,128)(2,1)S(1)}, bf16[128,256]{1,0:T(8,128)(2,1)S(1)}, u32[]{:S(2)}, u32[]{:S(2)}) collective-permute-start(bf16[128,256]{1,0:T(8,128)(2,1)S(1)} %attend2.1.refs_4_), channel_id=1, source_target_pairs={{0,4},{4,0},{8,12},{12,8},{1,5},{5,1},{9,13},{13,9},{2,6},{6,2},{1... | collective-permute-start | bytes 196616 | tf_op jit(solution)/shard_map/ppermute | solution.py:288
  31.9 0.7 %attend3.1.refs_3_ = bf16[128,256]{1,0:T(8,128)(2,1)S(1)} custom-call(bf16[384,256]{1,0:T(8,128)(2,1)S(1)} %collective-permute-done.refs_0_, bf16[384,256]{1,0:T(8,128)(2,1)S(1)} %collective-permute-done.1.refs_1_, bf16[384,256]{1,0:T(8,128)(2,1)S(1)} %collective-permute-done.2.refs_2_, bf16[384,256]{1,0:T(8,128)(2,1)S(1)} %get-tuple-element.26.refs_3_, ...), custom_call_target="tpu_custom_call" | custom-call | flops 67108864 | tf_op jit(solution)/shard_map/attend3/pallas_call | solution.py:29
  32.6 1.1 %partials.1 = (bf16[16,640]{1,0:T(8,128)(2,1)S(1)}, bf16[16,640]{1,0:T(8,128)(2,1)S(1)}, bf16[32,640]{1,0:T(8,128)(2,1)S(1)}) custom-call(bf16[128,512]{1,0:T(8,128)(2,1)S(1)} %get-tuple-element.30.ck, bf16[128,512]{1,0:T(8,128)(2,1)S(1)} %get-tuple-element.31.cv, bf16[48,512]{1,0:T(8,128)(2,1)S(1)} %get-tuple-element.28.refs_0_, ...), custom_call_target="tpu_custom_call" | custom-call | flops 3000000000 | tf_op jit(solution)/shard_map/partials/pallas_call | solution.py:29
  33.6 2.1 %collective-permute-start.14 = (bf16[32,640]{1,0:T(8,128)(2,1)S(1)}, bf16[32,640]{1,0:T(8,128)(2,1)S(1)}, u32[]{:S(2)}, u32[]{:S(2)}) collective-permute-start(bf16[32,640]{1,0:T(8,128)(2,1)S(1)} %get-tuple-element.38), channel_id=1, source_target_pairs={{0,8},{4,12},{8,0},{12,4},{1,9},{5,13},{9,1},{13,5},{2,10},{6,14},... | collective-permute-start | bytes 122888 | tf_op jit(solution)/shard_map/ppermute | solution.py:299
  37.6 1.6 %collective-permute-start.12 = (bf16[128,512]{1,0:T(8,128)(2,1)S(1)}, bf16[128,512]{1,0:T(8,128)(2,1)S(1)}, u32[]{:S(2)}, u32[]{:S(2)}) collective-permute-start(bf16[128,512]{1,0:T(8,128)(2,1)S(1)} %add_convert_fusion.2.refs_5_), channel_id=1, source_target_pairs={{0,2},{1,3},{2,0},{3,1},{4,6},{5,7},{6,4},{7,5},{8,10},{9,11},{10,... | collective-permute-start | bytes 393224 | tf_op jit(solution)/shard_map/ppermute | solution.py:320
  39.6 0.6 %collective-permute-start.13 = (bf16[128,512]{1,0:T(8,128)(2,1)S(1)}, bf16[128,512]{1,0:T(8,128)(2,1)S(1)}, u32[]{:S(2)}, u32[]{:S(2)}) collective-permute-start(bf16[128,512]{1,0:T(8,128)(2,1)S(1)} %add_convert_fusion.1.refs_5_.refs_4_.refs_3_), channel_id=1, source_target_pairs={{0,2},{1,3},{2,0},{3,1},{4,6},{5,7},{6,4},{7,5},{8,10},{9,11},{10,... | collective-permute-start | bytes 393224 | tf_op jit(solution)/shard_map/ppermute | solution.py:320
  40.1 0.8 %project_near.1 = (bf16[128,1024]{1,0:T(8,128)(2,1)S(1)}, f32[128,1024]{1,0:T(8,128)S(1)}) custom-call(bf16[128,256]{1,0:T(8,128)(2,1)S(1)} %collective-permute-done.3.refs_0_, bf16[128,256]{1,0:T(8,128)(2,1)S(1)} %collective-permute-done.5.refs_1_, bf16[128,256]{1,0:T(8,128)(2,1)S(1)} %collective-permute-done.6.refs_2_, ...), custom_call_target="tpu_custom_call" | custom-call | flops 536870912 | tf_op jit(solution)/shard_map/project_near/pallas_call | solution.py:29
  41.4 1.0 %collective-permute-start.15 = (bf16[16,640]{1,0:T(8,128)(2,1)S(1)}, bf16[16,640]{1,0:T(8,128)(2,1)S(1)}, u32[]{:S(2)}, u32[]{:S(2)}) collective-permute-start(bf16[16,640]{1,0:T(8,128)(2,1)S(1)} %get-tuple-element.40), channel_id=1, source_target_pairs={{0,4},{4,0},{8,12},{12,8},{1,5},{5,1},{9,13},{13,9},{2,6},{6,2},{1... | collective-permute-start | bytes 61448 | tf_op jit(solution)/shard_map/ppermute | solution.py:329
  42.3 1.3 %video_cross.1 = bf16[128,512]{1,0:T(8,128)(2,1)} custom-call(bf16[128,512]{1,0:T(8,128)(2,1)S(1)} %get-tuple-element.36.cq, bf16[48,512]{1,0:T(8,128)(2,1)S(1)} %get-tuple-element.28.refs_0_, bf16[48,512]{1,0:T(8,128)(2,1)S(1)} %collective-permute-done.7.refs_1_, bf16[48,512]{1,0:T(8,128)(2,1)S(1)} %collective-permute-done.4.refs_4_.refs_2_, ...), custom_call_target="tpu_custom_call" | custom-call | flops 16777216 | tf_op jit(solution)/shard_map/video_cross/pallas_call | solution.py:29
  43.6 1.6 %collective-permute-done.15.refs_1_ = bf16[16,640]{1,0:T(8,128)(2,1)S(1)} collective-permute-done((bf16[16,640]{1,0:T(8,128)(2,1)S(1)}, bf16[16,640]{1,0:T(8,128)(2,1)S(1)}, u32[]{:S(2)}, u32[]{:S(2)}) %collective-permute-start.15) | collective-permute-done | bytes 20512 | tf_op jit(solution)/shard_map/ppermute | solution.py:329
  45.2 0.8 %merge_last.1 = bf16[16,512]{1,0:T(8,128)(2,1)} custom-call(bf16[16,640]{1,0:T(8,128)(2,1)S(1)} %get-tuple-element.39.refs_0_, bf16[16,640]{1,0:T(8,128)(2,1)S(1)} %collective-permute-done.15.refs_1_), custom_call_target="tpu_custom_call" | custom-call | tf_op jit(solution)/shard_map/merge_last/pallas_call | solution.py:29
  46.0 0.8 %add_convert_fusion = bf16[128,1024]{1,0:T(8,128)(2,1)} fusion(bf16[128,1024]{1,0:T(8,128)(2,1)S(1)} %collective-permute-done.11, f32[128,1024]{1,0:T(8,128)S(1)} %get-tuple-element.34, bf16[128,1024]{1,0:T(8,128)(2,1)S(1)} %get-tuple-element.22, bf16[128,512]{1,0:T(8,128)(2,1)S(1)} %collective-permute-done.13, bf16[128,512]{1,0:T(8,128)(2,1)S(1)} %collective-permute-done.12), kind=kLoop, calls=%fused_computation | loop fusion | flops 1310720 | bytes 1572864 | tf_op jit(solution)/shard_map/convert_element_type | solution.py:326
  (26 shorter events, 2.8 us)
Async XLA Ops:
  1.8 13.7 %collective-permute-start = (bf16[384,256]{1,0:T(8,128)(2,1)S(1)}, bf16[384,256]{1,0:T(8,128)(2,1)S(1)}, u32[]{:S(2)}, u32[]{:S(2)}) collective-permute-start(bf16[384,256]{1,0:T(8,128)(2,1)S(1)} %get-tuple-element.23), channel_id=1, source_target_pairs={{0,12},{4,8},{8,4},{12,0},{1,13},{5,9},{9,5},{13,1},{2,14},{6,10},... | collective-permute-start | bytes 589832 | tf_op jit(solution)/shard_map/ppermute | solution.py:275
  6.9 18.3 %collective-permute-start.1 = (bf16[384,256]{1,0:T(8,128)(2,1)S(1)}, bf16[384,256]{1,0:T(8,128)(2,1)S(1)}, u32[]{:S(2)}, u32[]{:S(2)}) collective-permute-start(bf16[384,256]{1,0:T(8,128)(2,1)S(1)} %get-tuple-element.24), channel_id=1, source_target_pairs={{0,8},{4,12},{8,0},{12,4},{1,9},{5,13},{9,1},{13,5},{2,10},{6,14},... | collective-permute-start | bytes 589832 | tf_op jit(solution)/shard_map/ppermute | solution.py:275
  6.9 18.3 %collective-permute-start.2 = (bf16[384,256]{1,0:T(8,128)(2,1)S(1)}, bf16[384,256]{1,0:T(8,128)(2,1)S(1)}, u32[]{:S(2)}, u32[]{:S(2)}) collective-permute-start(bf16[384,256]{1,0:T(8,128)(2,1)S(1)} %get-tuple-element.25), channel_id=1, source_target_pairs={{0,4},{4,0},{8,12},{12,8},{1,5},{5,1},{9,13},{13,9},{2,6},{6,2},{1... | collective-permute-start | bytes 589832 | tf_op jit(solution)/shard_map/ppermute | solution.py:275
  11.2 14.7 %collective-permute-start.4 = (bf16[48,512]{1,0:T(8,128)(2,1)S(1)}, bf16[48,512]{1,0:T(8,128)(2,1)S(1)}, u32[]{:S(2)}, u32[]{:S(2)}) collective-permute-start(bf16[48,512]{1,0:T(8,128)(2,1)S(1)} %get-tuple-element.28.refs_0_), channel_id=1, source_target_pairs={{0,8},{4,12},{8,0},{12,4},{1,9},{5,13},{9,1},{13,5},{2,10},{6,14},... | collective-permute-start | bytes 147464 | tf_op jit(solution)/shard_map/ppermute | solution.py:277
  13.5 19.0 %collective-permute-start.7 = (bf16[48,512]{1,0:T(8,128)(2,1)S(1)}, bf16[48,512]{1,0:T(8,128)(2,1)S(1)}, u32[]{:S(2)}, u32[]{:S(2)}) collective-permute-start(bf16[48,512]{1,0:T(8,128)(2,1)S(1)} %get-tuple-element.28.refs_0_), channel_id=1, source_target_pairs={{0,4},{4,0},{8,12},{12,8},{1,5},{5,1},{9,13},{13,9},{2,6},{6,2},{1... | collective-permute-start | bytes 147464 | tf_op jit(solution)/shard_map/ppermute | solution.py:277
  26.6 6.0 %collective-permute-start.8 = (bf16[48,512]{1,0:T(8,128)(2,1)S(1)}, bf16[48,512]{1,0:T(8,128)(2,1)S(1)}, u32[]{:S(2)}, u32[]{:S(2)}) collective-permute-start(bf16[48,512]{1,0:T(8,128)(2,1)S(1)} %get-tuple-element.32), channel_id=1, source_target_pairs={{0,4},{4,0},{8,12},{12,8},{1,5},{5,1},{9,13},{13,9},{2,6},{6,2},{1... | collective-permute-start | bytes 147464 | tf_op jit(solution)/shard_map/ppermute | solution.py:283
  26.7 9.1 %collective-permute-start.3 = (bf16[128,256]{1,0:T(8,128)(2,1)S(1)}, bf16[128,256]{1,0:T(8,128)(2,1)S(1)}, u32[]{:S(2)}, u32[]{:S(2)}) collective-permute-start(bf16[128,256]{1,0:T(8,128)(2,1)S(1)} %attend0.1.refs_5_), channel_id=1, source_target_pairs={{0,12},{4,8},{8,4},{12,0},{1,13},{5,9},{9,5},{13,1},{2,14},{6,10},... | collective-permute-start | bytes 196616 | tf_op jit(solution)/shard_map/ppermute | solution.py:288
  29.2 6.6 %collective-permute-start.5 = (bf16[128,256]{1,0:T(8,128)(2,1)S(1)}, bf16[128,256]{1,0:T(8,128)(2,1)S(1)}, u32[]{:S(2)}, u32[]{:S(2)}) collective-permute-start(bf16[128,256]{1,0:T(8,128)(2,1)S(1)} %get-tuple-element.29.refs_4_), channel_id=1, source_target_pairs={{0,8},{4,12},{8,0},{12,4},{1,9},{5,13},{9,1},{13,5},{2,10},{6,14},... | collective-permute-start | bytes 196616 | tf_op jit(solution)/shard_map/ppermute | solution.py:288
  30.8 5.0 %collective-permute-start.6 = (bf16[128,256]{1,0:T(8,128)(2,1)S(1)}, bf16[128,256]{1,0:T(8,128)(2,1)S(1)}, u32[]{:S(2)}, u32[]{:S(2)}) collective-permute-start(bf16[128,256]{1,0:T(8,128)(2,1)S(1)} %attend2.1.refs_4_), channel_id=1, source_target_pairs={{0,4},{4,0},{8,12},{12,8},{1,5},{5,1},{9,13},{13,9},{2,6},{6,2},{1... | collective-permute-start | bytes 196616 | tf_op jit(solution)/shard_map/ppermute | solution.py:288
  33.6 7.4 %collective-permute-start.14 = (bf16[32,640]{1,0:T(8,128)(2,1)S(1)}, bf16[32,640]{1,0:T(8,128)(2,1)S(1)}, u32[]{:S(2)}, u32[]{:S(2)}) collective-permute-start(bf16[32,640]{1,0:T(8,128)(2,1)S(1)} %get-tuple-element.38), channel_id=1, source_target_pairs={{0,8},{4,12},{8,0},{12,4},{1,9},{5,13},{9,1},{13,5},{2,10},{6,14},... | collective-permute-start | bytes 122888 | tf_op jit(solution)/shard_map/ppermute | solution.py:299
  36.2 1.4 %collective-permute-start.9 = (bf16[128,512]{1,0:T(8,128)(2,1)S(1)}, bf16[128,512]{1,0:T(8,128)(2,1)S(1)}, u32[]{:S(2)}, u32[]{:S(2)}) collective-permute-start(bf16[128,512]{1,0:T(8,128)(2,1)S(1)} %project_far.2.refs_5_), channel_id=1, source_target_pairs={{0,1},{1,0},{2,3},{3,2},{4,5},{5,4},{6,7},{7,6},{8,9},{9,8},{10,11... | collective-permute-start | bytes 393224 | tf_op jit(solution)/shard_map/ppermute | solution.py:312
  36.6 2.9 %collective-permute-start.10 = (bf16[128,512]{1,0:T(8,128)(2,1)S(1)}, bf16[128,512]{1,0:T(8,128)(2,1)S(1)}, u32[]{:S(2)}, u32[]{:S(2)}) collective-permute-start(bf16[128,512]{1,0:T(8,128)(2,1)S(1)} %project_far.3.refs_5_), channel_id=1, source_target_pairs={{0,1},{1,0},{2,3},{3,2},{4,5},{5,4},{6,7},{7,6},{8,9},{9,8},{10,11... | collective-permute-start | bytes 393224 | tf_op jit(solution)/shard_map/ppermute | solution.py:312
  37.6 8.4 %collective-permute-start.12 = (bf16[128,512]{1,0:T(8,128)(2,1)S(1)}, bf16[128,512]{1,0:T(8,128)(2,1)S(1)}, u32[]{:S(2)}, u32[]{:S(2)}) collective-permute-start(bf16[128,512]{1,0:T(8,128)(2,1)S(1)} %add_convert_fusion.2.refs_5_), channel_id=1, source_target_pairs={{0,2},{1,3},{2,0},{3,1},{4,6},{5,7},{6,4},{7,5},{8,10},{9,11},{10,... | collective-permute-start | bytes 393224 | tf_op jit(solution)/shard_map/ppermute | solution.py:320
  39.6 6.5 %collective-permute-start.13 = (bf16[128,512]{1,0:T(8,128)(2,1)S(1)}, bf16[128,512]{1,0:T(8,128)(2,1)S(1)}, u32[]{:S(2)}, u32[]{:S(2)}) collective-permute-start(bf16[128,512]{1,0:T(8,128)(2,1)S(1)} %add_convert_fusion.1.refs_5_.refs_4_.refs_3_), channel_id=1, source_target_pairs={{0,2},{1,3},{2,0},{3,1},{4,6},{5,7},{6,4},{7,5},{8,10},{9,11},{10,... | collective-permute-start | bytes 393224 | tf_op jit(solution)/shard_map/ppermute | solution.py:320
  40.9 5.1 %collective-permute-start.11 = (bf16[128,1024]{1,0:T(8,128)(2,1)S(1)}, bf16[128,1024]{1,0:T(8,128)(2,1)S(1)}, u32[]{:S(2)}, u32[]{:S(2)}) collective-permute-start(bf16[128,1024]{1,0:T(8,128)(2,1)S(1)} %get-tuple-element.35), channel_id=1, source_target_pairs={{0,1},{1,0},{2,3},{3,2},{4,5},{5,4},{6,7},{7,6},{8,9},{9,8},{10,11... | collective-permute-start | bytes 786440 | tf_op jit(solution)/shard_map/ppermute | solution.py:323
  41.4 3.8 %collective-permute-start.15 = (bf16[16,640]{1,0:T(8,128)(2,1)S(1)}, bf16[16,640]{1,0:T(8,128)(2,1)S(1)}, u32[]{:S(2)}, u32[]{:S(2)}) collective-permute-start(bf16[16,640]{1,0:T(8,128)(2,1)S(1)} %get-tuple-element.40), channel_id=1, source_target_pairs={{0,4},{4,0},{8,12},{12,8},{1,5},{5,1},{9,13},{13,9},{2,6},{6,2},{1... | collective-permute-start | bytes 61448 | tf_op jit(solution)/shard_map/ppermute | solution.py:329

commit v7 on v6

--- a/solution.py
+++ b/solution.py
@@ -21,7 +21,7 @@
 WHOLE_VMEM = 62.75
 
 
-COSTS = {"merge": 10000000000, "partials": 3000000000, "project_kept": 10000000000}
+COSTS = {"merge": 10000000000, "partials": 3000000000, "project_kept": 10000000000, "attend2": 1000000000}
 
 
 def call(kernel, name, shapes, ins, outs, operands, limit, scratch=(), flops=0):

time: 47.1 us -> 47.9 us (1.017)
  waiting for transfers between devices: 11.5 us -> 12.1 us
    ppermute x1, waiting for transfers between devices: 0.01 us -> 0.99 us  [exchanged(): audios[m] = seq[1](one)]
where the time goes in v7:
time: 47.9 us; the launch traced here: 47.8 us
  starting transfers between devices  20.9 us (44%)
  Pallas kernels  13 us (27%)
  waiting for transfers between devices  12.1 us (25%)
  other arithmetic  0.91 us (2%)
  between operations  0.78 us (2%)
    pallas_call x15, Pallas kernels, call(): pl.pallas_call(kernel, out_shape=shapes, in_specs=ins, out_specs=outs, sc...  13 us
    ppermute x3, waiting for transfers between devices, exchanged(): packs[mask] = seq[mask](packs[mask])  9.65 us
    ppermute x3, starting transfers between devices, exchanged(): packs[mask] = seq[mask](packs[mask])  5.76 us
    ppermute x3, starting transfers between devices, exchanged(): heads[mask] = seq[mask](heads[mask])  4.62 us
    ppermute x2, starting transfers between devices, exchanged(): seq[mask](own_audio)  4.37 us
    ppermute x2, starting transfers between devices, exchanged(): partner('tensor', tensor, mask)(piece).astype(F32)  2.16 us
    ppermute x1, starting transfers between devices, halve(): other = seq[mask](pieces.pop())  2 us
    ppermute x1, waiting for transfers between devices, exchanged(): audio_cross, = merge(pieces[:1], seq[1](pieces[1]), True)  1.33 us
  transfers between devices with their start and end apart: 16, of which 4 were waited for; matrix products, arithmetic and copies ran while one was open for 0% of the time, Pallas kernels for 25%

profile of v7, /device:TPU:0, one launch (start us, length us, event | category | flops | bytes accessed | tf_op | source)
XLA Modules:
  0.0 47.8 jit_solution(7314596439039851606)
XLA Ops:
  0.6 1.2 %pack.1 = (bf16[384,256]{1,0:T(8,128)(2,1)S(1)}, bf16[384,256]{1,0:T(8,128)(2,1)S(1)}, bf16[384,256]{1,0:T(8,128)(2,1)S(1)}) custom-call(bf16[128,1024]{1,0:T(8,128)(2,1)} %q.1, bf16[128,1024]{1,0:T(8,128)(2,1)} %k.1, bf16[128,1024]{1,0:T(8,128)(2,1)} %v.1), custom_call_target="tpu_custom_call" | custom-call | tf_op jit(solution)/shard_map/pack/pallas_call | solution.py:29
  1.8 5.1 %collective-permute-start = (bf16[384,256]{1,0:T(8,128)(2,1)S(1)}, bf16[384,256]{1,0:T(8,128)(2,1)S(1)}, u32[]{:S(2)}, u32[]{:S(2)}) collective-permute-start(bf16[384,256]{1,0:T(8,128)(2,1)S(1)} %get-tuple-element.23), channel_id=1, source_target_pairs={{0,12},{4,8},{8,4},{12,0},{1,13},{5,9},{9,5},{13,1},{2,14},{6,10},... | collective-permute-start | bytes 589832 | tf_op jit(solution)/shard_map/ppermute | solution.py:275
  6.9 0.6 %collective-permute-start.2 = (bf16[384,256]{1,0:T(8,128)(2,1)S(1)}, bf16[384,256]{1,0:T(8,128)(2,1)S(1)}, u32[]{:S(2)}, u32[]{:S(2)}) collective-permute-start(bf16[384,256]{1,0:T(8,128)(2,1)S(1)} %get-tuple-element.25), channel_id=1, source_target_pairs={{0,4},{4,0},{8,12},{12,8},{1,5},{5,1},{9,13},{13,9},{2,6},{6,2},{1... | collective-permute-start | bytes 589832 | tf_op jit(solution)/shard_map/ppermute | solution.py:275
  7.6 3.6 %fetch.1 = (bf16[1024,4096]{1,0:T(8,128)(2,1)S(1)}, bf16[128,512]{1,0:T(8,128)(2,1)S(1)}, bf16[128,512]{1,0:T(8,128)(2,1)S(1)}, bf16[128,512]{1,0:T(8,128)(2,1)S...) custom-call(bf16[128,1024]{1,0:T(8,128)(2,1)} %q.1, ...), custom_call_target="tpu_custom_call" | custom-call | tf_op jit(solution)/shard_map/fetch/pallas_call | solution.py:29
  11.2 2.4 %collective-permute-start.4 = (bf16[48,512]{1,0:T(8,128)(2,1)S(1)}, bf16[48,512]{1,0:T(8,128)(2,1)S(1)}, u32[]{:S(2)}, u32[]{:S(2)}) collective-permute-start(bf16[48,512]{1,0:T(8,128)(2,1)S(1)} %get-tuple-element.28.refs_0_), channel_id=1, source_target_pairs={{0,8},{4,12},{8,0},{12,4},{1,9},{5,13},{9,1},{13,5},{2,10},{6,14},... | collective-permute-start | bytes 147464 | tf_op jit(solution)/shard_map/ppermute | solution.py:277
  13.5 2.0 %collective-permute-start.7 = (bf16[48,512]{1,0:T(8,128)(2,1)S(1)}, bf16[48,512]{1,0:T(8,128)(2,1)S(1)}, u32[]{:S(2)}, u32[]{:S(2)}) collective-permute-start(bf16[48,512]{1,0:T(8,128)(2,1)S(1)} %get-tuple-element.28.refs_0_), channel_id=1, source_target_pairs={{0,4},{4,0},{8,12},{12,8},{1,5},{5,1},{9,13},{13,9},{2,6},{6,2},{1... | collective-permute-start | bytes 147464 | tf_op jit(solution)/shard_map/ppermute | solution.py:277
  15.6 9.6 %collective-permute-done.1.refs_1_ = bf16[384,256]{1,0:T(8,128)(2,1)S(1)} collective-permute-done((bf16[384,256]{1,0:T(8,128)(2,1)S(1)}, bf16[384,256]{1,0:T(8,128)(2,1)S(1)}, u32[]{:S(2)}, u32[]{:S(2)}) %collective-permute-start.1) | collective-permute-done | bytes 196640 | tf_op jit(solution)/shard_map/ppermute | solution.py:275
  25.2 0.7 %attend0.1.refs_5_ = bf16[128,256]{1,0:T(8,128)(2,1)S(1)} custom-call(bf16[384,256]{1,0:T(8,128)(2,1)S(1)} %collective-permute-done.refs_0_, bf16[384,256]{1,0:T(8,128)(2,1)S(1)} %collective-permute-done.1.refs_1_, bf16[384,256]{1,0:T(8,128)(2,1)S(1)} %collective-permute-done.2.refs_2_, bf16[384,256]{1,0:T(8,128)(2,1)S(1)} %get-tuple-element.26.refs_3_, ...), custom_call_target="tpu_custom_call" | custom-call | flops 67108864 | tf_op jit(solution)/shard_map/attend0/pallas_call | solution.py:29
  25.9 2.5 %collective-permute-start.3 = (bf16[128,256]{1,0:T(8,128)(2,1)S(1)}, bf16[128,256]{1,0:T(8,128)(2,1)S(1)}, u32[]{:S(2)}, u32[]{:S(2)}) collective-permute-start(bf16[128,256]{1,0:T(8,128)(2,1)S(1)} %attend0.1.refs_5_), channel_id=1, source_target_pairs={{0,12},{4,8},{8,4},{12,0},{1,13},{5,9},{9,5},{13,1},{2,14},{6,10},... | collective-permute-start | bytes 196616 | tf_op jit(solution)/shard_map/ppermute | solution.py:288
  28.4 0.7 %attend1.1 = (bf16[128,256]{1,0:T(8,128)(2,1)S(1)}, bf16[48,512]{1,0:T(8,128)(2,1)S(1)}) custom-call(bf16[384,256]{1,0:T(8,128)(2,1)S(1)} %collective-permute-done.refs_0_, bf16[384,256]{1,0:T(8,128)(2,1)S(1)} %collective-permute-done.1.refs_1_, bf16[384,256]{1,0:T(8,128)(2,1)S(1)} %collective-permute-done.2.refs_2_, ...), custom_call_target="tpu_custom_call" | custom-call | flops 67108864 | tf_op jit(solution)/shard_map/attend1/pallas_call | solution.py:29
  29.2 1.9 %collective-permute-start.5 = (bf16[128,256]{1,0:T(8,128)(2,1)S(1)}, bf16[128,256]{1,0:T(8,128)(2,1)S(1)}, u32[]{:S(2)}, u32[]{:S(2)}) collective-permute-start(bf16[128,256]{1,0:T(8,128)(2,1)S(1)} %get-tuple-element.29.refs_4_), channel_id=1, source_target_pairs={{0,8},{4,12},{8,0},{12,4},{1,9},{5,13},{9,1},{13,5},{2,10},{6,14},... | collective-permute-start | bytes 196616 | tf_op jit(solution)/shard_map/ppermute | solution.py:288
  31.1 0.7 %attend2.1.refs_4_ = bf16[128,256]{1,0:T(8,128)(2,1)S(1)} custom-call(bf16[384,256]{1,0:T(8,128)(2,1)S(1)} %collective-permute-done.refs_0_, bf16[384,256]{1,0:T(8,128)(2,1)S(1)} %collective-permute-done.1.refs_1_, bf16[384,256]{1,0:T(8,128)(2,1)S(1)} %collective-permute-done.2.refs_2_, bf16[384,256]{1,0:T(8,128)(2,1)S(1)} %get-tuple-element.26.refs_3_, ...), custom_call_target="tpu_custom_call" | custom-call | flops 1000000000 | tf_op jit(solution)/shard_map/attend2/pallas_call | solution.py:29
  32.0 0.7 %attend3.1.refs_3_ = bf16[128,256]{1,0:T(8,128)(2,1)S(1)} custom-call(bf16[384,256]{1,0:T(8,128)(2,1)S(1)} %collective-permute-done.refs_0_, bf16[384,256]{1,0:T(8,128)(2,1)S(1)} %collective-permute-done.1.refs_1_, bf16[384,256]{1,0:T(8,128)(2,1)S(1)} %collective-permute-done.2.refs_2_, bf16[384,256]{1,0:T(8,128)(2,1)S(1)} %get-tuple-element.26.refs_3_, ...), custom_call_target="tpu_custom_call" | custom-call | flops 67108864 | tf_op jit(solution)/shard_map/attend3/pallas_call | solution.py:29
  32.6 1.0 %collective-permute-done.8.refs_3_ = bf16[48,512]{1,0:T(8,128)(2,1)S(1)} collective-permute-done((bf16[48,512]{1,0:T(8,128)(2,1)S(1)}, bf16[48,512]{1,0:T(8,128)(2,1)S(1)}, u32[]{:S(2)}, u32[]{:S(2)}) %collective-permute-start.8) | collective-permute-done | bytes 49184 | tf_op jit(solution)/shard_map/ppermute | solution.py:283
  33.6 1.1 %partials.1 = (bf16[16,640]{1,0:T(8,128)(2,1)S(1)}, bf16[16,640]{1,0:T(8,128)(2,1)S(1)}, bf16[32,640]{1,0:T(8,128)(2,1)S(1)}) custom-call(bf16[128,512]{1,0:T(8,128)(2,1)S(1)} %get-tuple-element.30.ck, bf16[128,512]{1,0:T(8,128)(2,1)S(1)} %get-tuple-element.31.cv, bf16[48,512]{1,0:T(8,128)(2,1)S(1)} %get-tuple-element.28.refs_0_, ...), custom_call_target="tpu_custom_call" | custom-call | flops 3000000000 | tf_op jit(solution)/shard_map/partials/pallas_call | solution.py:29
  34.7 2.0 %collective-permute-start.14 = (bf16[32,640]{1,0:T(8,128)(2,1)S(1)}, bf16[32,640]{1,0:T(8,128)(2,1)S(1)}, u32[]{:S(2)}, u32[]{:S(2)}) collective-permute-start(bf16[32,640]{1,0:T(8,128)(2,1)S(1)} %get-tuple-element.38), channel_id=1, source_target_pairs={{0,8},{4,12},{8,0},{12,4},{1,9},{5,13},{9,1},{13,5},{2,10},{6,14},... | collective-permute-start | bytes 122888 | tf_op jit(solution)/shard_map/ppermute | solution.py:299
  38.5 1.6 %collective-permute-start.12 = (bf16[128,512]{1,0:T(8,128)(2,1)S(1)}, bf16[128,512]{1,0:T(8,128)(2,1)S(1)}, u32[]{:S(2)}, u32[]{:S(2)}) collective-permute-start(bf16[128,512]{1,0:T(8,128)(2,1)S(1)} %add_convert_fusion.2.refs_5_), channel_id=1, source_target_pairs={{0,2},{1,3},{2,0},{3,1},{4,6},{5,7},{6,4},{7,5},{8,10},{9,11},{10,... | collective-permute-start | bytes 393224 | tf_op jit(solution)/shard_map/ppermute | solution.py:320
  40.4 0.6 %collective-permute-start.13 = (bf16[128,512]{1,0:T(8,128)(2,1)S(1)}, bf16[128,512]{1,0:T(8,128)(2,1)S(1)}, u32[]{:S(2)}, u32[]{:S(2)}) collective-permute-start(bf16[128,512]{1,0:T(8,128)(2,1)S(1)} %add_convert_fusion.1.refs_5_.refs_4_.refs_3_), channel_id=1, source_target_pairs={{0,2},{1,3},{2,0},{3,1},{4,6},{5,7},{6,4},{7,5},{8,10},{9,11},{10,... | collective-permute-start | bytes 393224 | tf_op jit(solution)/shard_map/ppermute | solution.py:320
  41.0 0.8 %project_near.1 = (bf16[128,1024]{1,0:T(8,128)(2,1)S(1)}, f32[128,1024]{1,0:T(8,128)S(1)}) custom-call(bf16[128,256]{1,0:T(8,128)(2,1)S(1)} %collective-permute-done.3.refs_0_, bf16[128,256]{1,0:T(8,128)(2,1)S(1)} %collective-permute-done.5.refs_1_, bf16[128,256]{1,0:T(8,128)(2,1)S(1)} %collective-permute-done.6.refs_2_, ...), custom_call_target="tpu_custom_call" | custom-call | flops 536870912 | tf_op jit(solution)/shard_map/project_near/pallas_call | solution.py:29
  42.2 1.3 %collective-permute-start.15 = (bf16[16,640]{1,0:T(8,128)(2,1)S(1)}, bf16[16,640]{1,0:T(8,128)(2,1)S(1)}, u32[]{:S(2)}, u32[]{:S(2)}) collective-permute-start(bf16[16,640]{1,0:T(8,128)(2,1)S(1)} %get-tuple-element.40), channel_id=1, source_target_pairs={{0,4},{4,0},{8,12},{12,8},{1,5},{5,1},{9,13},{13,9},{2,6},{6,2},{1... | collective-permute-start | bytes 61448 | tf_op jit(solution)/shard_map/ppermute | solution.py:329
  43.5 1.3 %video_cross.1 = bf16[128,512]{1,0:T(8,128)(2,1)} custom-call(bf16[128,512]{1,0:T(8,128)(2,1)S(1)} %get-tuple-element.36.cq, bf16[48,512]{1,0:T(8,128)(2,1)S(1)} %get-tuple-element.28.refs_0_, bf16[48,512]{1,0:T(8,128)(2,1)S(1)} %collective-permute-done.7.refs_1_, bf16[48,512]{1,0:T(8,128)(2,1)S(1)} %collective-permute-done.4.refs_4_.refs_2_, ...), custom_call_target="tpu_custom_call" | custom-call | flops 16777216 | tf_op jit(solution)/shard_map/video_cross/pallas_call | solution.py:29
  44.8 1.3 %collective-permute-done.15.refs_1_ = bf16[16,640]{1,0:T(8,128)(2,1)S(1)} collective-permute-done((bf16[16,640]{1,0:T(8,128)(2,1)S(1)}, bf16[16,640]{1,0:T(8,128)(2,1)S(1)}, u32[]{:S(2)}, u32[]{:S(2)}) %collective-permute-start.15) | collective-permute-done | bytes 20512 | tf_op jit(solution)/shard_map/ppermute | solution.py:329
  46.1 0.8 %merge_last.1 = bf16[16,512]{1,0:T(8,128)(2,1)} custom-call(bf16[16,640]{1,0:T(8,128)(2,1)S(1)} %get-tuple-element.39.refs_0_, bf16[16,640]{1,0:T(8,128)(2,1)S(1)} %collective-permute-done.15.refs_1_), custom_call_target="tpu_custom_call" | custom-call | tf_op jit(solution)/shard_map/merge_last/pallas_call | solution.py:29
  46.9 0.8 %add_convert_fusion = bf16[128,1024]{1,0:T(8,128)(2,1)} fusion(bf16[128,1024]{1,0:T(8,128)(2,1)S(1)} %collective-permute-done.11, f32[128,1024]{1,0:T(8,128)S(1)} %get-tuple-element.34, bf16[128,1024]{1,0:T(8,128)(2,1)S(1)} %get-tuple-element.22, bf16[128,512]{1,0:T(8,128)(2,1)S(1)} %collective-permute-done.13, bf16[128,512]{1,0:T(8,128)(2,1)S(1)} %collective-permute-done.12), kind=kLoop, calls=%fused_computation | loop fusion | flops 1310720 | bytes 1572864 | tf_op jit(solution)/shard_map/convert_element_type | solution.py:326
  (26 shorter events, 2.9 us)
Async XLA Ops:
  1.8 13.7 %collective-permute-start = (bf16[384,256]{1,0:T(8,128)(2,1)S(1)}, bf16[384,256]{1,0:T(8,128)(2,1)S(1)}, u32[]{:S(2)}, u32[]{:S(2)}) collective-permute-start(bf16[384,256]{1,0:T(8,128)(2,1)S(1)} %get-tuple-element.23), channel_id=1, source_target_pairs={{0,12},{4,8},{8,4},{12,0},{1,13},{5,9},{9,5},{13,1},{2,14},{6,10},... | collective-permute-start | bytes 589832 | tf_op jit(solution)/shard_map/ppermute | solution.py:275
  6.9 18.3 %collective-permute-start.1 = (bf16[384,256]{1,0:T(8,128)(2,1)S(1)}, bf16[384,256]{1,0:T(8,128)(2,1)S(1)}, u32[]{:S(2)}, u32[]{:S(2)}) collective-permute-start(bf16[384,256]{1,0:T(8,128)(2,1)S(1)} %get-tuple-element.24), channel_id=1, source_target_pairs={{0,8},{4,12},{8,0},{12,4},{1,9},{5,13},{9,1},{13,5},{2,10},{6,14},... | collective-permute-start | bytes 589832 | tf_op jit(solution)/shard_map/ppermute | solution.py:275
  6.9 18.3 %collective-permute-start.2 = (bf16[384,256]{1,0:T(8,128)(2,1)S(1)}, bf16[384,256]{1,0:T(8,128)(2,1)S(1)}, u32[]{:S(2)}, u32[]{:S(2)}) collective-permute-start(bf16[384,256]{1,0:T(8,128)(2,1)S(1)} %get-tuple-element.25), channel_id=1, source_target_pairs={{0,4},{4,0},{8,12},{12,8},{1,5},{5,1},{9,13},{13,9},{2,6},{6,2},{1... | collective-permute-start | bytes 589832 | tf_op jit(solution)/shard_map/ppermute | solution.py:275
  11.2 17.2 %collective-permute-start.4 = (bf16[48,512]{1,0:T(8,128)(2,1)S(1)}, bf16[48,512]{1,0:T(8,128)(2,1)S(1)}, u32[]{:S(2)}, u32[]{:S(2)}) collective-permute-start(bf16[48,512]{1,0:T(8,128)(2,1)S(1)} %get-tuple-element.28.refs_0_), channel_id=1, source_target_pairs={{0,8},{4,12},{8,0},{12,4},{1,9},{5,13},{9,1},{13,5},{2,10},{6,14},... | collective-permute-start | bytes 147464 | tf_op jit(solution)/shard_map/ppermute | solution.py:277
  13.5 19.1 %collective-permute-start.7 = (bf16[48,512]{1,0:T(8,128)(2,1)S(1)}, bf16[48,512]{1,0:T(8,128)(2,1)S(1)}, u32[]{:S(2)}, u32[]{:S(2)}) collective-permute-start(bf16[48,512]{1,0:T(8,128)(2,1)S(1)} %get-tuple-element.28.refs_0_), channel_id=1, source_target_pairs={{0,4},{4,0},{8,12},{12,8},{1,5},{5,1},{9,13},{13,9},{2,6},{6,2},{1... | collective-permute-start | bytes 147464 | tf_op jit(solution)/shard_map/ppermute | solution.py:277
  25.9 10.8 %collective-permute-start.3 = (bf16[128,256]{1,0:T(8,128)(2,1)S(1)}, bf16[128,256]{1,0:T(8,128)(2,1)S(1)}, u32[]{:S(2)}, u32[]{:S(2)}) collective-permute-start(bf16[128,256]{1,0:T(8,128)(2,1)S(1)} %attend0.1.refs_5_), channel_id=1, source_target_pairs={{0,12},{4,8},{8,4},{12,0},{1,13},{5,9},{9,5},{13,1},{2,14},{6,10},... | collective-permute-start | bytes 196616 | tf_op jit(solution)/shard_map/ppermute | solution.py:288
  29.1 4.5 %collective-permute-start.8 = (bf16[48,512]{1,0:T(8,128)(2,1)S(1)}, bf16[48,512]{1,0:T(8,128)(2,1)S(1)}, u32[]{:S(2)}, u32[]{:S(2)}) collective-permute-start(bf16[48,512]{1,0:T(8,128)(2,1)S(1)} %get-tuple-element.32), channel_id=1, source_target_pairs={{0,4},{4,0},{8,12},{12,8},{1,5},{5,1},{9,13},{13,9},{2,6},{6,2},{1... | collective-permute-start | bytes 147464 | tf_op jit(solution)/shard_map/ppermute | solution.py:283
  29.2 7.5 %collective-permute-start.5 = (bf16[128,256]{1,0:T(8,128)(2,1)S(1)}, bf16[128,256]{1,0:T(8,128)(2,1)S(1)}, u32[]{:S(2)}, u32[]{:S(2)}) collective-permute-start(bf16[128,256]{1,0:T(8,128)(2,1)S(1)} %get-tuple-element.29.refs_4_), channel_id=1, source_target_pairs={{0,8},{4,12},{8,0},{12,4},{1,9},{5,13},{9,1},{13,5},{2,10},{6,14},... | collective-permute-start | bytes 196616 | tf_op jit(solution)/shard_map/ppermute | solution.py:288
  31.8 4.9 %collective-permute-start.6 = (bf16[128,256]{1,0:T(8,128)(2,1)S(1)}, bf16[128,256]{1,0:T(8,128)(2,1)S(1)}, u32[]{:S(2)}, u32[]{:S(2)}) collective-permute-start(bf16[128,256]{1,0:T(8,128)(2,1)S(1)} %attend2.1.refs_4_), channel_id=1, source_target_pairs={{0,4},{4,0},{8,12},{12,8},{1,5},{5,1},{9,13},{13,9},{2,6},{6,2},{1... | collective-permute-start | bytes 196616 | tf_op jit(solution)/shard_map/ppermute | solution.py:288
  34.7 7.2 %collective-permute-start.14 = (bf16[32,640]{1,0:T(8,128)(2,1)S(1)}, bf16[32,640]{1,0:T(8,128)(2,1)S(1)}, u32[]{:S(2)}, u32[]{:S(2)}) collective-permute-start(bf16[32,640]{1,0:T(8,128)(2,1)S(1)} %get-tuple-element.38), channel_id=1, source_target_pairs={{0,8},{4,12},{8,0},{12,4},{1,9},{5,13},{9,1},{13,5},{2,10},{6,14},... | collective-permute-start | bytes 122888 | tf_op jit(solution)/shard_map/ppermute | solution.py:299
  37.0 1.4 %collective-permute-start.9 = (bf16[128,512]{1,0:T(8,128)(2,1)S(1)}, bf16[128,512]{1,0:T(8,128)(2,1)S(1)}, u32[]{:S(2)}, u32[]{:S(2)}) collective-permute-start(bf16[128,512]{1,0:T(8,128)(2,1)S(1)} %project_far.2.refs_5_), channel_id=1, source_target_pairs={{0,1},{1,0},{2,3},{3,2},{4,5},{5,4},{6,7},{7,6},{8,9},{9,8},{10,11... | collective-permute-start | bytes 393224 | tf_op jit(solution)/shard_map/ppermute | solution.py:312
  37.5 2.9 %collective-permute-start.10 = (bf16[128,512]{1,0:T(8,128)(2,1)S(1)}, bf16[128,512]{1,0:T(8,128)(2,1)S(1)}, u32[]{:S(2)}, u32[]{:S(2)}) collective-permute-start(bf16[128,512]{1,0:T(8,128)(2,1)S(1)} %project_far.3.refs_5_), channel_id=1, source_target_pairs={{0,1},{1,0},{2,3},{3,2},{4,5},{5,4},{6,7},{7,6},{8,9},{9,8},{10,11... | collective-permute-start | bytes 393224 | tf_op jit(solution)/shard_map/ppermute | solution.py:312
  38.5 8.4 %collective-permute-start.12 = (bf16[128,512]{1,0:T(8,128)(2,1)S(1)}, bf16[128,512]{1,0:T(8,128)(2,1)S(1)}, u32[]{:S(2)}, u32[]{:S(2)}) collective-permute-start(bf16[128,512]{1,0:T(8,128)(2,1)S(1)} %add_convert_fusion.2.refs_5_), channel_id=1, source_target_pairs={{0,2},{1,3},{2,0},{3,1},{4,6},{5,7},{6,4},{7,5},{8,10},{9,11},{10,... | collective-permute-start | bytes 393224 | tf_op jit(solution)/shard_map/ppermute | solution.py:320
  40.4 6.5 %collective-permute-start.13 = (bf16[128,512]{1,0:T(8,128)(2,1)S(1)}, bf16[128,512]{1,0:T(8,128)(2,1)S(1)}, u32[]{:S(2)}, u32[]{:S(2)}) collective-permute-start(bf16[128,512]{1,0:T(8,128)(2,1)S(1)} %add_convert_fusion.1.refs_5_.refs_4_.refs_3_), channel_id=1, source_target_pairs={{0,2},{1,3},{2,0},{3,1},{4,6},{5,7},{6,4},{7,5},{8,10},{9,11},{10,... | collective-permute-start | bytes 393224 | tf_op jit(solution)/shard_map/ppermute | solution.py:320
  41.8 5.1 %collective-permute-start.11 = (bf16[128,1024]{1,0:T(8,128)(2,1)S(1)}, bf16[128,1024]{1,0:T(8,128)(2,1)S(1)}, u32[]{:S(2)}, u32[]{:S(2)}) collective-permute-start(bf16[128,1024]{1,0:T(8,128)(2,1)S(1)} %get-tuple-element.35), channel_id=1, source_target_pairs={{0,1},{1,0},{2,3},{3,2},{4,5},{5,4},{6,7},{7,6},{8,9},{9,8},{10,11... | collective-permute-start | bytes 786440 | tf_op jit(solution)/shard_map/ppermute | solution.py:323
  42.2 3.8 %collective-permute-start.15 = (bf16[16,640]{1,0:T(8,128)(2,1)S(1)}, bf16[16,640]{1,0:T(8,128)(2,1)S(1)}, u32[]{:S(2)}, u32[]{:S(2)}) collective-permute-start(bf16[16,640]{1,0:T(8,128)(2,1)S(1)} %get-tuple-element.40), channel_id=1, source_target_pairs={{0,4},{4,0},{8,12},{12,8},{1,5},{5,1},{9,13},{13,9},{2,6},{6,2},{1... | collective-permute-start | bytes 61448 | tf_op jit(solution)/shard_map/ppermute | solution.py:329
